TPU v7x, 256 devices: a whole 4x4x8 slice. The times are simulated.
256 devices in a mesh: shot: 8 (over z_lo, core), probe: 32 (over x, z_hi, y).
Axes of the slice: x: 4, y: 4, z: 8 (z_hi: 2, z_lo: 4; z = z_hi * 4 + z_lo), core: 2. Of those that a mesh axis runs over, the one named last changes fastest.
Arguments:
- probes: float32 [64, 512, 512], P('probe'), may hold values from -6 to 6
- coarse_sample: float32 [64, 512, 512], P('probe', 'shot'), may hold values from -6 to 6
- coefficient: float32 [512, 512], replicated, may hold values from 0.05 to 0.45
- receiver: float32 [512, 512], replicated, may hold values from 0.05 to 0.5
- checkpoints: float32 [16, 2, 512, 512], P('shot', None, 'probe'), may hold values from -6 to 6
- encodings: int32 [16, 256], P('shot'), may hold values from -1 to 1, as said below
- wavelet: float32 [3, 256], replicated, may hold values from -6 to 6
- bounds: int32 [65], replicated, may hold values from 0 to 512, as said below
Outputs:
- samples: float32 [64, 512, 512], P('probe', 'shot')
Inputs may be any that keep to these rules, and one draw needn't show every extreme that they name: `encodings`: every entry is -1 or 1. bounds[0] = 0 and bounds[64] = 512; the entries rise strictly; blocks 2 i and 2 i + 1 together hold exactly 16 rows.
All inputs are finite; a program needn't handle non-finite values.
Results may differ from a plain program's by a relative error of at most 0.000094.
Values sent between devices are 32-bit elements; how exact they have to be, the bound alone decides.
No kernel may reach another device: no remote copies, remote signals or barrier semaphores. Data moves between devices by JAX's collectives and lax.ppermute only.
A program may use at most 128 MiB of HBM per device.

v0:
```python
import jax
import jax.numpy as jnp
from jax import lax
from jax.sharding import PartitionSpec as P

NZ = 512
NSHOT = 256
NT = 4


def with_halo(array, sides, width):
    for axis, dim in sides:
        devices, length = (lax.axis_size(axis), array.shape[dim])
        up = [(i, (i + 1) % devices) for i in range(devices - 1)]
        down = [(j, i) for i, j in up]
        last = lax.slice_in_dim(array, length - width, length, axis=dim)
        leading = lax.slice_in_dim(array, 0, width, axis=dim)
        before = lax.ppermute(last, axis, up)
        after = lax.ppermute(leading, axis, down)
        array = jnp.concatenate([before, array, after], axis=dim)
    return array


def laplace(values):
    pad_width = [(0, 0)] * (values.ndim - 2) + [(1, 1), (1, 1)]
    padded = jnp.pad(values, pad_width)
    return (
        padded[..., 2:, 1:-1]
        + padded[..., :-2, 1:-1]
        + padded[..., 1:-1, 2:]
        + padded[..., 1:-1, :-2]
        - 4.0 * values
    )


def laplace_framed(framed):
    padded = jnp.pad(framed, [(0, 0), (1, 1)])
    middle = framed[1:-1]
    return (
        padded[2:, 1:-1] + padded[:-2, 1:-1] + padded[1:-1, 2:] + padded[1:-1, :-2] - 4.0 * middle
    )


def shot_sources(encodings, wavelet):
    columns = jnp.arange(NZ)
    spacing = NZ // NSHOT
    position = jnp.arange(NSHOT) * NZ // NSHOT + spacing // 2
    onehot = (position[:, None] == columns[None, :]).astype(jnp.float32)
    amplitude = encodings.astype(jnp.float32)[:, None, :] * wavelet[None, :, :]
    return jnp.einsum("stk,kz->stz", amplitude, onehot, precision=lax.Precision.HIGHEST)


def block_parity(row_index, bounds):
    inner = bounds[1:-1]
    return jnp.sum((row_index[:, None] >= inner[None, :]).astype(jnp.int32), axis=1) % 2


def hessian_term(vectors, levels, coefficient, weight_square):
    before = jnp.zeros_like(vectors)
    current = jnp.zeros_like(vectors)
    deltas = []
    for moment in range(NT):
        following = (
            2.0 * current - before + coefficient * laplace(current) + vectors * levels[moment]
        )
        before, current = (current, following)
        deltas.append(following)
    upcoming = jnp.zeros_like(vectors)
    beyond = jnp.zeros_like(vectors)
    gradient = jnp.zeros_like(vectors)
    for moment in range(NT, 0, -1):
        adjoint = (
            weight_square * deltas[moment - 1]
            + 2.0 * upcoming
            + laplace(coefficient * upcoming)
            - beyond
        )
        gradient = gradient + levels[moment - 1] * adjoint
        beyond, upcoming = (upcoming, adjoint)
    return gradient


def on_device(
    probes, coarse_sample, coefficient, receiver, checkpoints, encodings, wavelet, bounds
):
    num_rows = probes.shape[1]
    slab_rows = checkpoints.shape[2]
    source_at = num_rows // 2
    sources = shot_sources(encodings, wavelet)
    colour = jnp.arange(probes.shape[0]) % 2
    parity_all = block_parity(jnp.arange(num_rows), bounds)
    support = (parity_all[None, :] == colour[:, None]).astype(jnp.float32)
    vectors = probes * support[:, :, None]
    weight_square = receiver * receiver
    accumulated = jnp.zeros_like(probes)
    for member in range(checkpoints.shape[0]):
        offset = lax.axis_index("probe") * slab_rows
        coef_slab = lax.dynamic_slice_in_dim(coefficient, offset, slab_rows, 0)
        at_source = (offset + jnp.arange(slab_rows) == source_at).astype(jnp.float32)[:, None]
        before = checkpoints[member, 0]
        current = checkpoints[member, 1]
        history = [current]
        for moment in range(NT - 1):
            framed = with_halo(current, (("probe", 0),), 1)
            following = (
                2.0 * current
                - before
                + coef_slab * laplace_framed(framed)
                + at_source * sources[member, moment][None, :]
            )
            before, current = (current, following)
            history.append(current)
        levels = lax.all_gather(jnp.stack(history), "probe", axis=1, tiled=True)
        accumulated = accumulated + hessian_term(vectors, levels, coefficient, weight_square)
    out_rows = coarse_sample.shape[1]
    summed = lax.psum(accumulated, "shot")
    share = lax.dynamic_slice_in_dim(summed, lax.axis_index("shot") * out_rows, out_rows, 1)
    row_out = lax.axis_index("shot") * out_rows + jnp.arange(out_rows)
    keep = (block_parity(row_out, bounds)[None, :] != colour[:, None]).astype(jnp.float32)
    return keep[:, :, None] * (share - coarse_sample)


def solution(mesh):
    return jax.shard_map(
        on_device,
        mesh=mesh,
        in_specs=(
            P("probe", None, None),
            P("probe", "shot", None),
            P(),
            P(),
            P("shot", None, "probe", None),
            P("shot", None),
            P(),
            P(),
        ),
        out_specs=P("probe", "shot", None),
        check_vma=False,
    )
```

profile of v0, /device:TPU:1, one launch (start us, length us, event | category | flops | bytes accessed | tf_op | source)
XLA Modules:
  0.0 445.9 jit_solution(4997056895417095035)
XLA Ops:
  6.5 0.9 slice_bitcast_fusion.12
  7.5 4.0 collective-permute-start.1
  11.5 1.3 collective-permute-start
  12.8 0.8 slice_bitcast_fusion.9
  13.6 0.7 convert_element_type.59
  14.3 1.0 fusion.94
  15.4 0.5 collective-permute-done
  15.9 0.9 fusion.128
  16.8 3.5 collective-permute-start.3
  20.3 1.3 collective-permute-start.2
  21.7 7.4 %collective-permute-done.2 = f32[1,512]{1,0:T(1,128)S(1)} collective-permute-done((f32[1,512]{1,0:T(1,128)S(1)}, f32[1,512]{1,0:T(1,128)S(1)}, u32[]{:S(2)}, u32[]{:S(2)}) %collective-permute-start.2) | collective-permute-done | bytes 2080 | tf_op jit(solution)/shard_map/ppermute | solution.py:19
  29.1 0.9 fusion.123
  30.0 9.4 %collective-permute-start.5 = (f32[1,512]{1,0:T(1,128)S(1)}, f32[1,512]{1,0:T(1,128)S(1)}, u32[]{:S(2)}, u32[]{:S(2)}) collective-permute-start(f32[1,512]{1,0:T(1,128)S(1)} %get-tuple-element.47), channel_id=1, source_target_pairs={{0,1},{1,2},{2,3},{3,4},{4,5},{5,6},{6,7},{7,8},{8,9},{9,10},{10,1... | collective-permute-start | bytes 6152 | tf_op jit(solution)/shard_map/ppermute | solution.py:18
  39.4 1.3 collective-permute-start.4
  40.7 3.2 collective-permute-done.4
  44.0 0.9 fusion.118
  44.8 0.7 pad_maximum_fusion
  45.6 9.4 %collective-permute-start.7 = (f32[1,512]{1,0:T(1,128)S(1)}, f32[1,512]{1,0:T(1,128)S(1)}, u32[]{:S(2)}, u32[]{:S(2)}) collective-permute-start(f32[1,512]{1,0:T(1,128)S(1)} %get-tuple-element.39), channel_id=1, source_target_pairs={{0,1},{1,2},{2,3},{3,4},{4,5},{5,6},{6,7},{7,8},{8,9},{9,10},{10,1... | collective-permute-start | bytes 6152 | tf_op jit(solution)/shard_map/ppermute | solution.py:18
  55.0 1.3 collective-permute-start.6
  56.3 3.0 collective-permute-done.6
  59.4 0.9 fusion.112
  60.3 7.9 %collective-permute-start.9 = (f32[1,512]{1,0:T(1,128)S(1)}, f32[1,512]{1,0:T(1,128)S(1)}, u32[]{:S(2)}, u32[]{:S(2)}) collective-permute-start(f32[1,512]{1,0:T(1,128)S(1)} %get-tuple-element.45), channel_id=1, source_target_pairs={{0,1},{1,2},{2,3},{3,4},{4,5},{5,6},{6,7},{7,8},{8,9},{9,10},{10,1... | collective-permute-start | bytes 6152 | tf_op jit(solution)/shard_map/ppermute | solution.py:18
  68.2 1.3 collective-permute-start.8
  69.5 3.0 collective-permute-done.8
  72.7 0.9 fusion.107
  73.5 8.1 %collective-permute-start.11 = (f32[1,512]{1,0:T(1,128)S(1)}, f32[1,512]{1,0:T(1,128)S(1)}, u32[]{:S(2)}, u32[]{:S(2)}) collective-permute-start(f32[1,512]{1,0:T(1,128)S(1)} %get-tuple-element.43), channel_id=1, source_target_pairs={{0,1},{1,2},{2,3},{3,4},{4,5},{5,6},{6,7},{7,8},{8,9},{9,10},{10,1... | collective-permute-start | bytes 6152 | tf_op jit(solution)/shard_map/ppermute | solution.py:18
  81.6 1.3 collective-permute-start.10
  82.9 3.4 collective-permute-done.10
  86.5 0.7 pad_maximum_fusion.1
  87.3 1.2 mul.566
  88.9 1.6 fusion.92
  90.5 1.6 fusion.88
  92.0 75.1 %all-gather.3.cloned.1.call-done = f32[4,512,512]{2,1,0:T(8,128)} async-done(((f32[4,16,512]{2,1,0:T(8,128)}), f32[4,512,512]{2,1,0:T(8,128)}) %all-gather.3.cloned.1.call-update) | async-done | bytes 4194320 | tf_op jit(solution)/shard_map/all_gather | solution.py:113
  167.1 4.2 slice_bitcast_fusion.4
  171.4 105.6 %all-gather.5.cloned.1.call-done = f32[4,512,512]{2,1,0:T(8,128)} async-done(((f32[4,16,512]{2,1,0:T(8,128)}), f32[4,512,512]{2,1,0:T(8,128)}) %all-gather.5.cloned.1.call-update) | async-done | bytes 4194320 | tf_op jit(solution)/shard_map/all_gather | solution.py:113
  277.0 3.8 slice_bitcast_fusion
  280.8 0.5 multiply_add_fusion
  281.3 0.5 copy-done.14
  282.1 2.0 fusion.49
  284.1 5.0 %fusion.56 = (f32[2,512,512]{2,1,0:T(8,128)}, f32[2,512,512]{2,1,0:T(8,128)S(1)}) fusion(f32[2,512,512]{2,1,0:T(8,128)S(1)} %fusion.49, f32[2,512,512]{2,1,0:T(8,128)S(1)} %get-tuple-element.29, f32[2,512,512]{2,1,0:T(8,128)S(1)} %copy-done.1, f32[512,512]{1,0:T(8,128)S(1)} %get-tuple-element.19, f32[512,512]{1,0:T(8,128)S(1)} %copy-done, ...), kind=kLoop, calls=%fused_computation.108 | loop fusion | flops 11534336 | bytes 15732736 | tf_op jit(solution)/shard_map/add | solution.py:64
  289.1 3.3 fusion.13
  292.3 13.9 %broadcast_multiply_fusion.2 = (f32[2,512,512]{2,1,0:T(8,128)}, f32[2,512,512]{2,1,0:T(8,128)}, f32[2,512,512]{2,1,0:T(8,128)}, f32[2,512,512]{2,1,0:T(8,128)S(1)}) fusion(f32[512,512]{1,0:T(8,128)S(1)} %copy-done, f32[512,512]{1,0:T(8,128)} %fusion.88, f32[512,512]{1,0:T(8,128)} %get-tuple-element.22, f32[2,512,512]{2,1,0:T(8,128)S(1)} %copy-done.1, ...), kind=kLoop, calls=%fused_computation.161 | loop fusion | flops 15204352 | bytes 24121344 | tf_op jit(solution)/shard_map/mul | solution.py:75
  306.3 9.5 %broadcast_multiply_fusion.1 = (f32[2,512,512]{2,1,0:T(8,128)}, f32[2,512,512]{2,1,0:T(8,128)}) fusion(f32[512,512]{1,0:T(8,128)S(1)} %copy-done, f32[2,512,512]{2,1,0:T(8,128)} %get-tuple-element.9, f32[2,512,512]{2,1,0:T(8,128)} %get-tuple-element.10, f32[2,512,512]{2,1,0:T(8,128)} %get-tuple-element.27, f32[512,512]{1,0:T(8,128)S(1)} %copy-done.2), kind=kLoop, calls=%fused_computation.160 | loop fusion | flops 5242880 | bytes 12582912 | tf_op jit(solution)/shard_map/mul | solution.py:75
  315.8 14.9 %broadcast_multiply_fusion = (f32[2,512,512]{2,1,0:T(8,128)}, f32[2,512,512]{2,1,0:T(8,128)}, f32[2,512,512]{2,1,0:T(8,128)}, f32[2,512,512]{2,1,0:T(8,128)}) fusion(f32[512,512]{1,0:T(8,128)S(1)} %copy-done, f32[2,512,512]{2,1,0:T(8,128)} %get-tuple-element.10, f32[2,512,512]{2,1,0:T(8,128)} %get-tuple-element.7, f32[2,512,512]{2,1,0:T(8,128)} %get-tuple-element.8, ...), kind=kLoop, calls=%fused_computation.159 | loop fusion | flops 11010048 | bytes 25165824 | tf_op jit(solution)/shard_map/mul | solution.py:75
  330.7 10.1 %broadcast_multiply_fusion.3 = (f32[2,512,512]{2,1,0:T(8,128)}, f32[2,512,512]{2,1,0:T(8,128)}) fusion(f32[512,512]{1,0:T(8,128)S(1)} %copy-done, f32[2,512,512]{2,1,0:T(8,128)} %copy-done.4, f32[2,512,512]{2,1,0:T(8,128)} %get-tuple-element.31, f32[2,512,512]{2,1,0:T(8,128)} %get-tuple-element.32, f32[2,512,512]{2,1,0:T(8,128)} %copy-done.5, ...), kind=kLoop, calls=%fused_computation.162 | loop fusion | flops 5767168 | bytes 14680064 | tf_op jit(solution)/shard_map/mul | solution.py:75
  340.8 19.6 %fusion.42 = f32[2,512,512]{2,1,0:T(8,128)} fusion(f32[2,512,512]{2,1,0:T(8,128)} %get-tuple-element.32, f32[2,512,512]{2,1,0:T(8,128)} %get-tuple-element.11, f32[2,512,512]{2,1,0:T(8,128)} %get-tuple-element.8, f32[2,512,512]{2,1,0:T(8,128)} %get-tuple-element.5, f32[2,512,512]{2,1,0:T(8,128)} %get-tuple-element.6, f32[2,512,512]{2,1,0:T(8,128)} %copy-done.8, ...), kind=kLoop, calls=%fused_computation.94 | loop fusion | flops 18350080 | bytes 32505856 | tf_op jit(solution)/shard_map/add | solution.py:114
  360.7 77.0 %all-reduce.22.cloned.1.call-done = f32[2,512,512]{2,1,0:T(8,128)} async-done(((f32[2,512,512]{2,1,0:T(8,128)}), f32[2,512,512]{2,1,0:T(8,128)}) %all-reduce.22.cloned.1.call-update) | async-done | bytes 2097168 | tf_op jit(solution)/shard_map/psum | solution.py:116
  437.7 1.7 subtract_multiply_fusion
  (75 shorter events, 1.9 us)
Async XLA Ops:
  6.5 66.1 %copy-start = (f32[512,512]{1,0:T(8,128)S(1)}, f32[512,512]{1,0:T(8,128)}, u32[]{:S(2)}) copy-start(f32[512,512]{1,0:T(8,128)} %param.10) | copy-start | bytes 3145732
  6.5 80.7 %copy-start.19 = (s32[65]{0:T(128)S(1)}, s32[65]{0:T(128)}, u32[]{:S(2)}) copy-start(s32[65]{0:T(128)} %param.15) | copy-start | bytes 784
  6.5 80.8 %copy-start.16 = (f32[512,512]{1,0:T(8,128)S(1)}, f32[512,512]{1,0:T(8,128)}, u32[]{:S(2)}) copy-start(f32[512,512]{1,0:T(8,128)} %param.11) | copy-start | bytes 3145732
  6.5 160.6 %all-gather.3.cloned.1.call-start = ((), (), s32[]{:S(2)}) async-start(), calls=%async_computation | async-start | bytes 4325376 | tf_op jit(solution)/shard_map/all_gather | solution.py:113
  7.5 7.9 %collective-permute-start.1 = (f32[1,512]{1,0:T(1,128)S(1)}, f32[1,512]{1,0:T(1,128)S(1)}, u32[]{:S(2)}, u32[]{:S(2)}) collective-permute-start(f32[1,512]{1,0:T(1,128)S(1)} %get-tuple-element.40), channel_id=1, source_target_pairs={{0,1},{1,2},{2,3},{3,4},{4,5},{5,6},{6,7},{7,8},{8,9},{9,10},{10,1... | collective-permute-start | bytes 6152 | tf_op jit(solution)/shard_map/ppermute | solution.py:18
  11.5 4.3 collective-permute-start
  16.8 4.8 %collective-permute-start.3 = (f32[1,512]{1,0:T(1,128)S(1)}, f32[1,512]{1,0:T(1,128)S(1)}, u32[]{:S(2)}, u32[]{:S(2)}) collective-permute-start(f32[1,512]{1,0:T(1,128)S(1)} %get-tuple-element.49), channel_id=1, source_target_pairs={{0,1},{1,2},{2,3},{3,4},{4,5},{5,6},{6,7},{7,8},{8,9},{9,10},{10,1... | collective-permute-start | bytes 6152 | tf_op jit(solution)/shard_map/ppermute | solution.py:18
  20.3 8.7 %collective-permute-start.2 = (f32[1,512]{1,0:T(1,128)S(1)}, f32[1,512]{1,0:T(1,128)S(1)}, u32[]{:S(2)}, u32[]{:S(2)}) collective-permute-start(f32[1,512]{1,0:T(1,128)S(1)} %get-tuple-element.50), channel_id=1, source_target_pairs={{1,0},{2,1},{3,2},{4,3},{5,4},{6,5},{7,6},{8,7},{9,8},{10,9},{11,1... | collective-permute-start | bytes 6152 | tf_op jit(solution)/shard_map/ppermute | solution.py:19
  30.0 10.7 %collective-permute-start.5 = (f32[1,512]{1,0:T(1,128)S(1)}, f32[1,512]{1,0:T(1,128)S(1)}, u32[]{:S(2)}, u32[]{:S(2)}) collective-permute-start(f32[1,512]{1,0:T(1,128)S(1)} %get-tuple-element.47), channel_id=1, source_target_pairs={{0,1},{1,2},{2,3},{3,4},{4,5},{5,6},{6,7},{7,8},{8,9},{9,10},{10,1... | collective-permute-start | bytes 6152 | tf_op jit(solution)/shard_map/ppermute | solution.py:18
  39.4 4.5 %collective-permute-start.4 = (f32[1,512]{1,0:T(1,128)S(1)}, f32[1,512]{1,0:T(1,128)S(1)}, u32[]{:S(2)}, u32[]{:S(2)}) collective-permute-start(f32[1,512]{1,0:T(1,128)S(1)} %get-tuple-element.48), channel_id=1, source_target_pairs={{1,0},{2,1},{3,2},{4,3},{5,4},{6,5},{7,6},{8,7},{9,8},{10,9},{11,1... | collective-permute-start | bytes 6152 | tf_op jit(solution)/shard_map/ppermute | solution.py:19
  45.5 231.4 %all-gather.5.cloned.1.call-start = ((), (), s32[]{:S(2)}) async-start(), calls=%async_computation.1 | async-start | bytes 4325376 | tf_op jit(solution)/shard_map/all_gather | solution.py:113
  45.6 10.7 %collective-permute-start.7 = (f32[1,512]{1,0:T(1,128)S(1)}, f32[1,512]{1,0:T(1,128)S(1)}, u32[]{:S(2)}, u32[]{:S(2)}) collective-permute-start(f32[1,512]{1,0:T(1,128)S(1)} %get-tuple-element.39), channel_id=1, source_target_pairs={{0,1},{1,2},{2,3},{3,4},{4,5},{5,6},{6,7},{7,8},{8,9},{9,10},{10,1... | collective-permute-start | bytes 6152 | tf_op jit(solution)/shard_map/ppermute | solution.py:18
  55.0 4.3 collective-permute-start.6
  60.3 9.2 %collective-permute-start.9 = (f32[1,512]{1,0:T(1,128)S(1)}, f32[1,512]{1,0:T(1,128)S(1)}, u32[]{:S(2)}, u32[]{:S(2)}) collective-permute-start(f32[1,512]{1,0:T(1,128)S(1)} %get-tuple-element.45), channel_id=1, source_target_pairs={{0,1},{1,2},{2,3},{3,4},{4,5},{5,6},{6,7},{7,8},{8,9},{9,10},{10,1... | collective-permute-start | bytes 6152 | tf_op jit(solution)/shard_map/ppermute | solution.py:18
  68.2 4.3 collective-permute-start.8
  73.5 9.4 %collective-permute-start.11 = (f32[1,512]{1,0:T(1,128)S(1)}, f32[1,512]{1,0:T(1,128)S(1)}, u32[]{:S(2)}, u32[]{:S(2)}) collective-permute-start(f32[1,512]{1,0:T(1,128)S(1)} %get-tuple-element.43), channel_id=1, source_target_pairs={{0,1},{1,2},{2,3},{3,4},{4,5},{5,6},{6,7},{7,8},{8,9},{9,10},{10,1... | collective-permute-start | bytes 6152 | tf_op jit(solution)/shard_map/ppermute | solution.py:18
  81.6 4.7 %collective-permute-start.10 = (f32[1,512]{1,0:T(1,128)S(1)}, f32[1,512]{1,0:T(1,128)S(1)}, u32[]{:S(2)}, u32[]{:S(2)}) collective-permute-start(f32[1,512]{1,0:T(1,128)S(1)} %get-tuple-element.44), channel_id=1, source_target_pairs={{1,0},{2,1},{3,2},{4,3},{5,4},{6,5},{7,6},{8,7},{9,8},{10,9},{11,1... | collective-permute-start | bytes 6152 | tf_op jit(solution)/shard_map/ppermute | solution.py:19
  87.2 350.5 %all-reduce.22.cloned.1.call-start = ((), (), s32[]{:S(2)}) async-start(), calls=%async_computation.2 | async-start | bytes 4194304 | tf_op jit(solution)/shard_map/psum | solution.py:116
  171.4 109.4 %copy-start.1 = (f32[2,512,512]{2,1,0:T(8,128)S(1)}, f32[2,512,512]{2,1,0:T(8,128)}, u32[]{:S(2)}) copy-start(f32[2,512,512]{2,1,0:T(8,128)} %param.8) | copy-start | bytes 6291460
  277.0 3.8 copy-start.12
  277.0 3.8 copy-start.17
  280.7 1.0 copy-start.14
  280.7 1.3 copy-start.15
  280.7 3.3 copy-start.13
  281.7 2.3 copy-start.8
  281.7 7.3 %copy-start.6 = (f32[2,512,512]{2,1,0:T(8,128)}, f32[2,512,512]{2,1,0:T(8,128)S(1)}, u32[]{:S(2)}) copy-start(f32[2,512,512]{2,1,0:T(8,128)S(1)} %get-tuple-element.30) | copy-start | bytes 6291460
  282.1 2.0 copy-start.11
  284.0 5.0 %copy-start.7 = (f32[2,512,512]{2,1,0:T(8,128)}, f32[2,512,512]{2,1,0:T(8,128)S(1)}, u32[]{:S(2)}) copy-start(f32[2,512,512]{2,1,0:T(8,128)S(1)} %fusion.49) | copy-start | bytes 6291460
  284.1 5.0 %copy-start.9 = (f32[512,512]{1,0:T(8,128)S(1)}, f32[512,512]{1,0:T(8,128)}, u32[]{:S(2)}) copy-start(f32[512,512]{1,0:T(8,128)} %get-tuple-element.23) | copy-start | bytes 3145732
  289.1 3.3 copy-start.5
  289.1 3.3 copy-start.2
  306.3 9.6 %copy-start.4 = (f32[2,512,512]{2,1,0:T(8,128)}, f32[2,512,512]{2,1,0:T(8,128)S(1)}, u32[]{:S(2)}) copy-start(f32[2,512,512]{2,1,0:T(8,128)S(1)} %get-tuple-element.18) | copy-start | bytes 6291460
  315.8 14.9 %copy-start.3 = (f32[512,512]{1,0:T(8,128)S(1)}, f32[512,512]{1,0:T(8,128)}, u32[]{:S(2)}) copy-start(f32[512,512]{1,0:T(8,128)} %mul.566) | copy-start | bytes 3145732
  330.7 10.1 %copy-start.10 = (f32[512,512]{1,0:T(8,128)S(1)}, f32[512,512]{1,0:T(8,128)}, u32[]{:S(2)}) copy-start(f32[512,512]{1,0:T(8,128)} %get-tuple-element.23) | copy-start | bytes 3145732
  360.4 77.3 %copy-start.18 = (f32[2,64,512]{2,1,0:T(8,128)S(1)}, f32[2,64,512]{2,1,0:T(8,128)}, u32[]{:S(2)}) copy-start(f32[2,64,512]{2,1,0:T(8,128)} %param.9) | copy-start | bytes 786436
Sparse Core Ops, SparseCore 0:
  45.6 121.4 all-gather.2
  170.7 106.2 all-gather.4
  360.5 77.0 all-reduce.21
where the time goes:
time: 447 us; the launch traced here: 446 us
  waiting for transfers between devices  278 us (62%)
  other arithmetic  92.2 us (21%)
  starting transfers between devices  50.1 us (11%)
  between operations  13.6 us (3%)
  local copies, waits for them, and re-layouts  10.8 us (2%)
    all_gather x2, waiting for transfers between devices, on_device(): levels = lax.all_gather(jnp.stack(history), 'probe', axis=1, tiled=True)  181 us
    psum x1, waiting for transfers between devices, on_device(): summed = lax.psum(accumulated, 'shot')  77 us
    mul x4, other arithmetic, hessian_term(): coefficient * upcoming  48.4 us
    ppermute x6, starting transfers between devices, with_halo(): before = lax.ppermute(last, axis, up)  42.3 us
    ppermute x6, waiting for transfers between devices, with_halo(): after = lax.ppermute(leading, axis, down)  20.5 us
    add x1, other arithmetic, on_device(): accumulated + hessian_term(vectors, levels, coefficient, weight_square)  19.6 us
    add x4, other arithmetic, hessian_term(): 2.0 * current - before + coefficient * laplace(current)  10.7 us
  transfers between devices with their start and end apart: 15, of which 9 were waited for; matrix products, arithmetic and copies ran while one was open for 3% of the time, Pallas kernels for 0%

commit v1 on v0

v1 whole, which is shorter than its diff:
```python
import functools
import jax
import jax.numpy as jnp
from jax import lax
from jax.experimental import pallas as pl
from jax.experimental.pallas import tpu as pltpu
from jax.sharding import PartitionSpec as P

NZ = 512
NSHOT = 256
CHUNK = 64
WIN = 80
EDGE = 8
LANES = 128
TILES = NZ // LANES
UNROLL = 4


def split(row):
    return [row[:, LANES * j : LANES * (j + 1)] for j in range(TILES)]


def sideways(tiles, first, last):
    right = [pltpu.roll(t, 1, 1) for t in tiles]
    left = [pltpu.roll(t, LANES - 1, 1) for t in tiles]
    zero = jnp.zeros_like(tiles[0])
    out = []
    for j in range(TILES):
        a = jnp.where(first, right[j - 1] if j else zero, right[j])
        b = jnp.where(last, left[j + 1] if j < TILES - 1 else zero, left[j])
        out.append(a + b)
    return out


def kernel(place, *refs, shots, has_total):
    slabs = refs[0:4]
    blocks = refs[4:8]
    parity_ref, coef_ref, recv_ref = refs[8:11]
    n = 11
    if has_total:
        totals = refs[n : n + 4]
        n += 4
    outs = refs[n : n + 4]
    u_ref, v_ref, e_ref, w_ref, grad_ref, *d_refs = refs[n + 4 :]
    d_refs = [d_refs[4 * i : 4 * i + 4] for i in range(shots)]

    lane = lax.broadcasted_iota(jnp.int32, (8, LANES), 1)
    first = lane == 0
    last = lane == LANES - 1

    for k in range(4):
        y = lax.rem(place[0] + k, 4)
        for i in range(shots):
            for lev in range(2):
                base = pl.multiple_of(EDGE + 16 * y, 8)
                u_ref[i, lev, pl.ds(base, 16), :] = slabs[k][i, lev, 0:16, :]

        @pl.when(y == 3)
        def _():
            for i in range(shots):
                for lev in range(2):
                    u_ref[i, lev, 0:8, :] = slabs[k][i, lev, 16:24, :]

        @pl.when(y == 0)
        def _():
            for i in range(shots):
                for lev in range(2):
                    u_ref[i, lev, 72:80, :] = slabs[k][i, lev, 16:24, :]
                for t in range(3):
                    u_ref[i, 5 + t // 2, 6 + t % 2 : 7 + t % 2, :] = slabs[k][
                        i, t // 2, 22 + t % 2 : 23 + t % 2, :
                    ]

    coef = coef_ref[...]
    e_ref[...] = 2.0 - 4.0 * coef
    w_ref[...] = recv_ref[...] * recv_ref[...]

    odd = parity_ref[...] > 0.5
    for q in range(4):
        w = blocks[q][...]
        for colour in range(2):
            v = jnp.where(odd if colour else jnp.logical_not(odd), w, 0.0)
            for j, tile in enumerate(split(v)):
                v_ref.at[j][pl.ds(2 * q + colour, WIN, stride=8), :] = tile

    row = lax.broadcasted_iota(jnp.int32, (WIN, NZ), 0)
    column = lax.broadcasted_iota(jnp.int32, (WIN, NZ), 1)
    at_source = row == place[1]
    for i in range(shots):
        for t in range(3):
            before = u_ref[i, t]
            now = u_ref[i, t + 1]
            up = pltpu.roll(now, 1, 0)
            down = pltpu.roll(now, WIN - 1, 0)
            right = jnp.where(column == 0, 0.0, pltpu.roll(now, 1, 1))
            left = jnp.where(column == NZ - 1, 0.0, pltpu.roll(now, NZ - 1, 1))
            amp = u_ref[i, 5 + t // 2, 6 + t % 2 : 7 + t % 2, :]
            after = (
                2.0 * now
                - before
                + coef * (up + down + left + right - 4.0 * now)
                + jnp.where(at_source, amp, 0.0)
            )
            u_ref[i, t + 2] = after

    def block(r):
        return pl.ds(pl.multiple_of(8 * r, 8), 8)

    def field(ref, r):
        return [ref[j, block(r), :] for j in range(TILES)]

    def wide(ref, r):
        return split(ref[pl.ds(r, 1), :])

    def store(ref, r, tiles):
        for j in range(TILES):
            ref[j, block(r), :] = tiles[j]

    def level(i, l, r):
        return split(u_ref[i, l + 1, pl.ds(r, 1), :])

    def start(r, _):
        v = field(v_ref, r)
        for i in range(shots):
            u = level(i, 0, r)
            store(d_refs[i][0], r, [a * b for a, b in zip(v, u)])
        return 0

    lax.fori_loop(2, 78, start, 0, unroll=UNROLL)

    def forward(t, r, carry):
        v = field(v_ref, r)
        c = wide(coef_ref, r)
        e = wide(e_ref, r)
        out = []
        for i in range(shots):
            up, mid = carry[2 * i], carry[2 * i + 1]
            down = field(d_refs[i][t - 1], r + 1)
            side = sideways(mid, first, last)
            u = level(i, t, r)
            new = []
            for j in range(TILES):
                x = e[j] * mid[j] + c[j] * (up[j] + down[j] + side[j]) + v[j] * u[j]
                new.append(x)
            if t >= 2:
                prev = field(d_refs[i][t - 2], r)
                new = [a - b for a, b in zip(new, prev)]
            store(d_refs[i][t], r, new)
            out += [mid, down]
        return out

    for t in range(1, 4):
        lo, hi = 2 + t, 78 - t
        init = []
        for i in range(shots):
            init += [field(d_refs[i][t - 1], lo - 1), field(d_refs[i][t - 1], lo)]
        lax.fori_loop(lo, hi, functools.partial(forward, t), init, unroll=UNROLL)

    def first_adjoint(r, _):
        w = wide(w_ref, r)
        for i in range(shots):
            d = field(d_refs[i][3], r)
            store(d_refs[i][3], r, [a * b for a, b in zip(w, d)])
        return 0

    lax.fori_loop(5, 75, first_adjoint, 0, unroll=UNROLL)

    def adjoint(t, r, carry):
        w = wide(w_ref, r)
        e = wide(e_ref, r)
        cn = wide(coef_ref, r + 1)
        out = []
        for i in range(shots):
            up, mid, here = carry[3 * i], carry[3 * i + 1], carry[3 * i + 2]
            below = field(d_refs[i][t + 1], r + 1)
            down = [a * b for a, b in zip(cn, below)]
            side = sideways(mid, first, last)
            d = field(d_refs[i][t], r)
            new = []
            for j in range(TILES):
                new.append(w[j] * d[j] + e[j] * here[j] + (up[j] + down[j] + side[j]))
            if t <= 1:
                beyond = field(d_refs[i][t + 2], r)
                new = [a - b for a, b in zip(new, beyond)]
            store(d_refs[i][t], r, new)
            out += [mid, down, below]
        return out

    for t in (2, 1, 0):
        lo, hi = 8 - t, 72 + t
        init = []
        c0, c1 = wide(coef_ref, lo - 1), wide(coef_ref, lo)
        for i in range(shots):
            a0, a1 = field(d_refs[i][t + 1], lo - 1), field(d_refs[i][t + 1], lo)
            init += [
                [a * b for a, b in zip(c0, a0)],
                [a * b for a, b in zip(c1, a1)],
                a1,
            ]
        lax.fori_loop(lo, hi, functools.partial(adjoint, t), init, unroll=UNROLL)

    def gather(r, _):
        total = None
        for i in range(shots):
            for t in range(4):
                a = field(d_refs[i][t], r)
                u = level(i, t, r)
                term = [p * q for p, q in zip(a, u)]
                total = term if total is None else [p + q for p, q in zip(total, term)]
        store(grad_ref, r - EDGE, total)
        return 0

    lax.fori_loop(EDGE, EDGE + CHUNK, gather, 0, unroll=UNROLL)

    odd = parity_ref[EDGE : EDGE + CHUNK, :] > 0.5
    for q in range(4):
        for j in range(TILES):
            here = slice(LANES * j, LANES * (j + 1))
            even = grad_ref.at[j][pl.ds(2 * q, CHUNK, stride=8), :]
            other = grad_ref.at[j][pl.ds(2 * q + 1, CHUNK, stride=8), :]
            result = jnp.where(odd[:, here], even, other)
            if has_total:
                result = result + totals[q][:, here]
            outs[q][:, here] = result


def apply(place, slabs, blocks, parity, coef, recv, totals=()):
    shots = slabs[0].shape[0]
    vm = pl.BlockSpec(memory_space=pltpu.VMEM)
    args = [*slabs, *blocks, parity, coef, recv, *totals]
    big = pltpu.VMEM((TILES, 8 * WIN, LANES), jnp.float32)
    return pl.pallas_call(
        functools.partial(kernel, shots=shots, has_total=bool(totals)),
        out_shape=[jax.ShapeDtypeStruct((CHUNK, NZ), jnp.float32)] * 4,
        in_specs=[pl.BlockSpec(memory_space=pltpu.SMEM)] + [vm] * len(args),
        out_specs=[vm] * 4,
        scratch_shapes=[
            pltpu.VMEM((shots, 7, WIN, NZ), jnp.float32),
            big,
            pltpu.VMEM((WIN, NZ), jnp.float32),
            pltpu.VMEM((WIN, NZ), jnp.float32),
            pltpu.VMEM((TILES, 8 * CHUNK, LANES), jnp.float32),
        ]
        + [big] * (4 * shots),
        compiler_params=pltpu.CompilerParams(vmem_limit_bytes=56 * 1024 * 1024),
        cost_estimate=pl.CostEstimate(
            flops=shots * 8 * 8 * 70 * 512 * 12, bytes_accessed=4 << 20, transcendentals=0
        ),
        name="hessian_rows",
    )(place, *args)


AXES = ("shot", "probe")


def index(x, zh, y, zl, c):
    return (zl * 2 + c) * 32 + x * 8 + zh * 4 + y


def routes(source_of):
    pairs = []
    for x in range(4):
        for zh in range(2):
            for y in range(4):
                for zl in range(4):
                    for c in range(2):
                        source = source_of(x, zh, y, zl, c)
                        if source is not None:
                            pairs.append((index(*source), index(x, zh, y, zl, c)))
    return pairs


def main_source(k, x, zh, y, zl, c):
    return zl, c, y, x, zh ^ k


def edge_source(k, x, zh, y, zl, c):
    chunk = zl * 2 + c + {0: 1, 3: -1}.get(y, 8)
    if chunk < 0 or chunk > 7:
        return None
    return chunk // 2, chunk % 2, y, x, zh ^ k


def along_y(k):
    return routes(lambda x, zh, y, zl, c: (x, zh, (y + k) % 4, zl, c))


def along_x(k):
    return routes(lambda x, zh, y, zl, c: ((x + k) % 4, zh, y, zl, c))


def shot_sources(encodings, wavelet):
    columns = jnp.arange(NZ)
    position = jnp.arange(NSHOT) * 2 + 1
    onehot = (position[:, None] == columns[None, :]).astype(jnp.float32)
    amplitude = encodings.astype(jnp.float32)[:, None, :] * wavelet[None, :, :]
    return jnp.einsum("stk,kz->stz", amplitude, onehot, precision=lax.Precision.HIGHEST)


def block_parity(row_index, bounds):
    inner = bounds[1:-1]
    return jnp.sum((row_index[:, None] >= inner[None, :]).astype(jnp.int32), axis=1) % 2


def window(array, chunk, dim):
    rows = array.shape[dim]
    top = lax.dynamic_slice_in_dim(array, jnp.maximum(chunk * CHUNK - EDGE, 0), EDGE, dim)
    mid = lax.dynamic_slice_in_dim(array, chunk * CHUNK, CHUNK, dim)
    low = lax.dynamic_slice_in_dim(
        array, jnp.minimum(chunk * CHUNK + CHUNK, rows - EDGE), EDGE, dim
    )
    return jnp.concatenate([top, mid, low], axis=dim)


def on_device(
    probes, coarse_sample, coefficient, receiver, checkpoints, encodings, wavelet, bounds
):
    chunk = lax.axis_index("shot")
    y = lax.axis_index("probe") % 4
    sources = shot_sources(encodings, wavelet)

    extra = jnp.concatenate([sources, jnp.zeros_like(sources[:, :1])], axis=1)
    extra = extra.reshape(2, 2, 2, NZ)
    below = jnp.concatenate([checkpoints[:, :, :6], extra], axis=2)
    edge = jnp.where(y == 0, below, checkpoints[:, :, 8:])

    slabs = []
    for k in range(2):
        main = lax.ppermute(checkpoints, AXES, routes(functools.partial(main_source, k)))
        side = lax.ppermute(edge, AXES, routes(functools.partial(edge_source, k)))
        own = jnp.concatenate([main, side], axis=2)
        slabs.append([own] + [lax.ppermute(own, AXES, along_y(d)) for d in (1, 2, 3)])

    row = chunk * CHUNK - EDGE + jnp.arange(WIN)
    inside = ((row >= 0) & (row < 512))[:, None]
    parity = block_parity(row, bounds)
    odd = (parity == 1)[:, None]
    pair = window(probes, chunk, 1)
    mine = jnp.where(inside, jnp.where(odd, pair[1], pair[0]), 0.0)
    blocks = [mine] + [lax.ppermute(mine, AXES, along_x(d)) for d in (1, 2, 3)]
    coef = jnp.where(inside, window(coefficient, chunk, 0), 0.0)
    recv = jnp.where(inside, window(receiver, chunk, 0), 0.0)
    colours = jnp.broadcast_to(odd.astype(jnp.float32), (WIN, NZ))
    place = jnp.stack([y, 256 - chunk * CHUNK + EDGE]).astype(jnp.int32)

    terms = apply(place, slabs[0], blocks, colours, coef, recv)
    terms = apply(place, slabs[1], blocks, colours, coef, recv, terms)
    total = terms[0]
    for d in (1, 2, 3):
        total = total + lax.ppermute(terms[d], AXES, along_x(4 - d))

    keep = odd[EDGE : EDGE + CHUNK]
    return jnp.stack(
        [
            jnp.where(keep, total - coarse_sample[0], 0.0),
            jnp.where(keep, 0.0, total - coarse_sample[1]),
        ]
    )


def solution(mesh):
    return jax.shard_map(
        on_device,
        mesh=mesh,
        in_specs=(
            P("probe", None, None),
            P("probe", "shot", None),
            P(),
            P(),
            P("shot", None, "probe", None),
            P("shot", None),
            P(),
            P(),
        ),
        out_specs=P("probe", "shot", None),
        check_vma=False,
    )
```

time: 447 us -> 117 us (0.26)
  waiting for transfers between devices: 278 us -> 18.6 us
  other arithmetic: 92.2 us -> 3.4 us
  Pallas kernels: 0 us -> 41.4 us
  between operations: 13.6 us -> 0.35 us
  local copies, waits for them, and re-layouts: 10.8 us -> 6.25 us
    all_gather x2 -> x0, waiting for transfers between devices: 181 us -> none  [on_device(): levels = lax.all_gather(jnp.stack(history), 'probe', axis=1, tiled=True)]
    psum x1 -> x0, waiting for transfers between devices: 77 us -> none  [on_device(): summed = lax.psum(accumulated, 'shot')]
    mul x7 -> x0, other arithmetic: 53 us -> none  [the longest x4 48.4 us: hessian_term(): coefficient * upcoming]
    pallas_call x0 -> x2, Pallas kernels: none -> 41.4 us  [apply(): pl.pallas_call(functools.partial(kernel, shots=shots, has_total=bool(tota...]
    add x11 -> x2, other arithmetic: 33.7 us -> 0.01 us  [the longest x1 0.01 us: shot_sources(): position = jnp.arange(NSHOT) * 2 + 1]
    mul x2 -> x0, local copies, waits for them, and re-layouts: 8 us -> none  [hessian_term(): vectors * levels[moment]]
    ppermute x12 -> x16, starting transfers between devices: 50 us -> 46.6 us  [the longest x3 22 us: on_device(): total = total + lax.ppermute(terms[d], AXES, along_x(4 - d))]
    ppermute x12 -> x16, waiting for transfers between devices: 20.5 us -> 18.6 us  [the longest x2 7.14 us: on_device(): side = lax.ppermute(edge, AXES, routes(functools.partial(edge_source, k)))]
  transfers between devices with their start and end apart: 15 -> 16, of which waited for: 9 -> 7; matrix products, arithmetic and copies ran while one was open for 3% -> 2% of each run, Pallas kernels for 0% -> 18%
where the time goes in v1:
time: 117 us
  starting transfers between devices  46.6 us (40%)
  Pallas kernels  41.4 us (35%)
  waiting for transfers between devices  18.6 us (16%)
  local copies, waits for them, and re-layouts  6.25 us (5%)
  other arithmetic  3.4 us (3%)
    pallas_call x2, Pallas kernels, apply(): pl.pallas_call(functools.partial(kernel, shots=shots, has_total=bool(tota...  41.4 us
    ppermute x3, starting transfers between devices, on_device(): total = total + lax.ppermute(terms[d], AXES, along_x(4 - d))  22 us
    ppermute x2, starting transfers between devices, on_device(): lax.ppermute(checkpoints, AXES, routes(functools.partial(main_source, k)))  10.3 us
    ppermute x6, starting transfers between devices, on_device(): lax.ppermute(own, AXES, along_y(d))  7.33 us
    ppermute x2, waiting for transfers between devices, on_device(): side = lax.ppermute(edge, AXES, routes(functools.partial(edge_source, k)))  7.14 us
    ppermute x3, waiting for transfers between devices, on_device(): total = total + lax.ppermute(terms[d], AXES, along_x(4 - d))  6.34 us
    ppermute x3, starting transfers between devices, on_device(): blocks = [mine] + [lax.ppermute(mine, AXES, along_x(d)) for d in (1, 2, 3)]  4.43 us
    ppermute x6, waiting for transfers between devices, on_device(): lax.ppermute(own, AXES, along_y(d))  2.75 us
  transfers between devices with their start and end apart: 16, of which 7 were waited for; matrix products, arithmetic and copies ran while one was open for 2% of the time, Pallas kernels for 18%

profile of v1, /device:TPU:1, one launch (start us, length us, event | category | flops | bytes accessed | tf_op | source)
XLA Modules:
  0.0 117.0 jit_solution(7177618852418122831)
XLA Ops:
  0.0 1.0 constant_dynamic-slice_fusion.7
  1.1 0.9 constant_dynamic-slice_fusion.8
  2.0 0.8 constant_dynamic-slice_fusion.2
  2.8 1.0 constant_dynamic-slice_fusion.1
  3.8 0.7 slice.25
  4.5 0.1 convert_reduce_fusion
  4.7 0.8 maximum_select_fusion.1
  5.5 3.3 %collective-permute-start.5 = (f32[80,512]{1,0:T(8,128)S(1)}, f32[80,512]{1,0:T(8,128)S(1)}, u32[]{:S(2)}, u32[]{:S(2)}) collective-permute-start(f32[80,512]{1,0:T(8,128)S(1)} %get-tuple-element.33.refs_4_), channel_id=1, source_target_pairs={{8,0},{40,32},{72,64},{104,96},{136,128},{168,160},{200,192},{232,... | collective-permute-start | bytes 491528 | tf_op jit(solution)/shard_map/ppermute | solution.py:340
  8.8 0.5 collective-permute-start.6
  9.3 0.6 collective-permute-start.7
  10.0 10.2 %collective-permute-start.8 = (f32[2,2,16,512]{3,2,1,0:T(8,128)S(1)}, f32[2,2,16,512]{3,2,1,0:T(8,128)S(1)}, u32[]{:S(2)}, u32[]{:S(2)}) collective-permute-start(f32[2,2,16,512]{3,2,1,0:T(8,128)S(1)} %copy-done.13), channel_id=1, source_target_pairs={{0,0},{4,32},{8,64},{12,96},{16,128},{20,160},{24,192},{28,224},{1... | collective-permute-start | bytes 393224 | tf_op jit(solution)/shard_map/ppermute | solution.py:329
  20.2 0.1 collective-permute-start
  20.4 0.3 fusion.1
  20.8 2.3 %collective-permute-done.8 = f32[2,2,16,512]{3,2,1,0:T(8,128)S(1)} collective-permute-done((f32[2,2,16,512]{3,2,1,0:T(8,128)S(1)}, f32[2,2,16,512]{3,2,1,0:T(8,128)S(1)}, u32[]{:S(2)}, u32[]{:S(2)}) %collective-permute-start.8) | collective-permute-done | bytes 131104 | tf_op jit(solution)/shard_map/ppermute | solution.py:329
  23.1 1.3 %collective-permute-start.9 = (f32[2,2,8,512]{3,2,1,0:T(8,128)S(1)}, f32[2,2,8,512]{3,2,1,0:T(8,128)S(1)}, u32[]{:S(2)}, u32[]{:S(2)}) collective-permute-start(f32[2,2,8,512]{3,2,1,0:T(8,128)S(1)} %maximum_select_fusion.2), channel_id=1, source_target_pairs={{4,0},{8,32},{12,64},{16,96},{20,128},{24,160},{28,192},{3,35},{7,... | collective-permute-start | bytes 196616 | tf_op jit(solution)/shard_map/ppermute | solution.py:330
  24.4 4.3 %collective-permute-done.9 = f32[2,2,8,512]{3,2,1,0:T(8,128)S(1)} collective-permute-done((f32[2,2,8,512]{3,2,1,0:T(8,128)S(1)}, f32[2,2,8,512]{3,2,1,0:T(8,128)S(1)}, u32[]{:S(2)}, u32[]{:S(2)}) %collective-permute-start.9) | collective-permute-done | bytes 65568 | tf_op jit(solution)/shard_map/ppermute | solution.py:330
  28.7 1.3 %collective-permute-start.1 = (f32[2,2,8,512]{3,2,1,0:T(8,128)S(1)}, f32[2,2,8,512]{3,2,1,0:T(8,128)S(1)}, u32[]{:S(2)}, u32[]{:S(2)}) collective-permute-start(f32[2,2,8,512]{3,2,1,0:T(8,128)S(1)} %maximum_select_fusion.2), channel_id=1, source_target_pairs={{36,0},{40,32},{44,64},{48,96},{52,128},{56,160},{60,192},{35,35},... | collective-permute-start | bytes 196616 | tf_op jit(solution)/shard_map/ppermute | solution.py:330
  30.0 0.0 collective-permute-done
  30.0 2.8 %collective-permute-start.10 = (f32[2,2,24,512]{3,2,1,0:T(8,128)S(1)}, f32[2,2,24,512]{3,2,1,0:T(8,128)S(1)}, u32[]{:S(2)}, u32[]{:S(2)}) collective-permute-start(f32[2,2,24,512]{3,2,1,0:T(8,128)S(1)} %constant_dynamic-update-slice_fusion.2.refs_0_), channel_id=1, source_target_pairs={{1,0},{33,32},{65,64},{97,96},{129,128},{161,160},{193,192},{225,2... | collective-permute-start | bytes 589832 | tf_op jit(solution)/shard_map/ppermute | solution.py:332
  32.9 2.9 %collective-permute-done.1 = f32[2,2,8,512]{3,2,1,0:T(8,128)S(1)} collective-permute-done((f32[2,2,8,512]{3,2,1,0:T(8,128)S(1)}, f32[2,2,8,512]{3,2,1,0:T(8,128)S(1)}, u32[]{:S(2)}, u32[]{:S(2)}) %collective-permute-start.1) | collective-permute-done | bytes 65568 | tf_op jit(solution)/shard_map/ppermute | solution.py:330
  35.7 0.0 collective-permute-start.11
  35.7 0.0 collective-permute-done.5.refs_5_
  35.7 0.1 collective-permute-start.12
  35.8 0.0 copy-start.5
  35.9 0.0 collective-permute-done.6.refs_6_
  35.9 2.7 %collective-permute-start.2 = (f32[2,2,24,512]{3,2,1,0:T(8,128)S(1)}, f32[2,2,24,512]{3,2,1,0:T(8,128)S(1)}, u32[]{:S(2)}, u32[]{:S(2)}) collective-permute-start(f32[2,2,24,512]{3,2,1,0:T(8,128)S(1)} %constant_dynamic-update-slice_fusion.refs_0_), channel_id=1, source_target_pairs={{1,0},{33,32},{65,64},{97,96},{129,128},{161,160},{193,192},{225,2... | collective-permute-start | bytes 589832 | tf_op jit(solution)/shard_map/ppermute | solution.py:332
  38.6 0.0 collective-permute-done.7.refs_7_
  38.6 1.7 %collective-permute-start.3 = (f32[2,2,24,512]{3,2,1,0:T(8,128)S(1)}, f32[2,2,24,512]{3,2,1,0:T(8,128)S(1)}, u32[]{:S(2)}, u32[]{:S(2)}) collective-permute-start(f32[2,2,24,512]{3,2,1,0:T(8,128)S(1)} %constant_dynamic-update-slice_fusion.refs_0_), channel_id=1, source_target_pairs={{2,0},{34,32},{66,64},{98,96},{130,128},{162,160},{194,192},{226,2... | collective-permute-start | bytes 589832 | tf_op jit(solution)/shard_map/ppermute | solution.py:332
  40.3 0.6 pad_add_fusion.place
  40.9 0.9 collective-permute-done.11.refs_2_
  41.9 1.8 %collective-permute-done.12.refs_3_ = f32[2,2,24,512]{3,2,1,0:T(8,128)S(1)} collective-permute-done((f32[2,2,24,512]{3,2,1,0:T(8,128)S(1)}, f32[2,2,24,512]{3,2,1,0:T(8,128)S(1)}, u32[]{:S(2)}, u32[]{:S(2)}) %collective-permute-start.12) | collective-permute-done | bytes 196640 | tf_op jit(solution)/shard_map/ppermute | solution.py:332
  43.7 0.8 broadcast_in_dim.66.refs_8_
  44.5 0.0 copy-start.6
  44.5 20.5 %hessian_rows.2 = (f32[64,512]{1,0:T(8,128)}, f32[64,512]{1,0:T(8,128)}, f32[64,512]{1,0:T(8,128)}, f32[64,512]{1,0:T(8,128)}) custom-call(s32[2]{0:T(128)} %pad_add_fusion.place, f32[2,2,24,512]{3,2,1,0:T(8,128)} %copy-done.4, f32[2,2,24,512]{3,2,1,0:T(8,128)} %copy-done.7, f32[2,2,24,512]{3,2,1,0:T(8,128)} %copy-done.8, f32[2,2,24,512]{3,2,1,0:T(8,128)} %copy-done.9, ...), custom_call_target="tpu_custom_call" | custom-call | flops 55050240 | bytes 4194304 | tf_op jit(solution)/shard_map/hessian_rows/pallas_call | solution.py:232
  65.0 0.0 collective-permute-done.2.refs_1_
  65.0 0.0 collective-permute-done.3.refs_2_
  65.1 0.6 copy-done.10
  65.7 0.1 copy-done.11
  65.8 0.1 copy-done.12
  65.9 20.8 %hessian_rows.3 = (f32[64,512]{1,0:T(8,128)}, f32[64,512]{1,0:T(8,128)}, f32[64,512]{1,0:T(8,128)}, f32[64,512]{1,0:T(8,128)}) custom-call(s32[2]{0:T(128)} %pad_add_fusion.place, f32[2,2,24,512]{3,2,1,0:T(8,128)} %copy-done.5, f32[2,2,24,512]{3,2,1,0:T(8,128)} %copy-done.10, f32[2,2,24,512]{3,2,1,0:T(8,128)} %copy-done.11, f32[2,2,24,512]{3,2,1,0:T(8,128)} %copy-done.12, ...), custom_call_target="tpu_custom_call" | custom-call | flops 55050240 | bytes 4194304 | tf_op jit(solution)/shard_map/hessian_rows/pallas_call | solution.py:232
  86.7 4.8 %collective-permute-start.13 = (f32[64,512]{1,0:T(8,128)}, f32[64,512]{1,0:T(8,128)S(1)}, u32[]{:S(2)}, u32[]{:S(2)}) collective-permute-start(f32[64,512]{1,0:T(8,128)} %get-tuple-element.18), channel_id=1, source_target_pairs={{24,0},{56,32},{88,64},{120,96},{152,128},{184,160},{216,192},{248... | collective-permute-start | bytes 393224 | tf_op jit(solution)/shard_map/ppermute | solution.py:350
  91.6 17.2 %collective-permute-start.14 = (f32[64,512]{1,0:T(8,128)}, f32[64,512]{1,0:T(8,128)S(1)}, u32[]{:S(2)}, u32[]{:S(2)}) collective-permute-start(f32[64,512]{1,0:T(8,128)} %get-tuple-element.19), channel_id=1, source_target_pairs={{16,0},{48,32},{80,64},{112,96},{144,128},{176,160},{208,192},{240... | collective-permute-start | bytes 393224 | tf_op jit(solution)/shard_map/ppermute | solution.py:350
  108.7 0.1 slice.26
  108.8 2.7 %collective-permute-done.13 = f32[64,512]{1,0:T(8,128)S(1)} collective-permute-done((f32[64,512]{1,0:T(8,128)}, f32[64,512]{1,0:T(8,128)S(1)}, u32[]{:S(2)}, u32[]{:S(2)}) %collective-permute-start.13) | collective-permute-done | bytes 131104 | tf_op jit(solution)/shard_map/ppermute | solution.py:350
  111.5 3.7 %collective-permute-done.14 = f32[64,512]{1,0:T(8,128)S(1)} collective-permute-done((f32[64,512]{1,0:T(8,128)}, f32[64,512]{1,0:T(8,128)S(1)}, u32[]{:S(2)}, u32[]{:S(2)}) %collective-permute-start.14) | collective-permute-done | bytes 131104 | tf_op jit(solution)/shard_map/ppermute | solution.py:350
  115.2 1.0 fusion.9
  116.1 0.1 fusion.7
  116.2 0.7 pad_maximum_fusion.1
  (45 shorter events, 0.2 us)
Async XLA Ops:
  0.0 10.0 %copy-start.13 = (f32[2,2,16,512]{3,2,1,0:T(8,128)S(1)}, f32[2,2,16,512]{3,2,1,0:T(8,128)}, u32[]{:S(2)}) copy-start(f32[2,2,16,512]{3,2,1,0:T(8,128)} %param.12) | copy-start | bytes 393220
  0.0 20.3 %copy-start.14 = (s32[2,256]{1,0:T(2,128)S(1)}, s32[2,256]{1,0:T(2,128)}, u32[]{:S(2)}) copy-start(s32[2,256]{1,0:T(2,128)} %param.13) | copy-start | bytes 6148
  0.0 20.3 %copy-start.15 = (f32[3,256]{1,0:T(4,128)S(1)}, f32[3,256]{1,0:T(4,128)}, u32[]{:S(2)}) copy-start(f32[3,256]{1,0:T(4,128)} %param.14) | copy-start | bytes 9220
  5.5 38.9 %copy-start = (f32[80,512]{1,0:T(8,128)}, f32[80,512]{1,0:T(8,128)S(1)}, u32[]{:S(2)}) copy-start(f32[80,512]{1,0:T(8,128)S(1)} %get-tuple-element.33.refs_4_) | copy-start | bytes 491524
  5.5 30.2 %collective-permute-start.5 = (f32[80,512]{1,0:T(8,128)S(1)}, f32[80,512]{1,0:T(8,128)S(1)}, u32[]{:S(2)}, u32[]{:S(2)}) collective-permute-start(f32[80,512]{1,0:T(8,128)S(1)} %get-tuple-element.33.refs_4_), channel_id=1, source_target_pairs={{8,0},{40,32},{72,64},{104,96},{136,128},{168,160},{200,192},{232,... | collective-permute-start | bytes 491528 | tf_op jit(solution)/shard_map/ppermute | solution.py:340
  8.8 27.0 %collective-permute-start.6 = (f32[80,512]{1,0:T(8,128)S(1)}, f32[80,512]{1,0:T(8,128)S(1)}, u32[]{:S(2)}, u32[]{:S(2)}) collective-permute-start(f32[80,512]{1,0:T(8,128)S(1)} %get-tuple-element.33.refs_4_), channel_id=1, source_target_pairs={{16,0},{48,32},{80,64},{112,96},{144,128},{176,160},{208,192},{240... | collective-permute-start | bytes 491528 | tf_op jit(solution)/shard_map/ppermute | solution.py:340
  9.3 29.3 %collective-permute-start.7 = (f32[80,512]{1,0:T(8,128)S(1)}, f32[80,512]{1,0:T(8,128)S(1)}, u32[]{:S(2)}, u32[]{:S(2)}) collective-permute-start(f32[80,512]{1,0:T(8,128)S(1)} %get-tuple-element.33.refs_4_), channel_id=1, source_target_pairs={{24,0},{56,32},{88,64},{120,96},{152,128},{184,160},{216,192},{248... | collective-permute-start | bytes 491528 | tf_op jit(solution)/shard_map/ppermute | solution.py:340
  10.0 13.1 %collective-permute-start.8 = (f32[2,2,16,512]{3,2,1,0:T(8,128)S(1)}, f32[2,2,16,512]{3,2,1,0:T(8,128)S(1)}, u32[]{:S(2)}, u32[]{:S(2)}) collective-permute-start(f32[2,2,16,512]{3,2,1,0:T(8,128)S(1)} %copy-done.13), channel_id=1, source_target_pairs={{0,0},{4,32},{8,64},{12,96},{16,128},{20,160},{24,192},{28,224},{1... | collective-permute-start | bytes 393224 | tf_op jit(solution)/shard_map/ppermute | solution.py:329
  20.2 9.8 %collective-permute-start = (f32[2,2,16,512]{3,2,1,0:T(8,128)S(1)}, f32[2,2,16,512]{3,2,1,0:T(8,128)S(1)}, u32[]{:S(2)}, u32[]{:S(2)}) collective-permute-start(f32[2,2,16,512]{3,2,1,0:T(8,128)S(1)} %copy-done.13), channel_id=1, source_target_pairs={{32,0},{36,32},{40,64},{44,96},{48,128},{52,160},{56,192},{60,224}... | collective-permute-start | bytes 393224 | tf_op jit(solution)/shard_map/ppermute | solution.py:329
  23.1 5.6 %collective-permute-start.9 = (f32[2,2,8,512]{3,2,1,0:T(8,128)S(1)}, f32[2,2,8,512]{3,2,1,0:T(8,128)S(1)}, u32[]{:S(2)}, u32[]{:S(2)}) collective-permute-start(f32[2,2,8,512]{3,2,1,0:T(8,128)S(1)} %maximum_select_fusion.2), channel_id=1, source_target_pairs={{4,0},{8,32},{12,64},{16,96},{20,128},{24,160},{28,192},{3,35},{7,... | collective-permute-start | bytes 196616 | tf_op jit(solution)/shard_map/ppermute | solution.py:330
  28.7 7.1 %collective-permute-start.1 = (f32[2,2,8,512]{3,2,1,0:T(8,128)S(1)}, f32[2,2,8,512]{3,2,1,0:T(8,128)S(1)}, u32[]{:S(2)}, u32[]{:S(2)}) collective-permute-start(f32[2,2,8,512]{3,2,1,0:T(8,128)S(1)} %maximum_select_fusion.2), channel_id=1, source_target_pairs={{36,0},{40,32},{44,64},{48,96},{52,128},{56,160},{60,192},{35,35},... | collective-permute-start | bytes 196616 | tf_op jit(solution)/shard_map/ppermute | solution.py:330
  30.0 14.4 %copy-start.4 = (f32[2,2,24,512]{3,2,1,0:T(8,128)}, f32[2,2,24,512]{3,2,1,0:T(8,128)S(1)}, u32[]{:S(2)}) copy-start(f32[2,2,24,512]{3,2,1,0:T(8,128)S(1)} %constant_dynamic-update-slice_fusion.2.refs_0_) | copy-start | bytes 589828
  30.0 10.3 %collective-permute-start.10 = (f32[2,2,24,512]{3,2,1,0:T(8,128)S(1)}, f32[2,2,24,512]{3,2,1,0:T(8,128)S(1)}, u32[]{:S(2)}, u32[]{:S(2)}) collective-permute-start(f32[2,2,24,512]{3,2,1,0:T(8,128)S(1)} %constant_dynamic-update-slice_fusion.2.refs_0_), channel_id=1, source_target_pairs={{1,0},{33,32},{65,64},{97,96},{129,128},{161,160},{193,192},{225,2... | collective-permute-start | bytes 589832 | tf_op jit(solution)/shard_map/ppermute | solution.py:332
  35.7 6.1 %collective-permute-start.11 = (f32[2,2,24,512]{3,2,1,0:T(8,128)S(1)}, f32[2,2,24,512]{3,2,1,0:T(8,128)S(1)}, u32[]{:S(2)}, u32[]{:S(2)}) collective-permute-start(f32[2,2,24,512]{3,2,1,0:T(8,128)S(1)} %constant_dynamic-update-slice_fusion.2.refs_0_), channel_id=1, source_target_pairs={{2,0},{34,32},{66,64},{98,96},{130,128},{162,160},{194,192},{226,2... | collective-permute-start | bytes 589832 | tf_op jit(solution)/shard_map/ppermute | solution.py:332
  35.7 8.7 %copy-start.1 = (f32[80,512]{1,0:T(8,128)}, f32[80,512]{1,0:T(8,128)S(1)}, u32[]{:S(2)}) copy-start(f32[80,512]{1,0:T(8,128)S(1)} %collective-permute-done.5.refs_5_) | copy-start | bytes 491524
  35.7 7.9 %collective-permute-start.12 = (f32[2,2,24,512]{3,2,1,0:T(8,128)S(1)}, f32[2,2,24,512]{3,2,1,0:T(8,128)S(1)}, u32[]{:S(2)}, u32[]{:S(2)}) collective-permute-start(f32[2,2,24,512]{3,2,1,0:T(8,128)S(1)} %constant_dynamic-update-slice_fusion.2.refs_0_), channel_id=1, source_target_pairs={{3,0},{35,32},{67,64},{99,96},{131,128},{163,160},{195,192},{227,2... | collective-permute-start | bytes 589832 | tf_op jit(solution)/shard_map/ppermute | solution.py:332
  35.8 29.2 %copy-start.5 = (f32[2,2,24,512]{3,2,1,0:T(8,128)}, f32[2,2,24,512]{3,2,1,0:T(8,128)S(1)}, u32[]{:S(2)}) copy-start(f32[2,2,24,512]{3,2,1,0:T(8,128)S(1)} %constant_dynamic-update-slice_fusion.refs_0_) | copy-start | bytes 589828
  35.9 8.6 %copy-start.2 = (f32[80,512]{1,0:T(8,128)}, f32[80,512]{1,0:T(8,128)S(1)}, u32[]{:S(2)}) copy-start(f32[80,512]{1,0:T(8,128)S(1)} %collective-permute-done.6.refs_6_) | copy-start | bytes 491524
  35.9 29.1 %collective-permute-start.2 = (f32[2,2,24,512]{3,2,1,0:T(8,128)S(1)}, f32[2,2,24,512]{3,2,1,0:T(8,128)S(1)}, u32[]{:S(2)}, u32[]{:S(2)}) collective-permute-start(f32[2,2,24,512]{3,2,1,0:T(8,128)S(1)} %constant_dynamic-update-slice_fusion.refs_0_), channel_id=1, source_target_pairs={{1,0},{33,32},{65,64},{97,96},{129,128},{161,160},{193,192},{225,2... | collective-permute-start | bytes 589832 | tf_op jit(solution)/shard_map/ppermute | solution.py:332
  38.6 5.8 %copy-start.3 = (f32[80,512]{1,0:T(8,128)}, f32[80,512]{1,0:T(8,128)S(1)}, u32[]{:S(2)}) copy-start(f32[80,512]{1,0:T(8,128)S(1)} %collective-permute-done.7.refs_7_) | copy-start | bytes 491524
  38.6 26.4 %collective-permute-start.3 = (f32[2,2,24,512]{3,2,1,0:T(8,128)S(1)}, f32[2,2,24,512]{3,2,1,0:T(8,128)S(1)}, u32[]{:S(2)}, u32[]{:S(2)}) collective-permute-start(f32[2,2,24,512]{3,2,1,0:T(8,128)S(1)} %constant_dynamic-update-slice_fusion.refs_0_), channel_id=1, source_target_pairs={{2,0},{34,32},{66,64},{98,96},{130,128},{162,160},{194,192},{226,2... | collective-permute-start | bytes 589832 | tf_op jit(solution)/shard_map/ppermute | solution.py:332
  40.3 4.1 %copy-start.7 = (f32[2,2,24,512]{3,2,1,0:T(8,128)}, f32[2,2,24,512]{3,2,1,0:T(8,128)S(1)}, u32[]{:S(2)}) copy-start(f32[2,2,24,512]{3,2,1,0:T(8,128)S(1)} %collective-permute-done.10.refs_1_) | copy-start | bytes 589828
  40.3 24.8 %collective-permute-start.4 = (f32[2,2,24,512]{3,2,1,0:T(8,128)S(1)}, f32[2,2,24,512]{3,2,1,0:T(8,128)S(1)}, u32[]{:S(2)}, u32[]{:S(2)}) collective-permute-start(f32[2,2,24,512]{3,2,1,0:T(8,128)S(1)} %constant_dynamic-update-slice_fusion.refs_0_), channel_id=1, source_target_pairs={{3,0},{35,32},{67,64},{99,96},{131,128},{163,160},{195,192},{227,2... | collective-permute-start | bytes 589832 | tf_op jit(solution)/shard_map/ppermute | solution.py:332
  41.9 2.6 %copy-start.8 = (f32[2,2,24,512]{3,2,1,0:T(8,128)}, f32[2,2,24,512]{3,2,1,0:T(8,128)S(1)}, u32[]{:S(2)}) copy-start(f32[2,2,24,512]{3,2,1,0:T(8,128)S(1)} %collective-permute-done.11.refs_2_) | copy-start | bytes 589828
  43.7 0.8 copy-start.9
  44.5 70.7 %copy-start.6 = (f32[2,64,512]{2,1,0:T(8,128)S(1)}, f32[2,64,512]{2,1,0:T(8,128)}, u32[]{:S(2)}) copy-start(f32[2,64,512]{2,1,0:T(8,128)} %param.9) | copy-start | bytes 786436
  65.0 0.7 copy-start.10
  65.0 0.7 copy-start.11
  65.1 0.8 copy-start.12
  86.7 24.8 %collective-permute-start.13 = (f32[64,512]{1,0:T(8,128)}, f32[64,512]{1,0:T(8,128)S(1)}, u32[]{:S(2)}, u32[]{:S(2)}) collective-permute-start(f32[64,512]{1,0:T(8,128)} %get-tuple-element.18), channel_id=1, source_target_pairs={{24,0},{56,32},{88,64},{120,96},{152,128},{184,160},{216,192},{248... | collective-permute-start | bytes 393224 | tf_op jit(solution)/shard_map/ppermute | solution.py:350
  91.6 23.6 %collective-permute-start.14 = (f32[64,512]{1,0:T(8,128)}, f32[64,512]{1,0:T(8,128)S(1)}, u32[]{:S(2)}, u32[]{:S(2)}) collective-permute-start(f32[64,512]{1,0:T(8,128)} %get-tuple-element.19), channel_id=1, source_target_pairs={{16,0},{48,32},{80,64},{112,96},{144,128},{176,160},{208,192},{240... | collective-permute-start | bytes 393224 | tf_op jit(solution)/shard_map/ppermute | solution.py:350
  108.7 6.4 %collective-permute-start.15 = (f32[64,512]{1,0:T(8,128)}, f32[64,512]{1,0:T(8,128)S(1)}, u32[]{:S(2)}, u32[]{:S(2)}) collective-permute-start(f32[64,512]{1,0:T(8,128)} %get-tuple-element.20), channel_id=1, source_target_pairs={{8,0},{40,32},{72,64},{104,96},{136,128},{168,160},{200,192},{232,... | collective-permute-start | bytes 393224 | tf_op jit(solution)/shard_map/ppermute | solution.py:350

commit v2 on v1

--- a/solution.py
+++ b/solution.py
@@ -13,7 +13,7 @@
 EDGE = 8
 LANES = 128
 TILES = NZ // LANES
-UNROLL = 4
+UNROLLS = (74, 72, 70, 68, 66, 64)
 
 
 def split(row):
@@ -21,15 +21,9 @@
 
 
 def sideways(tiles, first, last):
-    right = [pltpu.roll(t, 1, 1) for t in tiles]
-    left = [pltpu.roll(t, LANES - 1, 1) for t in tiles]
-    zero = jnp.zeros_like(tiles[0])
-    out = []
-    for j in range(TILES):
-        a = jnp.where(first, right[j - 1] if j else zero, right[j])
-        b = jnp.where(last, left[j + 1] if j < TILES - 1 else zero, left[j])
-        out.append(a + b)
-    return out
+    left = jnp.where(first, 0.0, pltpu.roll(tiles[3], 1, 1))
+    right = jnp.where(last, 0.0, pltpu.roll(tiles[0], LANES - 1, 1))
+    return [left + tiles[1], tiles[0] + tiles[2], tiles[1] + tiles[3], tiles[2] + right]
 
 
 def kernel(place, *refs, shots, has_total):
@@ -83,25 +77,24 @@
             for j, tile in enumerate(split(v)):
                 v_ref.at[j][pl.ds(2 * q + colour, WIN, stride=8), :] = tile
 
-    row = lax.broadcasted_iota(jnp.int32, (WIN, NZ), 0)
-    column = lax.broadcasted_iota(jnp.int32, (WIN, NZ), 1)
+    row = lax.broadcasted_iota(jnp.int32, (WIN, LANES), 0)
+    column = lax.broadcasted_iota(jnp.int32, (WIN, LANES), 1)
     at_source = row == place[1]
     for i in range(shots):
         for t in range(3):
-            before = u_ref[i, t]
-            now = u_ref[i, t + 1]
-            up = pltpu.roll(now, 1, 0)
-            down = pltpu.roll(now, WIN - 1, 0)
-            right = jnp.where(column == 0, 0.0, pltpu.roll(now, 1, 1))
-            left = jnp.where(column == NZ - 1, 0.0, pltpu.roll(now, NZ - 1, 1))
-            amp = u_ref[i, 5 + t // 2, 6 + t % 2 : 7 + t % 2, :]
-            after = (
-                2.0 * now
-                - before
-                + coef * (up + down + left + right - 4.0 * now)
-                + jnp.where(at_source, amp, 0.0)
-            )
-            u_ref[i, t + 2] = after
+            now = split(u_ref[i, t + 1])
+            side = sideways(now, column == 0, column == LANES - 1)
+            for j in range(TILES):
+                here = slice(LANES * j, LANES * (j + 1))
+                up = pltpu.roll(now[j], 1, 0)
+                down = pltpu.roll(now[j], WIN - 1, 0)
+                amp = u_ref[i, 5 + t // 2, 6 + t % 2 : 7 + t % 2, here]
+                u_ref[i, t + 2, :, here] = (
+                    e_ref[:, here] * now[j]
+                    - u_ref[i, t, :, here]
+                    + coef_ref[:, here] * (up + down + side[j])
+                    + jnp.where(at_source, amp, 0.0)
+                )
 
     def block(r):
         return pl.ds(pl.multiple_of(8 * r, 8), 8)
@@ -119,33 +112,40 @@
     def level(i, l, r):
         return split(u_ref[i, l + 1, pl.ds(r, 1), :])
 
-    def start(r, _):
-        v = field(v_ref, r)
-        for i in range(shots):
-            u = level(i, 0, r)
-            store(d_refs[i][0], r, [a * b for a, b in zip(v, u)])
-        return 0
-
-    lax.fori_loop(2, 78, start, 0, unroll=UNROLL)
+    def times(a, b):
+        return [p * q for p, q in zip(a, b)]
+
+    def plus(a, b):
+        return [p + q for p, q in zip(a, b)]
+
+    def minus(a, b):
+        return [p - q for p, q in zip(a, b)]
+
+    def stencil(c, e, up, mid, down):
+        side = sideways(mid, first, last)
+        return plus(times(e, mid), times(c, plus(plus(up, down), side)))
+
+    def source(i, r):
+        return times(field(v_ref, r), level(i, 0, r))
 
     def forward(t, r, carry):
         v = field(v_ref, r)
         c = wide(coef_ref, r)
         e = wide(e_ref, r)
+        w = wide(w_ref, r) if t == 3 else None
+        ahead = field(v_ref, r + 1) if t == 1 else None
         out = []
         for i in range(shots):
             up, mid = carry[2 * i], carry[2 * i + 1]
-            down = field(d_refs[i][t - 1], r + 1)
-            side = sideways(mid, first, last)
-            u = level(i, t, r)
-            new = []
-            for j in range(TILES):
-                x = e[j] * mid[j] + c[j] * (up[j] + down[j] + side[j]) + v[j] * u[j]
-                new.append(x)
+            if t == 1:
+                down = times(ahead, level(i, 0, r + 1))
+                store(d_refs[i][0], r + 1, down)
+            else:
+                down = field(d_refs[i][t - 1], r + 1)
+            new = plus(stencil(c, e, up, mid, down), times(v, level(i, t, r)))
             if t >= 2:
-                prev = field(d_refs[i][t - 2], r)
-                new = [a - b for a, b in zip(new, prev)]
-            store(d_refs[i][t], r, new)
+                new = minus(new, field(d_refs[i][t - 2], r))
+            store(d_refs[i][t], r, times(w, new) if t == 3 else new)
             out += [mid, down]
         return out
 
@@ -153,37 +153,40 @@
         lo, hi = 2 + t, 78 - t
         init = []
         for i in range(shots):
-            init += [field(d_refs[i][t - 1], lo - 1), field(d_refs[i][t - 1], lo)]
-        lax.fori_loop(lo, hi, functools.partial(forward, t), init, unroll=UNROLL)
-
-    def first_adjoint(r, _):
-        w = wide(w_ref, r)
-        for i in range(shots):
-            d = field(d_refs[i][3], r)
-            store(d_refs[i][3], r, [a * b for a, b in zip(w, d)])
-        return 0
-
-    lax.fori_loop(5, 75, first_adjoint, 0, unroll=UNROLL)
+            if t == 1:
+                rows = [source(i, lo - 1), source(i, lo)]
+                store(d_refs[i][0], lo, rows[1])
+            else:
+                rows = [field(d_refs[i][t - 1], lo - 1), field(d_refs[i][t - 1], lo)]
+            init += rows
+        lax.fori_loop(lo, hi, functools.partial(forward, t), init, unroll=UNROLLS[t - 1])
 
     def adjoint(t, r, carry):
         w = wide(w_ref, r)
         e = wide(e_ref, r)
         cn = wide(coef_ref, r + 1)
         out = []
+        total = None
         for i in range(shots):
             up, mid, here = carry[3 * i], carry[3 * i + 1], carry[3 * i + 2]
             below = field(d_refs[i][t + 1], r + 1)
-            down = [a * b for a, b in zip(cn, below)]
+            down = times(cn, below)
             side = sideways(mid, first, last)
-            d = field(d_refs[i][t], r)
-            new = []
-            for j in range(TILES):
-                new.append(w[j] * d[j] + e[j] * here[j] + (up[j] + down[j] + side[j]))
+            new = plus(times(w, field(d_refs[i][t], r)), times(e, here))
+            new = plus(new, plus(plus(up, down), side))
             if t <= 1:
                 beyond = field(d_refs[i][t + 2], r)
-                new = [a - b for a, b in zip(new, beyond)]
-            store(d_refs[i][t], r, new)
+                new = minus(new, beyond)
+            if t == 0:
+                final = field(d_refs[i][3], r)
+                for l, a in enumerate((new, here, beyond, final)):
+                    term = times(a, level(i, l, r))
+                    total = term if total is None else plus(total, term)
+            else:
+                store(d_refs[i][t], r, new)
             out += [mid, down, below]
+        if t == 0:
+            store(grad_ref, r - EDGE, total)
         return out
 
     for t in (2, 1, 0):
@@ -192,25 +195,8 @@
         c0, c1 = wide(coef_ref, lo - 1), wide(coef_ref, lo)
         for i in range(shots):
             a0, a1 = field(d_refs[i][t + 1], lo - 1), field(d_refs[i][t + 1], lo)
-            init += [
-                [a * b for a, b in zip(c0, a0)],
-                [a * b for a, b in zip(c1, a1)],
-                a1,
-            ]
-        lax.fori_loop(lo, hi, functools.partial(adjoint, t), init, unroll=UNROLL)
-
-    def gather(r, _):
-        total = None
-        for i in range(shots):
-            for t in range(4):
-                a = field(d_refs[i][t], r)
-                u = level(i, t, r)
-                term = [p * q for p, q in zip(a, u)]
-                total = term if total is None else [p + q for p, q in zip(total, term)]
-        store(grad_ref, r - EDGE, total)
-        return 0
-
-    lax.fori_loop(EDGE, EDGE + CHUNK, gather, 0, unroll=UNROLL)
+            init += [times(c0, a0), times(c1, a1), a1]
+        lax.fori_loop(lo, hi, functools.partial(adjoint, t), init, unroll=UNROLLS[5 - t])
 
     odd = parity_ref[EDGE : EDGE + CHUNK, :] > 0.5
     for q in range(4):
@@ -289,9 +275,25 @@
     return routes(lambda x, zh, y, zl, c: ((x + k) % 4, zh, y, zl, c))
 
 
+def place_of(column):
+    return column % TILES * LANES + column // TILES
+
+
+def reorder(array, back=False):
+    columns = jnp.arange(NZ)
+    match = columns[None, :] == place_of(columns)[:, None]
+    match = match.T if back else match
+    return lax.dot_general(
+        array,
+        match.astype(jnp.float32),
+        (((array.ndim - 1,), (0,)), ((), ())),
+        precision=lax.Precision.HIGHEST,
+    )
+
+
 def shot_sources(encodings, wavelet):
     columns = jnp.arange(NZ)
-    position = jnp.arange(NSHOT) * 2 + 1
+    position = place_of(jnp.arange(NSHOT) * 2 + 1)
     onehot = (position[:, None] == columns[None, :]).astype(jnp.float32)
     amplitude = encodings.astype(jnp.float32)[:, None, :] * wavelet[None, :, :]
     return jnp.einsum("stk,kz->stz", amplitude, onehot, precision=lax.Precision.HIGHEST)
@@ -318,30 +320,35 @@
     chunk = lax.axis_index("shot")
     y = lax.axis_index("probe") % 4
     sources = shot_sources(encodings, wavelet)
+    checkpoints = reorder(checkpoints)
+
+    row = chunk * CHUNK - EDGE + jnp.arange(WIN)
+    inside = ((row >= 0) & (row < 512))[:, None]
+    odd = (block_parity(row, bounds) == 1)[:, None]
 
     extra = jnp.concatenate([sources, jnp.zeros_like(sources[:, :1])], axis=1)
     extra = extra.reshape(2, 2, 2, NZ)
     below = jnp.concatenate([checkpoints[:, :, :6], extra], axis=2)
     edge = jnp.where(y == 0, below, checkpoints[:, :, 8:])
-
-    slabs = []
+    checkpoints, edge = lax.optimization_barrier((checkpoints, edge))
+    owns = []
     for k in range(2):
         main = lax.ppermute(checkpoints, AXES, routes(functools.partial(main_source, k)))
         side = lax.ppermute(edge, AXES, routes(functools.partial(edge_source, k)))
-        own = jnp.concatenate([main, side], axis=2)
-        slabs.append([own] + [lax.ppermute(own, AXES, along_y(d)) for d in (1, 2, 3)])
-
-    row = chunk * CHUNK - EDGE + jnp.arange(WIN)
-    inside = ((row >= 0) & (row < 512))[:, None]
-    parity = block_parity(row, bounds)
-    odd = (parity == 1)[:, None]
+        owns.append(jnp.concatenate([main, side], axis=2))
+
     pair = window(probes, chunk, 1)
-    mine = jnp.where(inside, jnp.where(odd, pair[1], pair[0]), 0.0)
-    blocks = [mine] + [lax.ppermute(mine, AXES, along_x(d)) for d in (1, 2, 3)]
-    coef = jnp.where(inside, window(coefficient, chunk, 0), 0.0)
-    recv = jnp.where(inside, window(receiver, chunk, 0), 0.0)
+    mine = reorder(jnp.where(inside, jnp.where(odd, pair[1], pair[0]), 0.0))
+    coef = reorder(jnp.where(inside, window(coefficient, chunk, 0), 0.0))
+    recv = reorder(jnp.where(inside, window(receiver, chunk, 0), 0.0))
     colours = jnp.broadcast_to(odd.astype(jnp.float32), (WIN, NZ))
     place = jnp.stack([y, 256 - chunk * CHUNK + EDGE]).astype(jnp.int32)
+    owns[0], mine, coef, recv, colours, place = lax.optimization_barrier(
+        (owns[0], mine, coef, recv, colours, place)
+    )
+
+    slabs = [[own] + [lax.ppermute(own, AXES, along_y(d)) for d in (1, 2, 3)] for own in owns]
+    blocks = [mine] + [lax.ppermute(mine, AXES, along_x(d)) for d in (1, 2, 3)]
 
     terms = apply(place, slabs[0], blocks, colours, coef, recv)
     terms = apply(place, slabs[1], blocks, colours, coef, recv, terms)
@@ -349,6 +356,7 @@
     for d in (1, 2, 3):
         total = total + lax.ppermute(terms[d], AXES, along_x(4 - d))
 
+    total = reorder(total, back=True)
     keep = odd[EDGE : EDGE + CHUNK]
     return jnp.stack(
         [

time: 117 us -> 86.4 us (0.74); the launches traced: 117 us -> 84.7 us
  Pallas kernels: 41.4 us -> 17.6 us
  starting transfers between devices: 46.6 us -> 36.5 us
  matrix products: 0.33 us -> 6.31 us
  waiting for transfers between devices: 18.6 us -> 14.7 us
  other arithmetic: 3.4 us -> 1.53 us
  local copies, waits for them, and re-layouts: 6.25 us -> 7.7 us
    pallas_call x2, Pallas kernels: 41.4 us -> 17.6 us  [apply(): pl.pallas_call(functools.partial(kernel, shots=shots, has_total=bool(tota...]
    ppermute x3, starting transfers between devices: 22 us -> 3.46 us  [on_device(): total = total + lax.ppermute(terms[d], AXES, along_x(4 - d))]
    ppermute x3, starting transfers between devices: 4.43 us -> 13.6 us  [on_device(): blocks = [mine] + [lax.ppermute(mine, AXES, along_x(d)) for d in (1, 2, 3)]]
    ppermute x2, waiting for transfers between devices: 7.14 us -> 0.01 us  [on_device(): side = lax.ppermute(edge, AXES, routes(functools.partial(edge_source, k)))]
    dot_general x0 -> x5, matrix products: none -> 5.29 us  [reorder(): lax.dot_general(array, match.astype(jnp.float32), (((array.ndim - 1,), (0...]
    ppermute x6, waiting for transfers between devices: 2.75 us -> 7.5 us  [on_device(): lax.ppermute(own, AXES, along_y(d))]
    ppermute x2, waiting for transfers between devices: 2.35 us -> 0.01 us  [on_device(): lax.ppermute(checkpoints, AXES, routes(functools.partial(main_source, k)))]
    unnamed x34 -> x33, local copies, waits for them, and re-layouts: 0.87 us -> 3.06 us
  transfers between devices with their start and end apart: 16 -> 16, of which waited for: 7 -> 7; matrix products, arithmetic and copies ran while one was open for 2% -> 10% of each run, Pallas kernels for 18% -> 10%
where the time goes in v2:
time: 86.4 us; the launch traced here: 84.7 us
  starting transfers between devices  36.5 us (42%)
  Pallas kernels  17.6 us (20%)
  waiting for transfers between devices  14.7 us (17%)
  local copies, waits for them, and re-layouts  7.7 us (9%)
  matrix products  6.31 us (7%)
  other arithmetic  1.53 us (2%)
    pallas_call x2, Pallas kernels, apply(): pl.pallas_call(functools.partial(kernel, shots=shots, has_total=bool(tota...  17.6 us
    ppermute x3, starting transfers between devices, on_device(): blocks = [mine] + [lax.ppermute(mine, AXES, along_x(d)) for d in (1, 2, 3)]  13.6 us
    ppermute x2, starting transfers between devices, on_device(): lax.ppermute(checkpoints, AXES, routes(functools.partial(main_source, k)))  10.3 us
    ppermute x6, waiting for transfers between devices, on_device(): lax.ppermute(own, AXES, along_y(d))  7.5 us
    ppermute x6, starting transfers between devices, on_device(): lax.ppermute(own, AXES, along_y(d))  6.56 us
    dot_general x5, matrix products, reorder(): lax.dot_general(array, match.astype(jnp.float32), (((array.ndim - 1,), (0...  5.29 us
    ppermute x3, waiting for transfers between devices, on_device(): total = total + lax.ppermute(terms[d], AXES, along_x(4 - d))  5.16 us
    ppermute x3, starting transfers between devices, on_device(): total = total + lax.ppermute(terms[d], AXES, along_x(4 - d))  3.46 us
  transfers between devices with their start and end apart: 16, of which 7 were waited for; matrix products, arithmetic and copies ran while one was open for 10% of the time, Pallas kernels for 10%

profile of v2, /device:TPU:1, one launch (start us, length us, event | category | flops | bytes accessed | tf_op | source)
XLA Modules:
  0.0 84.7 jit_solution(10738579461141245658)
XLA Ops:
  0.0 0.9 %copy-done = f32[2,2,16,512]{3,2,1,0:T(8,128)S(1)} copy-done((f32[2,2,16,512]{3,2,1,0:T(8,128)S(1)}, f32[2,2,16,512]{3,2,1,0:T(8,128)}, u32[]{:S(2)}) %copy-start) | copy-done | bytes 131096
  0.9 0.6 convolution_bitcast_fusion
  1.5 0.7 convert_element_type.21
  2.2 1.0 %fusion.12 = f32[2,3,512]{2,1,0:T(4,128)S(1)} fusion(s32[256]{0:T(256)S(1)} %fusion.53, f32[3,256]{1,0:T(4,128)} %param.14, f32[2,256]{1,0:T(2,128)S(1)} %convert_element_type.21), kind=kOutput, calls=%fused_computation.14 | convolution fusion | flops 9569792 | bytes 18432 | tf_op jit(solution)/shard_map/stk,kz->stz/dot_general | solution.py:299
  3.3 10.2 %collective-permute-start = (f32[2,2,16,512]{3,2,1,0:T(8,128)S(1)}, f32[2,2,16,512]{3,2,1,0:T(8,128)S(1)}, u32[]{:S(2)}, u32[]{:S(2)}) collective-permute-start(f32[2,2,16,512]{3,2,1,0:T(8,128)S(1)} %convolution_bitcast_fusion), channel_id=1, source_target_pairs={{0,0},{4,32},{8,64},{12,96},{16,128},{20,160},{24,192},{28,224},{1... | collective-permute-start | bytes 393224 | tf_op jit(solution)/shard_map/ppermute | solution.py:336
  13.5 0.1 collective-permute-start.2
  13.6 1.3 %collective-permute-start.1 = (f32[2,2,8,512]{3,2,1,0:T(8,128)S(1)}, f32[2,2,8,512]{3,2,1,0:T(8,128)S(1)}, u32[]{:S(2)}, u32[]{:S(2)}) collective-permute-start(f32[2,2,8,512]{3,2,1,0:T(8,128)S(1)} %slice_select_fusion), channel_id=1, source_target_pairs={{4,0},{8,32},{12,64},{16,96},{20,128},{24,160},{28,192},{3,35},{7,... | collective-permute-start | bytes 196616 | tf_op jit(solution)/shard_map/ppermute | solution.py:337
  14.9 1.0 %constant_dynamic-slice_fusion.7 = f32[2,64,512]{2,1,0:T(8,128)S(1)} fusion(f32[2,512,512]{2,1,0:T(8,128)} %param.8, s32[]{:T(128)S(6)} %select_n.137), kind=kLoop, calls=%fused_computation.71 | loop fusion | bytes 524292 | tf_op jit(solution)/shard_map/dynamic_slice | solution.py:310
  15.9 0.9 %constant_dynamic-slice_fusion.8 = (f32[2,8,512]{2,1,0:T(8,128)S(1)}, f32[2,8,512]{2,1,0:T(8,128)S(1)}) fusion(f32[2,512,512]{2,1,0:T(8,128)} %param.8, s32[]{:T(128)S(6)} %max.2, s32[]{:T(128)S(6)} %select_n.138), kind=kLoop, calls=%fused_computation.72 | loop fusion | bytes 131080 | tf_op jit(solution)/shard_map/dynamic_slice | solution.py:309
  16.8 0.8 constant_dynamic-slice_fusion.2
  17.6 1.0 %constant_dynamic-slice_fusion.1 = (f32[64,512]{1,0:T(8,128)S(1)}, f32[64,512]{1,0:T(8,128)S(1)}) fusion(f32[512,512]{1,0:T(8,128)} %param.11, s32[]{:T(128)S(6)} %select_n.137, f32[512,512]{1,0:T(8,128)} %param.10), kind=kLoop, calls=%fused_computation.65 | loop fusion | bytes 524292 | tf_op jit(solution)/shard_map/dynamic_slice | solution.py:310
  18.6 0.1 slice.25
  18.7 0.1 convert_reduce_fusion
  18.9 0.6 fusion.3.refs_4_
  19.4 1.3 %fusion.1.refs_10_ = f32[80,512]{1,0:T(8,128)} fusion(s32[512]{0:T(512)S(1)} %fusion.47, f32[8,512]{1,0:T(8,128)S(1)} %get-tuple-element.42, f32[64,512]{1,0:T(8,128)S(1)} %get-tuple-element.49, f32[8,512]{1,0:T(8,128)S(1)} %get-tuple-element.41, pred[80]{0:T(512)(128)(4,1)S(1)} %compare_and_fusion), kind=kOutput, calls=%fused_computation.3 | convolution fusion | flops 252043264 | bytes 329808 | tf_op jit(solution)/shard_map/dot_general | solution.py:286
  20.7 1.2 %fusion.2.refs_9_ = f32[80,512]{1,0:T(8,128)} fusion(s32[512]{0:T(512)S(1)} %fusion.47, f32[8,512]{1,0:T(8,128)S(1)} %get-tuple-element.47, f32[64,512]{1,0:T(8,128)S(1)} %get-tuple-element.50, f32[8,512]{1,0:T(8,128)S(1)} %get-tuple-element.48, pred[80]{0:T(512)(128)(4,1)S(1)} %compare_and_fusion), kind=kOutput, calls=%fused_computation.4 | convolution fusion | flops 252043264 | bytes 329808 | tf_op jit(solution)/shard_map/dot_general | solution.py:286
  21.9 0.6 pad_add_fusion.place
  22.6 0.7 broadcast_in_dim.76.refs_8_
  23.4 8.1 %collective-permute-start.7 = (f32[80,512]{1,0:T(8,128)S(1)}, f32[80,512]{1,0:T(8,128)S(1)}, u32[]{:S(2)}, u32[]{:S(2)}) collective-permute-start(f32[80,512]{1,0:T(8,128)S(1)} %fusion.3.refs_4_), channel_id=1, source_target_pairs={{8,0},{40,32},{72,64},{104,96},{136,128},{168,160},{200,192},{232,... | collective-permute-start | bytes 491528 | tf_op jit(solution)/shard_map/ppermute | solution.py:351
  31.5 1.3 %collective-permute-start.3 = (f32[2,2,8,512]{3,2,1,0:T(8,128)S(1)}, f32[2,2,8,512]{3,2,1,0:T(8,128)S(1)}, u32[]{:S(2)}, u32[]{:S(2)}) collective-permute-start(f32[2,2,8,512]{3,2,1,0:T(8,128)S(1)} %slice_select_fusion), channel_id=1, source_target_pairs={{36,0},{40,32},{44,64},{48,96},{52,128},{56,160},{60,192},{35,35},... | collective-permute-start | bytes 196616 | tf_op jit(solution)/shard_map/ppermute | solution.py:337
  32.8 4.9 %collective-permute-start.8 = (f32[80,512]{1,0:T(8,128)S(1)}, f32[80,512]{1,0:T(8,128)S(1)}, u32[]{:S(2)}, u32[]{:S(2)}) collective-permute-start(f32[80,512]{1,0:T(8,128)S(1)} %fusion.3.refs_4_), channel_id=1, source_target_pairs={{16,0},{48,32},{80,64},{112,96},{144,128},{176,160},{208,192},{240... | collective-permute-start | bytes 491528 | tf_op jit(solution)/shard_map/ppermute | solution.py:351
  37.6 0.6 collective-permute-start.9
  38.2 0.0 collective-permute-done.2
  38.2 2.9 %collective-permute-start.10 = (f32[2,2,24,512]{3,2,1,0:T(8,128)S(1)}, f32[2,2,24,512]{3,2,1,0:T(8,128)S(1)}, u32[]{:S(2)}, u32[]{:S(2)}) collective-permute-start(f32[2,2,24,512]{3,2,1,0:T(8,128)S(1)} %pad_maximum_fusion.2.refs_0_), channel_id=1, source_target_pairs={{1,0},{33,32},{65,64},{97,96},{129,128},{161,160},{193,192},{225,2... | collective-permute-start | bytes 589832 | tf_op jit(solution)/shard_map/ppermute | solution.py:350
  41.1 0.0 collective-permute-done.3
  41.2 0.1 collective-permute-start.11
  41.3 0.6 collective-permute-start.12
  41.8 0.0 copy-start.13
  41.9 0.4 collective-permute-done.8.refs_6_
  42.2 1.9 %collective-permute-start.4 = (f32[2,2,24,512]{3,2,1,0:T(8,128)S(1)}, f32[2,2,24,512]{3,2,1,0:T(8,128)S(1)}, u32[]{:S(2)}, u32[]{:S(2)}) collective-permute-start(f32[2,2,24,512]{3,2,1,0:T(8,128)S(1)} %constant_dynamic-update-slice_fusion.refs_0_), channel_id=1, source_target_pairs={{1,0},{33,32},{65,64},{97,96},{129,128},{161,160},{193,192},{225,2... | collective-permute-start | bytes 589832 | tf_op jit(solution)/shard_map/ppermute | solution.py:350
  44.2 1.7 %collective-permute-done.9.refs_7_ = f32[80,512]{1,0:T(8,128)S(1)} collective-permute-done((f32[80,512]{1,0:T(8,128)S(1)}, f32[80,512]{1,0:T(8,128)S(1)}, u32[]{:S(2)}, u32[]{:S(2)}) %collective-permute-start.9) | collective-permute-done | bytes 163872 | tf_op jit(solution)/shard_map/ppermute | solution.py:351
  45.9 1.1 %collective-permute-start.6 = (f32[2,2,24,512]{3,2,1,0:T(8,128)S(1)}, f32[2,2,24,512]{3,2,1,0:T(8,128)S(1)}, u32[]{:S(2)}, u32[]{:S(2)}) collective-permute-start(f32[2,2,24,512]{3,2,1,0:T(8,128)S(1)} %constant_dynamic-update-slice_fusion.refs_0_), channel_id=1, source_target_pairs={{3,0},{35,32},{67,64},{99,96},{131,128},{163,160},{195,192},{227,2... | collective-permute-start | bytes 589832 | tf_op jit(solution)/shard_map/ppermute | solution.py:350
  47.0 1.2 %collective-permute-done.11.refs_2_ = f32[2,2,24,512]{3,2,1,0:T(8,128)S(1)} collective-permute-done((f32[2,2,24,512]{3,2,1,0:T(8,128)S(1)}, f32[2,2,24,512]{3,2,1,0:T(8,128)S(1)}, u32[]{:S(2)}, u32[]{:S(2)}) %collective-permute-start.11) | collective-permute-done | bytes 196640 | tf_op jit(solution)/shard_map/ppermute | solution.py:350
  48.1 6.3 %collective-permute-done.12.refs_3_ = f32[2,2,24,512]{3,2,1,0:T(8,128)S(1)} collective-permute-done((f32[2,2,24,512]{3,2,1,0:T(8,128)S(1)}, f32[2,2,24,512]{3,2,1,0:T(8,128)S(1)}, u32[]{:S(2)}, u32[]{:S(2)}) %collective-permute-start.12) | collective-permute-done | bytes 196640 | tf_op jit(solution)/shard_map/ppermute | solution.py:350
  54.5 0.7 copy-done.9
  55.2 8.7 %hessian_rows.2 = (f32[64,512]{1,0:T(8,128)}, f32[64,512]{1,0:T(8,128)}, f32[64,512]{1,0:T(8,128)}, f32[64,512]{1,0:T(8,128)}) custom-call(s32[2]{0:T(128)} %pad_add_fusion.place, f32[2,2,24,512]{3,2,1,0:T(8,128)} %copy-done.1, f32[2,2,24,512]{3,2,1,0:T(8,128)} %copy-done.7, f32[2,2,24,512]{3,2,1,0:T(8,128)} %copy-done.8, f32[2,2,24,512]{3,2,1,0:T(8,128)} %copy-done.9, ...), custom_call_target="tpu_custom_call" | custom-call | flops 55050240 | bytes 4194304 | tf_op jit(solution)/shard_map/hessian_rows/pallas_call | solution.py:218
  63.9 0.6 copy-done.10
  64.6 0.1 copy-done.11
  64.6 0.1 copy-done.12
  64.7 8.9 %hessian_rows.3 = (f32[64,512]{1,0:T(8,128)}, f32[64,512]{1,0:T(8,128)}, f32[64,512]{1,0:T(8,128)}, f32[64,512]{1,0:T(8,128)}) custom-call(s32[2]{0:T(128)} %pad_add_fusion.place, f32[2,2,24,512]{3,2,1,0:T(8,128)} %copy-done.6, f32[2,2,24,512]{3,2,1,0:T(8,128)} %copy-done.10, f32[2,2,24,512]{3,2,1,0:T(8,128)} %copy-done.11, f32[2,2,24,512]{3,2,1,0:T(8,128)} %copy-done.12, ...), custom_call_target="tpu_custom_call" | custom-call | flops 55050240 | bytes 4194304 | tf_op jit(solution)/shard_map/hessian_rows/pallas_call | solution.py:218
  73.6 3.5 %collective-permute-start.14 = (f32[64,512]{1,0:T(8,128)}, f32[64,512]{1,0:T(8,128)S(1)}, u32[]{:S(2)}, u32[]{:S(2)}) collective-permute-start(f32[64,512]{1,0:T(8,128)} %get-tuple-element.35), channel_id=1, source_target_pairs={{16,0},{48,32},{80,64},{112,96},{144,128},{176,160},{208,192},{240... | collective-permute-start | bytes 393224 | tf_op jit(solution)/shard_map/ppermute | solution.py:357
  77.1 0.1 slice.26
  77.2 1.7 %collective-permute-done.13 = f32[64,512]{1,0:T(8,128)S(1)} collective-permute-done((f32[64,512]{1,0:T(8,128)}, f32[64,512]{1,0:T(8,128)S(1)}, u32[]{:S(2)}, u32[]{:S(2)}) %collective-permute-start.13) | collective-permute-done | bytes 131104 | tf_op jit(solution)/shard_map/ppermute | solution.py:357
  78.9 2.7 %collective-permute-done.14 = f32[64,512]{1,0:T(8,128)S(1)} collective-permute-done((f32[64,512]{1,0:T(8,128)}, f32[64,512]{1,0:T(8,128)S(1)}, u32[]{:S(2)}, u32[]{:S(2)}) %collective-permute-start.14) | collective-permute-done | bytes 131104 | tf_op jit(solution)/shard_map/ppermute | solution.py:357
  81.5 0.8 collective-permute-done.15
  82.3 1.6 %fusion.29 = (f32[2,64,512]{2,1,0:T(8,128)S(1)}, f32[2,64,512]{2,1,0:T(8,128)S(1)}) fusion(f32[2,64,512]{2,1,0:T(8,128)S(1)} %copy-done.13, pred[64]{0:T(512)(128)(4,1)S(1)} %slice.26, s32[512]{0:T(512)S(1)} %fusion.47, f32[64,512]{1,0:T(8,128)S(1)} %collective-permute-done.15, ...), kind=kOutput, output_to_operand_aliasing={{0}: (7, {}), {1}: (7, {})}, calls=%fused_computation.38 | convolution fusion | flops 201818112 | bytes 1051136 | tf_op jit(solution)/shard_map/dot_general | solution.py:286
  84.0 0.0 copy-start.14
  84.0 0.7 copy-done.14
  (48 shorter events, 0.2 us)
Async XLA Ops:
  0.0 0.9 %copy-start = (f32[2,2,16,512]{3,2,1,0:T(8,128)S(1)}, f32[2,2,16,512]{3,2,1,0:T(8,128)}, u32[]{:S(2)}) copy-start(f32[2,2,16,512]{3,2,1,0:T(8,128)} %param.12) | copy-start | bytes 393220
  0.0 18.6 %copy-start.15 = (s32[65]{0:T(128)S(1)}, s32[65]{0:T(128)}, u32[]{:S(2)}) copy-start(s32[65]{0:T(128)} %param.15) | copy-start | bytes 784
  3.3 19.3 %collective-permute-start = (f32[2,2,16,512]{3,2,1,0:T(8,128)S(1)}, f32[2,2,16,512]{3,2,1,0:T(8,128)S(1)}, u32[]{:S(2)}, u32[]{:S(2)}) collective-permute-start(f32[2,2,16,512]{3,2,1,0:T(8,128)S(1)} %convolution_bitcast_fusion), channel_id=1, source_target_pairs={{0,0},{4,32},{8,64},{12,96},{16,128},{20,160},{24,192},{28,224},{1... | collective-permute-start | bytes 393224 | tf_op jit(solution)/shard_map/ppermute | solution.py:336
  13.5 24.8 %collective-permute-start.2 = (f32[2,2,16,512]{3,2,1,0:T(8,128)S(1)}, f32[2,2,16,512]{3,2,1,0:T(8,128)S(1)}, u32[]{:S(2)}, u32[]{:S(2)}) collective-permute-start(f32[2,2,16,512]{3,2,1,0:T(8,128)S(1)} %convolution_bitcast_fusion), channel_id=1, source_target_pairs={{32,0},{36,32},{40,64},{44,96},{48,128},{52,160},{56,192},{60,224}... | collective-permute-start | bytes 393224 | tf_op jit(solution)/shard_map/ppermute | solution.py:336
  13.6 9.0 %collective-permute-start.1 = (f32[2,2,8,512]{3,2,1,0:T(8,128)S(1)}, f32[2,2,8,512]{3,2,1,0:T(8,128)S(1)}, u32[]{:S(2)}, u32[]{:S(2)}) collective-permute-start(f32[2,2,8,512]{3,2,1,0:T(8,128)S(1)} %slice_select_fusion), channel_id=1, source_target_pairs={{4,0},{8,32},{12,64},{16,96},{20,128},{24,160},{28,192},{3,35},{7,... | collective-permute-start | bytes 196616 | tf_op jit(solution)/shard_map/ppermute | solution.py:337
  19.4 35.0 %copy-start.2 = (f32[80,512]{1,0:T(8,128)}, f32[80,512]{1,0:T(8,128)S(1)}, u32[]{:S(2)}) copy-start(f32[80,512]{1,0:T(8,128)S(1)} %fusion.3.refs_4_) | copy-start | bytes 491524
  22.6 31.8 %copy-start.1 = (f32[2,2,24,512]{3,2,1,0:T(8,128)}, f32[2,2,24,512]{3,2,1,0:T(8,128)S(1)}, u32[]{:S(2)}) copy-start(f32[2,2,24,512]{3,2,1,0:T(8,128)S(1)} %pad_maximum_fusion.2.refs_0_) | copy-start | bytes 589828
  23.4 17.9 %collective-permute-start.7 = (f32[80,512]{1,0:T(8,128)S(1)}, f32[80,512]{1,0:T(8,128)S(1)}, u32[]{:S(2)}, u32[]{:S(2)}) collective-permute-start(f32[80,512]{1,0:T(8,128)S(1)} %fusion.3.refs_4_), channel_id=1, source_target_pairs={{8,0},{40,32},{72,64},{104,96},{136,128},{168,160},{200,192},{232,... | collective-permute-start | bytes 491528 | tf_op jit(solution)/shard_map/ppermute | solution.py:351
  31.5 9.7 %collective-permute-start.3 = (f32[2,2,8,512]{3,2,1,0:T(8,128)S(1)}, f32[2,2,8,512]{3,2,1,0:T(8,128)S(1)}, u32[]{:S(2)}, u32[]{:S(2)}) collective-permute-start(f32[2,2,8,512]{3,2,1,0:T(8,128)S(1)} %slice_select_fusion), channel_id=1, source_target_pairs={{36,0},{40,32},{44,64},{48,96},{52,128},{56,160},{60,192},{35,35},... | collective-permute-start | bytes 196616 | tf_op jit(solution)/shard_map/ppermute | solution.py:337
  32.8 9.5 %collective-permute-start.8 = (f32[80,512]{1,0:T(8,128)S(1)}, f32[80,512]{1,0:T(8,128)S(1)}, u32[]{:S(2)}, u32[]{:S(2)}) collective-permute-start(f32[80,512]{1,0:T(8,128)S(1)} %fusion.3.refs_4_), channel_id=1, source_target_pairs={{16,0},{48,32},{80,64},{112,96},{144,128},{176,160},{208,192},{240... | collective-permute-start | bytes 491528 | tf_op jit(solution)/shard_map/ppermute | solution.py:351
  37.6 8.2 %collective-permute-start.9 = (f32[80,512]{1,0:T(8,128)S(1)}, f32[80,512]{1,0:T(8,128)S(1)}, u32[]{:S(2)}, u32[]{:S(2)}) collective-permute-start(f32[80,512]{1,0:T(8,128)S(1)} %fusion.3.refs_4_), channel_id=1, source_target_pairs={{24,0},{56,32},{88,64},{120,96},{152,128},{184,160},{216,192},{248... | collective-permute-start | bytes 491528 | tf_op jit(solution)/shard_map/ppermute | solution.py:351
  38.2 7.6 %collective-permute-start.10 = (f32[2,2,24,512]{3,2,1,0:T(8,128)S(1)}, f32[2,2,24,512]{3,2,1,0:T(8,128)S(1)}, u32[]{:S(2)}, u32[]{:S(2)}) collective-permute-start(f32[2,2,24,512]{3,2,1,0:T(8,128)S(1)} %pad_maximum_fusion.2.refs_0_), channel_id=1, source_target_pairs={{1,0},{33,32},{65,64},{97,96},{129,128},{161,160},{193,192},{225,2... | collective-permute-start | bytes 589832 | tf_op jit(solution)/shard_map/ppermute | solution.py:350
  41.2 7.0 %collective-permute-start.11 = (f32[2,2,24,512]{3,2,1,0:T(8,128)S(1)}, f32[2,2,24,512]{3,2,1,0:T(8,128)S(1)}, u32[]{:S(2)}, u32[]{:S(2)}) collective-permute-start(f32[2,2,24,512]{3,2,1,0:T(8,128)S(1)} %pad_maximum_fusion.2.refs_0_), channel_id=1, source_target_pairs={{2,0},{34,32},{66,64},{98,96},{130,128},{162,160},{194,192},{226,2... | collective-permute-start | bytes 589832 | tf_op jit(solution)/shard_map/ppermute | solution.py:350
  41.3 13.2 %copy-start.3 = (f32[80,512]{1,0:T(8,128)}, f32[80,512]{1,0:T(8,128)S(1)}, u32[]{:S(2)}) copy-start(f32[80,512]{1,0:T(8,128)S(1)} %collective-permute-done.7.refs_5_) | copy-start | bytes 491524
  41.3 13.2 %collective-permute-start.12 = (f32[2,2,24,512]{3,2,1,0:T(8,128)S(1)}, f32[2,2,24,512]{3,2,1,0:T(8,128)S(1)}, u32[]{:S(2)}, u32[]{:S(2)}) collective-permute-start(f32[2,2,24,512]{3,2,1,0:T(8,128)S(1)} %pad_maximum_fusion.2.refs_0_), channel_id=1, source_target_pairs={{3,0},{35,32},{67,64},{99,96},{131,128},{163,160},{195,192},{227,2... | collective-permute-start | bytes 589832 | tf_op jit(solution)/shard_map/ppermute | solution.py:350
  41.8 22.1 %copy-start.6 = (f32[2,2,24,512]{3,2,1,0:T(8,128)}, f32[2,2,24,512]{3,2,1,0:T(8,128)S(1)}, u32[]{:S(2)}) copy-start(f32[2,2,24,512]{3,2,1,0:T(8,128)S(1)} %constant_dynamic-update-slice_fusion.refs_0_) | copy-start | bytes 589828
  41.8 40.5 %copy-start.13 = (f32[2,64,512]{2,1,0:T(8,128)S(1)}, f32[2,64,512]{2,1,0:T(8,128)}, u32[]{:S(2)}) copy-start(f32[2,64,512]{2,1,0:T(8,128)} %param.9) | copy-start | bytes 786436
  42.2 12.2 %copy-start.4 = (f32[80,512]{1,0:T(8,128)}, f32[80,512]{1,0:T(8,128)S(1)}, u32[]{:S(2)}) copy-start(f32[80,512]{1,0:T(8,128)S(1)} %collective-permute-done.8.refs_6_) | copy-start | bytes 491524
  42.2 21.6 %collective-permute-start.4 = (f32[2,2,24,512]{3,2,1,0:T(8,128)S(1)}, f32[2,2,24,512]{3,2,1,0:T(8,128)S(1)}, u32[]{:S(2)}, u32[]{:S(2)}) collective-permute-start(f32[2,2,24,512]{3,2,1,0:T(8,128)S(1)} %constant_dynamic-update-slice_fusion.refs_0_), channel_id=1, source_target_pairs={{1,0},{33,32},{65,64},{97,96},{129,128},{161,160},{193,192},{225,2... | collective-permute-start | bytes 589832 | tf_op jit(solution)/shard_map/ppermute | solution.py:350
  45.8 8.7 %copy-start.5 = (f32[80,512]{1,0:T(8,128)}, f32[80,512]{1,0:T(8,128)S(1)}, u32[]{:S(2)}) copy-start(f32[80,512]{1,0:T(8,128)S(1)} %collective-permute-done.9.refs_7_) | copy-start | bytes 491524
  45.8 18.1 %collective-permute-start.5 = (f32[2,2,24,512]{3,2,1,0:T(8,128)S(1)}, f32[2,2,24,512]{3,2,1,0:T(8,128)S(1)}, u32[]{:S(2)}, u32[]{:S(2)}) collective-permute-start(f32[2,2,24,512]{3,2,1,0:T(8,128)S(1)} %constant_dynamic-update-slice_fusion.refs_0_), channel_id=1, source_target_pairs={{2,0},{34,32},{66,64},{98,96},{130,128},{162,160},{194,192},{226,2... | collective-permute-start | bytes 589832 | tf_op jit(solution)/shard_map/ppermute | solution.py:350
  45.8 8.7 %copy-start.7 = (f32[2,2,24,512]{3,2,1,0:T(8,128)}, f32[2,2,24,512]{3,2,1,0:T(8,128)S(1)}, u32[]{:S(2)}) copy-start(f32[2,2,24,512]{3,2,1,0:T(8,128)S(1)} %collective-permute-done.10.refs_1_) | copy-start | bytes 589828
  45.9 18.1 %collective-permute-start.6 = (f32[2,2,24,512]{3,2,1,0:T(8,128)S(1)}, f32[2,2,24,512]{3,2,1,0:T(8,128)S(1)}, u32[]{:S(2)}, u32[]{:S(2)}) collective-permute-start(f32[2,2,24,512]{3,2,1,0:T(8,128)S(1)} %constant_dynamic-update-slice_fusion.refs_0_), channel_id=1, source_target_pairs={{3,0},{35,32},{67,64},{99,96},{131,128},{163,160},{195,192},{227,2... | collective-permute-start | bytes 589832 | tf_op jit(solution)/shard_map/ppermute | solution.py:350
  48.1 6.4 %copy-start.8 = (f32[2,2,24,512]{3,2,1,0:T(8,128)}, f32[2,2,24,512]{3,2,1,0:T(8,128)S(1)}, u32[]{:S(2)}) copy-start(f32[2,2,24,512]{3,2,1,0:T(8,128)S(1)} %collective-permute-done.11.refs_2_) | copy-start | bytes 589828
  54.5 0.7 copy-start.9
  63.9 0.7 copy-start.10
  63.9 0.7 copy-start.11
  63.9 0.8 copy-start.12
  73.6 5.2 %collective-permute-start.13 = (f32[64,512]{1,0:T(8,128)}, f32[64,512]{1,0:T(8,128)S(1)}, u32[]{:S(2)}, u32[]{:S(2)}) collective-permute-start(f32[64,512]{1,0:T(8,128)} %get-tuple-element.34), channel_id=1, source_target_pairs={{24,0},{56,32},{88,64},{120,96},{152,128},{184,160},{216,192},{248... | collective-permute-start | bytes 393224 | tf_op jit(solution)/shard_map/ppermute | solution.py:357
  73.6 7.9 %collective-permute-start.14 = (f32[64,512]{1,0:T(8,128)}, f32[64,512]{1,0:T(8,128)S(1)}, u32[]{:S(2)}, u32[]{:S(2)}) collective-permute-start(f32[64,512]{1,0:T(8,128)} %get-tuple-element.35), channel_id=1, source_target_pairs={{16,0},{48,32},{80,64},{112,96},{144,128},{176,160},{208,192},{240... | collective-permute-start | bytes 393224 | tf_op jit(solution)/shard_map/ppermute | solution.py:357
  77.1 5.2 %collective-permute-start.15 = (f32[64,512]{1,0:T(8,128)}, f32[64,512]{1,0:T(8,128)S(1)}, u32[]{:S(2)}, u32[]{:S(2)}) collective-permute-start(f32[64,512]{1,0:T(8,128)} %get-tuple-element.36), channel_id=1, source_target_pairs={{8,0},{40,32},{72,64},{104,96},{136,128},{168,160},{200,192},{232,... | collective-permute-start | bytes 393224 | tf_op jit(solution)/shard_map/ppermute | solution.py:357
  84.0 0.7 copy-start.14

commit v3 on v2

--- a/solution.py
+++ b/solution.py
@@ -26,7 +26,9 @@
     return [left + tiles[1], tiles[0] + tiles[2], tiles[1] + tiles[3], tiles[2] + right]
 
 
-def kernel(place, *refs, shots, has_total):
+def kernel(*refs, shots, has_total):
+    my_y = lax.rem(lax.axis_index("probe"), 4)
+    source_row = NZ // 2 + EDGE - CHUNK * lax.axis_index("shot")
     slabs = refs[0:4]
     blocks = refs[4:8]
     parity_ref, coef_ref, recv_ref = refs[8:11]
@@ -43,7 +45,7 @@
     last = lane == LANES - 1
 
     for k in range(4):
-        y = lax.rem(place[0] + k, 4)
+        y = lax.rem(my_y + k, 4)
         for i in range(shots):
             for lev in range(2):
                 base = pl.multiple_of(EDGE + 16 * y, 8)
@@ -79,7 +81,7 @@
 
     row = lax.broadcasted_iota(jnp.int32, (WIN, LANES), 0)
     column = lax.broadcasted_iota(jnp.int32, (WIN, LANES), 1)
-    at_source = row == place[1]
+    at_source = row == source_row
     for i in range(shots):
         for t in range(3):
             now = split(u_ref[i, t + 1])
@@ -210,7 +212,7 @@
             outs[q][:, here] = result
 
 
-def apply(place, slabs, blocks, parity, coef, recv, totals=()):
+def apply(slabs, blocks, parity, coef, recv, totals=()):
     shots = slabs[0].shape[0]
     vm = pl.BlockSpec(memory_space=pltpu.VMEM)
     args = [*slabs, *blocks, parity, coef, recv, *totals]
@@ -218,7 +220,7 @@
     return pl.pallas_call(
         functools.partial(kernel, shots=shots, has_total=bool(totals)),
         out_shape=[jax.ShapeDtypeStruct((CHUNK, NZ), jnp.float32)] * 4,
-        in_specs=[pl.BlockSpec(memory_space=pltpu.SMEM)] + [vm] * len(args),
+        in_specs=[vm] * len(args),
         out_specs=[vm] * 4,
         scratch_shapes=[
             pltpu.VMEM((shots, 7, WIN, NZ), jnp.float32),
@@ -233,7 +235,130 @@
             flops=shots * 8 * 8 * 70 * 512 * 12, bytes_accessed=4 << 20, transcendentals=0
         ),
         name="hessian_rows",
-    )(place, *args)
+    )(*args)
+
+
+def match(sources, column_of):
+    shape = (sources, NZ)
+    column = column_of(lax.broadcasted_iota(jnp.int32, shape, 0))
+    place = lax.broadcasted_iota(jnp.int32, shape, 1)
+    kept = TILES * (place & (LANES - 1)) + place // LANES
+    return jnp.where(column == kept, 1.0, 0.0).astype(jnp.float32)
+
+
+def exact_dot(a, b, transposed=False):
+    dims = (((1,), (1 if transposed else 0,)), ((), ()))
+    return lax.dot_general(
+        a, b, dims, precision=lax.Precision.HIGHEST, preferred_element_type=jnp.float32
+    )
+
+
+def emit_kernel(levels_ref, enc_ref, wav_ref, main_ref, edge_ref):
+    y = lax.rem(lax.axis_index("probe"), 4)
+    moved = exact_dot(levels_ref[...].reshape(64, NZ), match(NZ, lambda c: c))
+    main_ref[...] = moved.reshape(2, 2, 16, NZ)
+    signs = enc_ref[...].astype(jnp.float32)
+    rows = [signs[i : i + 1] * wav_ref[t : t + 1, :] for i in range(2) for t in range(3)]
+    rows += [jnp.zeros_like(rows[0])] * 2
+    amps = exact_dot(jnp.concatenate(rows, axis=0), match(NSHOT, lambda k: 2 * k + 1))
+    lowest = y == 0
+    for i in range(2):
+        for lev in range(2):
+            base = 16 * (2 * i + lev)
+            edge_ref[i, lev] = jnp.where(lowest, moved[base : base + 8], moved[base + 8 : base + 16])
+
+    @pl.when(lowest)
+    def _():
+        for i in range(2):
+            for t in range(3):
+                row = 6 + t % 2
+                edge_ref[i, t // 2, row : row + 1, :] = amps[3 * i + t : 3 * i + t + 1]
+
+
+def emit(levels, encodings, wavelet):
+    vm = pl.BlockSpec(memory_space=pltpu.VMEM)
+    return pl.pallas_call(
+        emit_kernel,
+        out_shape=[
+            jax.ShapeDtypeStruct((2, 2, 16, NZ), jnp.float32),
+            jax.ShapeDtypeStruct((2, 2, 8, NZ), jnp.float32),
+        ],
+        in_specs=[vm] * 3,
+        out_specs=[vm] * 2,
+        name="own_rows",
+    )(levels, encodings, wavelet)
+
+
+def prepare_kernel(bounds_ref, probes, coefficient, receiver, *refs):
+    mine_ref, coef_ref, recv_ref, colour_ref, pair, coef, recv, sem = refs
+    chunk = lax.axis_index("shot")
+    first = pl.multiple_of(chunk * CHUNK, 8)
+    above = pl.multiple_of(jnp.maximum(first - EDGE, 0), 8)
+    below = pl.multiple_of(jnp.minimum(first + CHUNK, NZ - EDGE), 8)
+    copies = []
+    for start, at, size in ((above, 0, EDGE), (first, EDGE, CHUNK), (below, EDGE + CHUNK, EDGE)):
+        rows, spot = pl.ds(start, size), pl.ds(at, size)
+        for source, target in (
+            (probes.at[:, rows, :], pair.at[:, spot, :]),
+            (coefficient.at[rows, :], coef.at[spot, :]),
+            (receiver.at[rows, :], recv.at[spot, :]),
+        ):
+            copy = pltpu.make_async_copy(source, target, sem.at[len(copies)])
+            copy.start()
+            copies.append(copy)
+    order = match(NZ, lambda c: c)
+    row = chunk * CHUNK - EDGE + lax.broadcasted_iota(jnp.int32, (WIN, 65), 0)
+    lane = lax.broadcasted_iota(jnp.int32, (WIN, 65), 1)
+    counted = (row >= bounds_ref[...]) & (lane >= 1) & (lane <= 63)
+    block = jnp.sum(jnp.where(counted, 1.0, 0.0), axis=1, keepdims=True)
+    odd = block - 2.0 * jnp.floor(0.5 * block)
+    odd = jnp.broadcast_to(odd, (WIN, NZ))
+    colour_ref[...] = odd
+    row = chunk * CHUNK - EDGE + lax.broadcasted_iota(jnp.int32, (WIN, NZ), 0)
+    inside = (row >= 0) & (row < NZ)
+    for copy in copies:
+        copy.wait()
+    mine = jnp.where(odd > 0.5, pair[1], pair[0])
+    for value, out in ((mine, mine_ref), (coef[...], coef_ref), (recv[...], recv_ref)):
+        out[...] = exact_dot(jnp.where(inside, value, 0.0), order)
+
+
+def prepare(bounds, probes, coefficient, receiver):
+    vm = pl.BlockSpec(memory_space=pltpu.VMEM)
+    hbm = pl.BlockSpec(memory_space=pl.ANY)
+    field = pltpu.VMEM((WIN, NZ), jnp.float32)
+    return pl.pallas_call(
+        prepare_kernel,
+        out_shape=[jax.ShapeDtypeStruct((WIN, NZ), jnp.float32)] * 4,
+        in_specs=[vm, hbm, hbm, hbm],
+        out_specs=[vm] * 4,
+        scratch_shapes=[
+            pltpu.VMEM((2, WIN, NZ), jnp.float32),
+            field,
+            field,
+            pltpu.SemaphoreType.DMA((9,)),
+        ],
+        cost_estimate=pl.CostEstimate(flops=0, bytes_accessed=12 << 20, transcendentals=0),
+        name="own_windows",
+    )(bounds, probes, coefficient, receiver)
+
+
+def finish_kernel(a, b, c, d, colour, coarse, out):
+    total = exact_dot(a[...] + b[...] + c[...] + d[...], match(NZ, lambda c: c), transposed=True)
+    odd = colour[EDGE : EDGE + CHUNK, :] > 0.5
+    out[0] = jnp.where(odd, total - coarse[0], 0.0)
+    out[1] = jnp.where(odd, 0.0, total - coarse[1])
+
+
+def finish(terms, colour, coarse):
+    vm = pl.BlockSpec(memory_space=pltpu.VMEM)
+    return pl.pallas_call(
+        finish_kernel,
+        out_shape=jax.ShapeDtypeStruct((2, CHUNK, NZ), jnp.float32),
+        in_specs=[vm] * 6,
+        out_specs=vm,
+        name="samples",
+    )(*terms, colour, coarse)
 
 
 AXES = ("shot", "probe")
@@ -275,95 +400,30 @@
     return routes(lambda x, zh, y, zl, c: ((x + k) % 4, zh, y, zl, c))
 
 
-def place_of(column):
-    return column % TILES * LANES + column // TILES
-
-
-def reorder(array, back=False):
-    columns = jnp.arange(NZ)
-    match = columns[None, :] == place_of(columns)[:, None]
-    match = match.T if back else match
-    return lax.dot_general(
-        array,
-        match.astype(jnp.float32),
-        (((array.ndim - 1,), (0,)), ((), ())),
-        precision=lax.Precision.HIGHEST,
-    )
-
-
-def shot_sources(encodings, wavelet):
-    columns = jnp.arange(NZ)
-    position = place_of(jnp.arange(NSHOT) * 2 + 1)
-    onehot = (position[:, None] == columns[None, :]).astype(jnp.float32)
-    amplitude = encodings.astype(jnp.float32)[:, None, :] * wavelet[None, :, :]
-    return jnp.einsum("stk,kz->stz", amplitude, onehot, precision=lax.Precision.HIGHEST)
-
-
-def block_parity(row_index, bounds):
-    inner = bounds[1:-1]
-    return jnp.sum((row_index[:, None] >= inner[None, :]).astype(jnp.int32), axis=1) % 2
-
-
-def window(array, chunk, dim):
-    rows = array.shape[dim]
-    top = lax.dynamic_slice_in_dim(array, jnp.maximum(chunk * CHUNK - EDGE, 0), EDGE, dim)
-    mid = lax.dynamic_slice_in_dim(array, chunk * CHUNK, CHUNK, dim)
-    low = lax.dynamic_slice_in_dim(
-        array, jnp.minimum(chunk * CHUNK + CHUNK, rows - EDGE), EDGE, dim
-    )
-    return jnp.concatenate([top, mid, low], axis=dim)
-
-
 def on_device(
     probes, coarse_sample, coefficient, receiver, checkpoints, encodings, wavelet, bounds
 ):
-    chunk = lax.axis_index("shot")
-    y = lax.axis_index("probe") % 4
-    sources = shot_sources(encodings, wavelet)
-    checkpoints = reorder(checkpoints)
-
-    row = chunk * CHUNK - EDGE + jnp.arange(WIN)
-    inside = ((row >= 0) & (row < 512))[:, None]
-    odd = (block_parity(row, bounds) == 1)[:, None]
-
-    extra = jnp.concatenate([sources, jnp.zeros_like(sources[:, :1])], axis=1)
-    extra = extra.reshape(2, 2, 2, NZ)
-    below = jnp.concatenate([checkpoints[:, :, :6], extra], axis=2)
-    edge = jnp.where(y == 0, below, checkpoints[:, :, 8:])
-    checkpoints, edge = lax.optimization_barrier((checkpoints, edge))
+    levels, edge = emit(checkpoints, encodings, wavelet)
     owns = []
     for k in range(2):
-        main = lax.ppermute(checkpoints, AXES, routes(functools.partial(main_source, k)))
+        main = lax.ppermute(levels, AXES, routes(functools.partial(main_source, k)))
         side = lax.ppermute(edge, AXES, routes(functools.partial(edge_source, k)))
         owns.append(jnp.concatenate([main, side], axis=2))
 
-    pair = window(probes, chunk, 1)
-    mine = reorder(jnp.where(inside, jnp.where(odd, pair[1], pair[0]), 0.0))
-    coef = reorder(jnp.where(inside, window(coefficient, chunk, 0), 0.0))
-    recv = reorder(jnp.where(inside, window(receiver, chunk, 0), 0.0))
-    colours = jnp.broadcast_to(odd.astype(jnp.float32), (WIN, NZ))
-    place = jnp.stack([y, 256 - chunk * CHUNK + EDGE]).astype(jnp.int32)
-    owns[0], mine, coef, recv, colours, place = lax.optimization_barrier(
-        (owns[0], mine, coef, recv, colours, place)
+    mine, coef, recv, colours = prepare(
+        bounds.reshape(1, 65), probes, coefficient, receiver
+    )
+    owns[1], mine, coef, recv, colours = lax.optimization_barrier(
+        (owns[1], mine, coef, recv, colours)
     )
 
     slabs = [[own] + [lax.ppermute(own, AXES, along_y(d)) for d in (1, 2, 3)] for own in owns]
     blocks = [mine] + [lax.ppermute(mine, AXES, along_x(d)) for d in (1, 2, 3)]
 
-    terms = apply(place, slabs[0], blocks, colours, coef, recv)
-    terms = apply(place, slabs[1], blocks, colours, coef, recv, terms)
-    total = terms[0]
-    for d in (1, 2, 3):
-        total = total + lax.ppermute(terms[d], AXES, along_x(4 - d))
-
-    total = reorder(total, back=True)
-    keep = odd[EDGE : EDGE + CHUNK]
-    return jnp.stack(
-        [
-            jnp.where(keep, total - coarse_sample[0], 0.0),
-            jnp.where(keep, 0.0, total - coarse_sample[1]),
-        ]
-    )
+    terms = apply(slabs[0], blocks, colours, coef, recv)
+    terms = apply(slabs[1], blocks, colours, coef, recv, terms)
+    parts = [terms[0]] + [lax.ppermute(terms[d], AXES, along_x(4 - d)) for d in (1, 2, 3)]
+    return finish(parts, colours, coarse_sample)
 
 
 def solution(mesh):

time: 86.4 us -> 85.1 us (0.985)
  the two profiles are of different devices: /device:TPU:1 before, /device:TPU:88 now
where the time goes in v3:
time: 85.1 us; the launch traced here: 84.8 us
  starting transfers between devices  30.5 us (36%)
  Pallas kernels  27.5 us (32%)
  waiting for transfers between devices  24.4 us (29%)
  local copies, waits for them, and re-layouts  2.15 us (3%)
    pallas_call x2, Pallas kernels, apply(): pl.pallas_call(functools.partial(kernel, shots=shots, has_total=bool(tota...  17.5 us
    ppermute x2, starting transfers between devices, on_device(): side = lax.ppermute(edge, AXES, routes(functools.partial(edge_source, k)))  10.2 us
    ppermute x2, starting transfers between devices, on_device(): main = lax.ppermute(levels, AXES, routes(functools.partial(main_source, k)))  9.41 us
    ppermute x6, waiting for transfers between devices, on_device(): lax.ppermute(own, AXES, along_y(d))  9.01 us
    ppermute x3, waiting for transfers between devices, on_device(): blocks = [mine] + [lax.ppermute(mine, AXES, along_x(d)) for d in (1, 2, 3)]  8.34 us
    ppermute x3, waiting for transfers between devices, on_device(): lax.ppermute(terms[d], AXES, along_x(4 - d))  5.45 us
    pallas_call x1, Pallas kernels, prepare(): pl.pallas_call(prepare_kernel, out_shape=[jax.ShapeDtypeStruct((WIN, NZ),...  4.32 us
    ppermute x6, starting transfers between devices, on_device(): lax.ppermute(own, AXES, along_y(d))  4.26 us
  transfers between devices with their start and end apart: 16, of which 5 were waited for; matrix products, arithmetic and copies ran while one was open for 0% of the time, Pallas kernels for 15%

profile of v3, /device:TPU:88, one launch (start us, length us, event | category | flops | bytes accessed | tf_op | source)
XLA Modules:
  0.0 84.8 jit_solution(4268288462849640710)
XLA Ops:
  0.0 2.7 %own_rows.1 = (f32[2,2,16,512]{3,2,1,0:T(8,128)}, f32[2,2,8,512]{3,2,1,0:T(8,128)}) custom-call(f32[2,2,16,512]{3,2,1,0:T(8,128)} %levels_ref.1, s32[2,256]{1,0:T(2,128)} %enc_ref.1, f32[3,256]{1,0:T(4,128)} %wav_ref.1), custom_call_target="tpu_custom_call" | custom-call | tf_op jit(solution)/shard_map/own_rows/pallas_call | solution.py:280
  2.7 4.0 %collective-permute-start.8 = (f32[2,2,16,512]{3,2,1,0:T(8,128)}, f32[2,2,16,512]{3,2,1,0:T(8,128)S(1)}, u32[]{:S(2)}, u32[]{:S(2)}) collective-permute-start(f32[2,2,16,512]{3,2,1,0:T(8,128)} %get-tuple-element.24), channel_id=1, source_target_pairs={{0,0},{4,32},{8,64},{12,96},{16,128},{20,160},{24,192},{28,224},{1... | collective-permute-start | bytes 393224 | tf_op jit(solution)/shard_map/ppermute | solution.py:409
  6.7 7.9 %collective-permute-start.9 = (f32[2,2,8,512]{3,2,1,0:T(8,128)}, f32[2,2,8,512]{3,2,1,0:T(8,128)S(1)}, u32[]{:S(2)}, u32[]{:S(2)}) collective-permute-start(f32[2,2,8,512]{3,2,1,0:T(8,128)} %get-tuple-element.25), channel_id=1, source_target_pairs={{4,0},{8,32},{12,64},{16,96},{20,128},{24,160},{28,192},{3,35},{7,... | collective-permute-start | bytes 196616 | tf_op jit(solution)/shard_map/ppermute | solution.py:410
  14.6 2.4 %collective-permute-start.1 = (f32[2,2,8,512]{3,2,1,0:T(8,128)}, f32[2,2,8,512]{3,2,1,0:T(8,128)S(1)}, u32[]{:S(2)}, u32[]{:S(2)}) collective-permute-start(f32[2,2,8,512]{3,2,1,0:T(8,128)} %get-tuple-element.25), channel_id=1, source_target_pairs={{36,0},{40,32},{44,64},{48,96},{52,128},{56,160},{60,192},{35,35},... | collective-permute-start | bytes 196616 | tf_op jit(solution)/shard_map/ppermute | solution.py:410
  16.9 5.4 %collective-permute-start = (f32[2,2,16,512]{3,2,1,0:T(8,128)}, f32[2,2,16,512]{3,2,1,0:T(8,128)S(1)}, u32[]{:S(2)}, u32[]{:S(2)}) collective-permute-start(f32[2,2,16,512]{3,2,1,0:T(8,128)} %get-tuple-element.24), channel_id=1, source_target_pairs={{32,0},{36,32},{40,64},{44,96},{48,128},{52,160},{56,192},{60,224}... | collective-permute-start | bytes 393224 | tf_op jit(solution)/shard_map/ppermute | solution.py:409
  22.3 4.3 %own_windows.1 = (f32[80,512]{1,0:T(8,128)}, f32[80,512]{1,0:T(8,128)}, f32[80,512]{1,0:T(8,128)}, f32[80,512]{1,0:T(8,128)}) custom-call(s32[1,65]{1,0:T(1,128)} %bitcast.1, f32[2,512,512]{2,1,0:T(8,128)} %probes.1, f32[512,512]{1,0:T(8,128)} %coefficient.1, f32[512,512]{1,0:T(8,128)} %receiver.1), custom_call_target="tpu_custom_call" | custom-call | bytes 12582912 | tf_op jit(solution)/shard_map/own_windows/pallas_call | solution.py:330
  26.7 0.0 collective-permute-done.8
  26.7 0.0 collective-permute-done.9
  26.7 0.0 copy-start.4
  26.7 0.1 collective-permute-start.12
  26.8 0.0 collective-permute-done.1
  26.8 1.6 %collective-permute-done = f32[2,2,16,512]{3,2,1,0:T(8,128)S(1)} collective-permute-done((f32[2,2,16,512]{3,2,1,0:T(8,128)}, f32[2,2,16,512]{3,2,1,0:T(8,128)S(1)}, u32[]{:S(2)}, u32[]{:S(2)}) %collective-permute-start) | collective-permute-done | bytes 131104 | tf_op jit(solution)/shard_map/ppermute | solution.py:409
  28.4 0.0 copy-start
  28.5 0.1 collective-permute-start.7
  28.5 1.4 %collective-permute-start.6 = (f32[80,512]{1,0:T(8,128)}, f32[80,512]{1,0:T(8,128)S(1)}, u32[]{:S(2)}, u32[]{:S(2)}) collective-permute-start(f32[80,512]{1,0:T(8,128)} %get-tuple-element.31.refs_4_), channel_id=1, source_target_pairs={{16,0},{48,32},{80,64},{112,96},{144,128},{176,160},{208,192},{240... | collective-permute-start | bytes 491528 | tf_op jit(solution)/shard_map/ppermute | solution.py:421
  29.9 1.9 %collective-permute-start.5 = (f32[80,512]{1,0:T(8,128)}, f32[80,512]{1,0:T(8,128)S(1)}, u32[]{:S(2)}, u32[]{:S(2)}) collective-permute-start(f32[80,512]{1,0:T(8,128)} %get-tuple-element.31.refs_4_), channel_id=1, source_target_pairs={{8,0},{40,32},{72,64},{104,96},{136,128},{168,160},{200,192},{232,... | collective-permute-start | bytes 491528 | tf_op jit(solution)/shard_map/ppermute | solution.py:421
  31.8 0.0 collective-permute-start.11
  31.8 8.3 %collective-permute-done.7.refs_7_ = f32[80,512]{1,0:T(8,128)S(1)} collective-permute-done((f32[80,512]{1,0:T(8,128)}, f32[80,512]{1,0:T(8,128)S(1)}, u32[]{:S(2)}, u32[]{:S(2)}) %collective-permute-start.7) | collective-permute-done | bytes 163872 | tf_op jit(solution)/shard_map/ppermute | solution.py:421
  40.1 0.0 collective-permute-start.10
  40.1 0.0 collective-permute-done.6.refs_6_
  40.1 0.0 copy-start.2
  40.1 3.2 %collective-permute-start.4 = (f32[2,2,24,512]{3,2,1,0:T(8,128)S(1)}, f32[2,2,24,512]{3,2,1,0:T(8,128)S(1)}, u32[]{:S(2)}, u32[]{:S(2)}) collective-permute-start(f32[2,2,24,512]{3,2,1,0:T(8,128)S(1)} %pad_maximum_fusion.refs_0_), channel_id=1, source_target_pairs={{3,0},{35,32},{67,64},{99,96},{131,128},{163,160},{195,192},{227,2... | collective-permute-start | bytes 589832 | tf_op jit(solution)/shard_map/ppermute | solution.py:420
  43.4 0.0 collective-permute-done.5.refs_5_
  43.4 0.0 collective-permute-start.3
  43.4 0.0 collective-permute-done.12.refs_3_
  43.4 0.9 %collective-permute-start.2 = (f32[2,2,24,512]{3,2,1,0:T(8,128)S(1)}, f32[2,2,24,512]{3,2,1,0:T(8,128)S(1)}, u32[]{:S(2)}, u32[]{:S(2)}) collective-permute-start(f32[2,2,24,512]{3,2,1,0:T(8,128)S(1)} %pad_maximum_fusion.refs_0_), channel_id=1, source_target_pairs={{1,0},{33,32},{65,64},{97,96},{129,128},{161,160},{193,192},{225,2... | collective-permute-start | bytes 589832 | tf_op jit(solution)/shard_map/ppermute | solution.py:420
  44.3 0.0 collective-permute-done.11.refs_2_
  44.3 9.0 %collective-permute-done.10.refs_1_ = f32[2,2,24,512]{3,2,1,0:T(8,128)S(1)} collective-permute-done((f32[2,2,24,512]{3,2,1,0:T(8,128)S(1)}, f32[2,2,24,512]{3,2,1,0:T(8,128)S(1)}, u32[]{:S(2)}, u32[]{:S(2)}) %collective-permute-start.10) | collective-permute-done | bytes 196640 | tf_op jit(solution)/shard_map/ppermute | solution.py:420
  53.3 0.0 copy-done.4
  53.3 0.0 copy-done.2
  53.4 0.7 copy-done.10
  54.1 8.6 %hessian_rows.2 = (f32[64,512]{1,0:T(8,128)}, f32[64,512]{1,0:T(8,128)}, f32[64,512]{1,0:T(8,128)}, f32[64,512]{1,0:T(8,128)}) custom-call(f32[2,2,24,512]{3,2,1,0:T(8,128)} %copy-done.4, f32[2,2,24,512]{3,2,1,0:T(8,128)} %copy-done.10, f32[2,2,24,512]{3,2,1,0:T(8,128)} %copy-done.8, f32[2,2,24,512]{3,2,1,0:T(8,128)} %copy-done.5, ...), custom_call_target="tpu_custom_call" | custom-call | flops 55050240 | bytes 4194304 | tf_op jit(solution)/shard_map/hessian_rows/pallas_call | solution.py:220
  62.7 0.0 collective-permute-done.4.refs_3_
  62.7 0.0 collective-permute-done.3.refs_2_
  62.7 0.0 collective-permute-done.2.refs_1_
  62.8 0.6 copy-done.6
  63.4 0.1 copy-done.7
  63.5 0.1 copy-done.9
  63.5 8.8 %hessian_rows.3 = (f32[64,512]{1,0:T(8,128)}, f32[64,512]{1,0:T(8,128)}, f32[64,512]{1,0:T(8,128)}, f32[64,512]{1,0:T(8,128)}) custom-call(f32[2,2,24,512]{3,2,1,0:T(8,128)} %copy-done, f32[2,2,24,512]{3,2,1,0:T(8,128)} %copy-done.9, f32[2,2,24,512]{3,2,1,0:T(8,128)} %copy-done.7, f32[2,2,24,512]{3,2,1,0:T(8,128)} %copy-done.6, ...), custom_call_target="tpu_custom_call" | custom-call | flops 55050240 | bytes 4194304 | tf_op jit(solution)/shard_map/hessian_rows/pallas_call | solution.py:220
  72.4 0.0 collective-permute-start.13
  72.4 0.6 collective-permute-start.14
  73.0 2.6 %collective-permute-start.15 = (f32[64,512]{1,0:T(8,128)}, f32[64,512]{1,0:T(8,128)S(1)}, u32[]{:S(2)}, u32[]{:S(2)}) collective-permute-start(f32[64,512]{1,0:T(8,128)} %get-tuple-element.42), channel_id=1, source_target_pairs={{8,0},{40,32},{72,64},{104,96},{136,128},{168,160},{200,192},{232,... | collective-permute-start | bytes 393224 | tf_op jit(solution)/shard_map/ppermute | solution.py:425
  75.6 4.6 %collective-permute-done.13.b = f32[64,512]{1,0:T(8,128)S(1)} collective-permute-done((f32[64,512]{1,0:T(8,128)}, f32[64,512]{1,0:T(8,128)S(1)}, u32[]{:S(2)}, u32[]{:S(2)}) %collective-permute-start.13) | collective-permute-done | bytes 131104 | tf_op jit(solution)/shard_map/ppermute | solution.py:425
  80.2 0.0 collective-permute-done.14.c
  80.2 0.9 %collective-permute-done.15.d = f32[64,512]{1,0:T(8,128)S(1)} collective-permute-done((f32[64,512]{1,0:T(8,128)}, f32[64,512]{1,0:T(8,128)S(1)}, u32[]{:S(2)}, u32[]{:S(2)}) %collective-permute-start.15) | collective-permute-done | bytes 131104 | tf_op jit(solution)/shard_map/ppermute | solution.py:425
  81.1 0.0 copy-done.11
  81.1 0.6 copy-done.13
  81.7 3.1 %samples.1 = f32[2,64,512]{2,1,0:T(8,128)} custom-call(f32[64,512]{1,0:T(8,128)} %get-tuple-element.39.a, f32[64,512]{1,0:T(8,128)} %copy-done.11, f32[64,512]{1,0:T(8,128)} %copy-done.12, f32[64,512]{1,0:T(8,128)} %copy-done.13, f32[80,512]{1,0:T(8,128)} %get-tuple-element.32.refs_8_.colour, f32[2,64,512]{2,1,0:T(8,128)} %coarse.1), custom_call_target="tpu_custom_call" | custom-call | tf_op jit(solution)/shard_map/samples/pallas_call | solution.py:355
  (20 shorter events, 0.1 us)
Async XLA Ops:
  2.7 24.0 %collective-permute-start.8 = (f32[2,2,16,512]{3,2,1,0:T(8,128)}, f32[2,2,16,512]{3,2,1,0:T(8,128)S(1)}, u32[]{:S(2)}, u32[]{:S(2)}) collective-permute-start(f32[2,2,16,512]{3,2,1,0:T(8,128)} %get-tuple-element.24), channel_id=1, source_target_pairs={{0,0},{4,32},{8,64},{12,96},{16,128},{20,160},{24,192},{28,224},{1... | collective-permute-start | bytes 393224 | tf_op jit(solution)/shard_map/ppermute | solution.py:409
  6.7 20.0 %collective-permute-start.9 = (f32[2,2,8,512]{3,2,1,0:T(8,128)}, f32[2,2,8,512]{3,2,1,0:T(8,128)S(1)}, u32[]{:S(2)}, u32[]{:S(2)}) collective-permute-start(f32[2,2,8,512]{3,2,1,0:T(8,128)} %get-tuple-element.25), channel_id=1, source_target_pairs={{4,0},{8,32},{12,64},{16,96},{20,128},{24,160},{28,192},{3,35},{7,... | collective-permute-start | bytes 196616 | tf_op jit(solution)/shard_map/ppermute | solution.py:410
  14.6 12.3 %collective-permute-start.1 = (f32[2,2,8,512]{3,2,1,0:T(8,128)}, f32[2,2,8,512]{3,2,1,0:T(8,128)S(1)}, u32[]{:S(2)}, u32[]{:S(2)}) collective-permute-start(f32[2,2,8,512]{3,2,1,0:T(8,128)} %get-tuple-element.25), channel_id=1, source_target_pairs={{36,0},{40,32},{44,64},{48,96},{52,128},{56,160},{60,192},{35,35},... | collective-permute-start | bytes 196616 | tf_op jit(solution)/shard_map/ppermute | solution.py:410
  16.9 11.5 %collective-permute-start = (f32[2,2,16,512]{3,2,1,0:T(8,128)}, f32[2,2,16,512]{3,2,1,0:T(8,128)S(1)}, u32[]{:S(2)}, u32[]{:S(2)}) collective-permute-start(f32[2,2,16,512]{3,2,1,0:T(8,128)} %get-tuple-element.24), channel_id=1, source_target_pairs={{32,0},{36,32},{40,64},{44,96},{48,128},{52,160},{56,192},{60,224}... | collective-permute-start | bytes 393224 | tf_op jit(solution)/shard_map/ppermute | solution.py:409
  26.7 26.6 %copy-start.4 = (f32[2,2,24,512]{3,2,1,0:T(8,128)}, f32[2,2,24,512]{3,2,1,0:T(8,128)S(1)}, u32[]{:S(2)}) copy-start(f32[2,2,24,512]{3,2,1,0:T(8,128)S(1)} %constant_dynamic-update-slice_fusion.refs_0_) | copy-start | bytes 589828
  26.7 16.6 %collective-permute-start.12 = (f32[2,2,24,512]{3,2,1,0:T(8,128)S(1)}, f32[2,2,24,512]{3,2,1,0:T(8,128)S(1)}, u32[]{:S(2)}, u32[]{:S(2)}) collective-permute-start(f32[2,2,24,512]{3,2,1,0:T(8,128)S(1)} %constant_dynamic-update-slice_fusion.refs_0_), channel_id=1, source_target_pairs={{3,0},{35,32},{67,64},{99,96},{131,128},{163,160},{195,192},{227,2... | collective-permute-start | bytes 589832 | tf_op jit(solution)/shard_map/ppermute | solution.py:420
  28.4 34.3 %copy-start = (f32[2,2,24,512]{3,2,1,0:T(8,128)}, f32[2,2,24,512]{3,2,1,0:T(8,128)S(1)}, u32[]{:S(2)}) copy-start(f32[2,2,24,512]{3,2,1,0:T(8,128)S(1)} %pad_maximum_fusion.refs_0_) | copy-start | bytes 589828
  28.5 11.7 %collective-permute-start.7 = (f32[80,512]{1,0:T(8,128)}, f32[80,512]{1,0:T(8,128)S(1)}, u32[]{:S(2)}, u32[]{:S(2)}) collective-permute-start(f32[80,512]{1,0:T(8,128)} %get-tuple-element.31.refs_4_), channel_id=1, source_target_pairs={{24,0},{56,32},{88,64},{120,96},{152,128},{184,160},{216,192},{248... | collective-permute-start | bytes 491528 | tf_op jit(solution)/shard_map/ppermute | solution.py:421
  28.5 11.6 %collective-permute-start.6 = (f32[80,512]{1,0:T(8,128)}, f32[80,512]{1,0:T(8,128)S(1)}, u32[]{:S(2)}, u32[]{:S(2)}) collective-permute-start(f32[80,512]{1,0:T(8,128)} %get-tuple-element.31.refs_4_), channel_id=1, source_target_pairs={{16,0},{48,32},{80,64},{112,96},{144,128},{176,160},{208,192},{240... | collective-permute-start | bytes 491528 | tf_op jit(solution)/shard_map/ppermute | solution.py:421
  29.9 13.5 %collective-permute-start.5 = (f32[80,512]{1,0:T(8,128)}, f32[80,512]{1,0:T(8,128)S(1)}, u32[]{:S(2)}, u32[]{:S(2)}) collective-permute-start(f32[80,512]{1,0:T(8,128)} %get-tuple-element.31.refs_4_), channel_id=1, source_target_pairs={{8,0},{40,32},{72,64},{104,96},{136,128},{168,160},{200,192},{232,... | collective-permute-start | bytes 491528 | tf_op jit(solution)/shard_map/ppermute | solution.py:421
  31.8 12.6 %collective-permute-start.11 = (f32[2,2,24,512]{3,2,1,0:T(8,128)S(1)}, f32[2,2,24,512]{3,2,1,0:T(8,128)S(1)}, u32[]{:S(2)}, u32[]{:S(2)}) collective-permute-start(f32[2,2,24,512]{3,2,1,0:T(8,128)S(1)} %constant_dynamic-update-slice_fusion.refs_0_), channel_id=1, source_target_pairs={{2,0},{34,32},{66,64},{98,96},{130,128},{162,160},{194,192},{226,2... | collective-permute-start | bytes 589832 | tf_op jit(solution)/shard_map/ppermute | solution.py:420
  40.1 13.2 %copy-start.1 = (f32[80,512]{1,0:T(8,128)}, f32[80,512]{1,0:T(8,128)S(1)}, u32[]{:S(2)}) copy-start(f32[80,512]{1,0:T(8,128)S(1)} %collective-permute-done.7.refs_7_) | copy-start | bytes 491524
  40.1 13.2 %collective-permute-start.10 = (f32[2,2,24,512]{3,2,1,0:T(8,128)S(1)}, f32[2,2,24,512]{3,2,1,0:T(8,128)S(1)}, u32[]{:S(2)}, u32[]{:S(2)}) collective-permute-start(f32[2,2,24,512]{3,2,1,0:T(8,128)S(1)} %constant_dynamic-update-slice_fusion.refs_0_), channel_id=1, source_target_pairs={{1,0},{33,32},{65,64},{97,96},{129,128},{161,160},{193,192},{225,2... | collective-permute-start | bytes 589832 | tf_op jit(solution)/shard_map/ppermute | solution.py:420
  40.1 13.2 %copy-start.2 = (f32[80,512]{1,0:T(8,128)}, f32[80,512]{1,0:T(8,128)S(1)}, u32[]{:S(2)}) copy-start(f32[80,512]{1,0:T(8,128)S(1)} %collective-permute-done.6.refs_6_) | copy-start | bytes 491524
  40.1 22.6 %collective-permute-start.4 = (f32[2,2,24,512]{3,2,1,0:T(8,128)S(1)}, f32[2,2,24,512]{3,2,1,0:T(8,128)S(1)}, u32[]{:S(2)}, u32[]{:S(2)}) collective-permute-start(f32[2,2,24,512]{3,2,1,0:T(8,128)S(1)} %pad_maximum_fusion.refs_0_), channel_id=1, source_target_pairs={{3,0},{35,32},{67,64},{99,96},{131,128},{163,160},{195,192},{227,2... | collective-permute-start | bytes 589832 | tf_op jit(solution)/shard_map/ppermute | solution.py:420
  43.4 10.0 %copy-start.3 = (f32[80,512]{1,0:T(8,128)}, f32[80,512]{1,0:T(8,128)S(1)}, u32[]{:S(2)}) copy-start(f32[80,512]{1,0:T(8,128)S(1)} %collective-permute-done.5.refs_5_) | copy-start | bytes 491524
  43.4 19.4 %collective-permute-start.3 = (f32[2,2,24,512]{3,2,1,0:T(8,128)S(1)}, f32[2,2,24,512]{3,2,1,0:T(8,128)S(1)}, u32[]{:S(2)}, u32[]{:S(2)}) collective-permute-start(f32[2,2,24,512]{3,2,1,0:T(8,128)S(1)} %pad_maximum_fusion.refs_0_), channel_id=1, source_target_pairs={{2,0},{34,32},{66,64},{98,96},{130,128},{162,160},{194,192},{226,2... | collective-permute-start | bytes 589832 | tf_op jit(solution)/shard_map/ppermute | solution.py:420
  43.4 10.0 %copy-start.5 = (f32[2,2,24,512]{3,2,1,0:T(8,128)}, f32[2,2,24,512]{3,2,1,0:T(8,128)S(1)}, u32[]{:S(2)}) copy-start(f32[2,2,24,512]{3,2,1,0:T(8,128)S(1)} %collective-permute-done.12.refs_3_) | copy-start | bytes 589828
  43.4 19.3 %collective-permute-start.2 = (f32[2,2,24,512]{3,2,1,0:T(8,128)S(1)}, f32[2,2,24,512]{3,2,1,0:T(8,128)S(1)}, u32[]{:S(2)}, u32[]{:S(2)}) collective-permute-start(f32[2,2,24,512]{3,2,1,0:T(8,128)S(1)} %pad_maximum_fusion.refs_0_), channel_id=1, source_target_pairs={{1,0},{33,32},{65,64},{97,96},{129,128},{161,160},{193,192},{225,2... | collective-permute-start | bytes 589832 | tf_op jit(solution)/shard_map/ppermute | solution.py:420
  44.3 9.0 %copy-start.8 = (f32[2,2,24,512]{3,2,1,0:T(8,128)}, f32[2,2,24,512]{3,2,1,0:T(8,128)S(1)}, u32[]{:S(2)}) copy-start(f32[2,2,24,512]{3,2,1,0:T(8,128)S(1)} %collective-permute-done.11.refs_2_) | copy-start | bytes 589828
  53.4 0.7 copy-start.10
  62.7 0.7 copy-start.6
  62.7 0.7 copy-start.7
  62.7 0.8 copy-start.9
  72.4 7.8 %collective-permute-start.13 = (f32[64,512]{1,0:T(8,128)}, f32[64,512]{1,0:T(8,128)S(1)}, u32[]{:S(2)}, u32[]{:S(2)}) collective-permute-start(f32[64,512]{1,0:T(8,128)} %get-tuple-element.40), channel_id=1, source_target_pairs={{24,0},{56,32},{88,64},{120,96},{152,128},{184,160},{216,192},{248... | collective-permute-start | bytes 393224 | tf_op jit(solution)/shard_map/ppermute | solution.py:425
  72.4 7.8 %collective-permute-start.14 = (f32[64,512]{1,0:T(8,128)}, f32[64,512]{1,0:T(8,128)S(1)}, u32[]{:S(2)}, u32[]{:S(2)}) collective-permute-start(f32[64,512]{1,0:T(8,128)} %get-tuple-element.41), channel_id=1, source_target_pairs={{16,0},{48,32},{80,64},{112,96},{144,128},{176,160},{208,192},{240... | collective-permute-start | bytes 393224 | tf_op jit(solution)/shard_map/ppermute | solution.py:425
  73.0 8.1 %collective-permute-start.15 = (f32[64,512]{1,0:T(8,128)}, f32[64,512]{1,0:T(8,128)S(1)}, u32[]{:S(2)}, u32[]{:S(2)}) collective-permute-start(f32[64,512]{1,0:T(8,128)} %get-tuple-element.42), channel_id=1, source_target_pairs={{8,0},{40,32},{72,64},{104,96},{136,128},{168,160},{200,192},{232,... | collective-permute-start | bytes 393224 | tf_op jit(solution)/shard_map/ppermute | solution.py:425
  80.2 0.9 %copy-start.11 = (f32[64,512]{1,0:T(8,128)}, f32[64,512]{1,0:T(8,128)S(1)}, u32[]{:S(2)}) copy-start(f32[64,512]{1,0:T(8,128)S(1)} %collective-permute-done.13.b) | copy-start | bytes 393220
  80.2 0.9 %copy-start.12 = (f32[64,512]{1,0:T(8,128)}, f32[64,512]{1,0:T(8,128)S(1)}, u32[]{:S(2)}) copy-start(f32[64,512]{1,0:T(8,128)S(1)} %collective-permute-done.14.c) | copy-start | bytes 393220
  81.1 0.7 copy-start.13

commit v4 on v3

--- a/solution.py
+++ b/solution.py
@@ -26,47 +26,32 @@
     return [left + tiles[1], tiles[0] + tiles[2], tiles[1] + tiles[3], tiles[2] + right]
 
 
-def kernel(*refs, shots, has_total):
+def kernel(*refs, shots):
     my_y = lax.rem(lax.axis_index("probe"), 4)
     source_row = NZ // 2 + EDGE - CHUNK * lax.axis_index("shot")
     slabs = refs[0:4]
     blocks = refs[4:8]
     parity_ref, coef_ref, recv_ref = refs[8:11]
     n = 11
-    if has_total:
-        totals = refs[n : n + 4]
-        n += 4
     outs = refs[n : n + 4]
-    u_ref, v_ref, e_ref, w_ref, grad_ref, *d_refs = refs[n + 4 :]
-    d_refs = [d_refs[4 * i : 4 * i + 4] for i in range(shots)]
+    u_ref, edge_ref, sem, v_ref, e_ref, w_ref, grad_ref, back_ref, *d_refs = refs[n + 4 :]
+    d_refs = [d_refs[4 * i : 4 * i + 4] for i in range(2)]
 
     lane = lax.broadcasted_iota(jnp.int32, (8, LANES), 1)
     first = lane == 0
     last = lane == LANES - 1
 
+    copies = []
     for k in range(4):
-        y = lax.rem(my_y + k, 4)
-        for i in range(shots):
-            for lev in range(2):
-                base = pl.multiple_of(EDGE + 16 * y, 8)
-                u_ref[i, lev, pl.ds(base, 16), :] = slabs[k][i, lev, 0:16, :]
-
-        @pl.when(y == 3)
-        def _():
-            for i in range(shots):
-                for lev in range(2):
-                    u_ref[i, lev, 0:8, :] = slabs[k][i, lev, 16:24, :]
-
-        @pl.when(y == 0)
-        def _():
-            for i in range(shots):
-                for lev in range(2):
-                    u_ref[i, lev, 72:80, :] = slabs[k][i, lev, 16:24, :]
-                for t in range(3):
-                    u_ref[i, 5 + t // 2, 6 + t % 2 : 7 + t % 2, :] = slabs[k][
-                        i, t // 2, 22 + t % 2 : 23 + t % 2, :
-                    ]
-
+        base = pl.multiple_of(EDGE + 16 * lax.rem(my_y + k, 4), 8)
+        for source, target in (
+            (slabs[k].at[:, :, 0:16, :], u_ref.at[:, 0:2, pl.ds(base, 16), :]),
+            (slabs[k].at[:, :, 16:24, :], edge_ref.at[k]),
+        ):
+            copies.append(pltpu.make_async_copy(source, target, sem.at[len(copies)]))
+            copies[-1].start()
+
+    back_ref[...] = match(NZ, None, back=True)
     coef = coef_ref[...]
     e_ref[...] = 2.0 - 4.0 * coef
     w_ref[...] = recv_ref[...] * recv_ref[...]
@@ -78,6 +63,20 @@
             v = jnp.where(odd if colour else jnp.logical_not(odd), w, 0.0)
             for j, tile in enumerate(split(v)):
                 v_ref.at[j][pl.ds(2 * q + colour, WIN, stride=8), :] = tile
+
+    for copy in copies:
+        copy.wait()
+    for k in range(4):
+        y = lax.rem(my_y + k, 4)
+
+        @pl.when(y == 3)
+        def _():
+            u_ref[:, 0:2, 0:8, :] = edge_ref[k]
+
+        @pl.when(y == 0)
+        def _():
+            u_ref[:, 0:2, 72:80, :] = edge_ref[k]
+            u_ref[:, 5:7, 6:8, :] = edge_ref[k, :, :, 6:8, :]
 
     row = lax.broadcasted_iota(jnp.int32, (WIN, LANES), 0)
     column = lax.broadcasted_iota(jnp.int32, (WIN, LANES), 1)
@@ -127,109 +126,120 @@
         side = sideways(mid, first, last)
         return plus(times(e, mid), times(c, plus(plus(up, down), side)))
 
-    def source(i, r):
-        return times(field(v_ref, r), level(i, 0, r))
-
-    def forward(t, r, carry):
-        v = field(v_ref, r)
-        c = wide(coef_ref, r)
-        e = wide(e_ref, r)
-        w = wide(w_ref, r) if t == 3 else None
-        ahead = field(v_ref, r + 1) if t == 1 else None
-        out = []
-        for i in range(shots):
-            up, mid = carry[2 * i], carry[2 * i + 1]
-            if t == 1:
-                down = times(ahead, level(i, 0, r + 1))
-                store(d_refs[i][0], r + 1, down)
-            else:
-                down = field(d_refs[i][t - 1], r + 1)
-            new = plus(stencil(c, e, up, mid, down), times(v, level(i, t, r)))
-            if t >= 2:
-                new = minus(new, field(d_refs[i][t - 2], r))
-            store(d_refs[i][t], r, times(w, new) if t == 3 else new)
-            out += [mid, down]
-        return out
-
-    for t in range(1, 4):
-        lo, hi = 2 + t, 78 - t
-        init = []
-        for i in range(shots):
-            if t == 1:
-                rows = [source(i, lo - 1), source(i, lo)]
-                store(d_refs[i][0], lo, rows[1])
-            else:
-                rows = [field(d_refs[i][t - 1], lo - 1), field(d_refs[i][t - 1], lo)]
-            init += rows
-        lax.fori_loop(lo, hi, functools.partial(forward, t), init, unroll=UNROLLS[t - 1])
-
-    def adjoint(t, r, carry):
-        w = wide(w_ref, r)
-        e = wide(e_ref, r)
-        cn = wide(coef_ref, r + 1)
-        out = []
-        total = None
-        for i in range(shots):
-            up, mid, here = carry[3 * i], carry[3 * i + 1], carry[3 * i + 2]
-            below = field(d_refs[i][t + 1], r + 1)
-            down = times(cn, below)
-            side = sideways(mid, first, last)
-            new = plus(times(w, field(d_refs[i][t], r)), times(e, here))
-            new = plus(new, plus(plus(up, down), side))
-            if t <= 1:
-                beyond = field(d_refs[i][t + 2], r)
-                new = minus(new, beyond)
+    def sweeps(group):
+        def source(i, r):
+            return times(field(v_ref, r), level(2 * group + i, 0, r))
+
+        def forward(t, r, carry):
+            v = field(v_ref, r)
+            c = wide(coef_ref, r)
+            e = wide(e_ref, r)
+            w = wide(w_ref, r) if t == 3 else None
+            ahead = field(v_ref, r + 1) if t == 1 else None
+            out = []
+            for i in range(2):
+                up, mid = carry[2 * i], carry[2 * i + 1]
+                if t == 1:
+                    down = times(ahead, level(2 * group + i, 0, r + 1))
+                    store(d_refs[i][0], r + 1, down)
+                else:
+                    down = field(d_refs[i][t - 1], r + 1)
+                new = plus(stencil(c, e, up, mid, down), times(v, level(2 * group + i, t, r)))
+                if t >= 2:
+                    new = minus(new, field(d_refs[i][t - 2], r))
+                store(d_refs[i][t], r, times(w, new) if t == 3 else new)
+                out += [mid, down]
+            return out
+
+        for t in range(1, 4):
+            lo, hi = 2 + t, 78 - t
+            init = []
+            for i in range(2):
+                if t == 1:
+                    rows = [source(i, lo - 1), source(i, lo)]
+                    store(d_refs[i][0], lo, rows[1])
+                else:
+                    rows = [field(d_refs[i][t - 1], lo - 1), field(d_refs[i][t - 1], lo)]
+                init += rows
+            lax.fori_loop(lo, hi, functools.partial(forward, t), init, unroll=UNROLLS[t - 1])
+
+        def adjoint(t, r, carry):
+            w = wide(w_ref, r)
+            e = wide(e_ref, r)
+            cn = wide(coef_ref, r + 1)
+            out = []
+            total = None
+            for i in range(2):
+                up, mid, here = carry[3 * i], carry[3 * i + 1], carry[3 * i + 2]
+                below = field(d_refs[i][t + 1], r + 1)
+                down = times(cn, below)
+                side = sideways(mid, first, last)
+                new = plus(times(w, field(d_refs[i][t], r)), times(e, here))
+                new = plus(new, plus(plus(up, down), side))
+                if t <= 1:
+                    beyond = field(d_refs[i][t + 2], r)
+                    new = minus(new, beyond)
+                if t == 0:
+                    final = field(d_refs[i][3], r)
+                    for l, a in enumerate((new, here, beyond, final)):
+                        term = times(a, level(2 * group + i, l, r))
+                        total = term if total is None else plus(total, term)
+                else:
+                    store(d_refs[i][t], r, new)
+                out += [mid, down, below]
             if t == 0:
-                final = field(d_refs[i][3], r)
-                for l, a in enumerate((new, here, beyond, final)):
-                    term = times(a, level(i, l, r))
-                    total = term if total is None else plus(total, term)
-            else:
-                store(d_refs[i][t], r, new)
-            out += [mid, down, below]
-        if t == 0:
-            store(grad_ref, r - EDGE, total)
-        return out
-
-    for t in (2, 1, 0):
-        lo, hi = 8 - t, 72 + t
-        init = []
-        c0, c1 = wide(coef_ref, lo - 1), wide(coef_ref, lo)
-        for i in range(shots):
-            a0, a1 = field(d_refs[i][t + 1], lo - 1), field(d_refs[i][t + 1], lo)
-            init += [times(c0, a0), times(c1, a1), a1]
-        lax.fori_loop(lo, hi, functools.partial(adjoint, t), init, unroll=UNROLLS[5 - t])
+                if group:
+                    total = plus(total, field(grad_ref, r - EDGE))
+                store(grad_ref, r - EDGE, total)
+            return out
+
+        for t in (2, 1, 0):
+            lo, hi = 8 - t, 72 + t
+            init = []
+            c0, c1 = wide(coef_ref, lo - 1), wide(coef_ref, lo)
+            for i in range(2):
+                a0, a1 = field(d_refs[i][t + 1], lo - 1), field(d_refs[i][t + 1], lo)
+                init += [times(c0, a0), times(c1, a1), a1]
+            lax.fori_loop(lo, hi, functools.partial(adjoint, t), init, unroll=UNROLLS[5 - t])
+
+    for group in range(shots // 2):
+        sweeps(group)
 
     odd = parity_ref[EDGE : EDGE + CHUNK, :] > 0.5
+    rows = []
     for q in range(4):
+        tiles = []
         for j in range(TILES):
-            here = slice(LANES * j, LANES * (j + 1))
             even = grad_ref.at[j][pl.ds(2 * q, CHUNK, stride=8), :]
             other = grad_ref.at[j][pl.ds(2 * q + 1, CHUNK, stride=8), :]
-            result = jnp.where(odd[:, here], even, other)
-            if has_total:
-                result = result + totals[q][:, here]
-            outs[q][:, here] = result
-
-
-def apply(slabs, blocks, parity, coef, recv, totals=()):
+            tiles.append(jnp.where(odd[:, LANES * j : LANES * (j + 1)], even, other))
+        rows.append(jnp.concatenate(tiles, axis=1))
+    result = exact_dot(jnp.concatenate(rows, axis=0), back_ref[...])
+    for q in range(4):
+        outs[q][...] = result[CHUNK * q : CHUNK * (q + 1)]
+
+
+def apply(slabs, blocks, parity, coef, recv):
     shots = slabs[0].shape[0]
     vm = pl.BlockSpec(memory_space=pltpu.VMEM)
-    args = [*slabs, *blocks, parity, coef, recv, *totals]
+    args = [*slabs, *blocks, parity, coef, recv]
     big = pltpu.VMEM((TILES, 8 * WIN, LANES), jnp.float32)
     return pl.pallas_call(
-        functools.partial(kernel, shots=shots, has_total=bool(totals)),
+        functools.partial(kernel, shots=shots),
         out_shape=[jax.ShapeDtypeStruct((CHUNK, NZ), jnp.float32)] * 4,
-        in_specs=[vm] * len(args),
+        in_specs=[pl.BlockSpec(memory_space=pltpu.HBM)] * 4 + [vm] * (len(args) - 4),
         out_specs=[vm] * 4,
         scratch_shapes=[
             pltpu.VMEM((shots, 7, WIN, NZ), jnp.float32),
+            pltpu.VMEM((4, shots, 2, 8, NZ), jnp.float32),
+            pltpu.SemaphoreType.DMA((8,)),
             big,
             pltpu.VMEM((WIN, NZ), jnp.float32),
             pltpu.VMEM((WIN, NZ), jnp.float32),
             pltpu.VMEM((TILES, 8 * CHUNK, LANES), jnp.float32),
+            pltpu.VMEM((NZ, NZ), jnp.bfloat16),
         ]
-        + [big] * (4 * shots),
+        + [big] * 8,
         compiler_params=pltpu.CompilerParams(vmem_limit_bytes=56 * 1024 * 1024),
         cost_estimate=pl.CostEstimate(
             flops=shots * 8 * 8 * 70 * 512 * 12, bytes_accessed=4 << 20, transcendentals=0
@@ -238,19 +248,22 @@
     )(*args)
 
 
-def match(sources, column_of):
+def match(sources, column_of, back=False):
     shape = (sources, NZ)
-    column = column_of(lax.broadcasted_iota(jnp.int32, shape, 0))
-    place = lax.broadcasted_iota(jnp.int32, shape, 1)
-    kept = TILES * (place & (LANES - 1)) + place // LANES
-    return jnp.where(column == kept, 1.0, 0.0).astype(jnp.float32)
-
-
-def exact_dot(a, b, transposed=False):
-    dims = (((1,), (1 if transposed else 0,)), ((), ()))
-    return lax.dot_general(
-        a, b, dims, precision=lax.Precision.HIGHEST, preferred_element_type=jnp.float32
-    )
+    here = lax.broadcasted_iota(jnp.int32, shape, 0)
+    there = lax.broadcasted_iota(jnp.int32, shape, 1)
+    place, column = (here, there) if back else (there, column_of(here))
+    kept = TILES * (place & (LANES - 1)) + (place >> 7)
+    return jnp.where(column == kept, 1.0, 0.0).astype(jnp.bfloat16)
+
+
+def exact_dot(a, b):
+    high = a.astype(jnp.bfloat16)
+    rest = a - high.astype(jnp.float32)
+    middle = rest.astype(jnp.bfloat16)
+    low = (rest - middle.astype(jnp.float32)).astype(jnp.bfloat16)
+    x, y, z = (jnp.dot(part, b, preferred_element_type=jnp.float32) for part in (high, middle, low))
+    return x + y + z
 
 
 def emit_kernel(levels_ref, enc_ref, wav_ref, main_ref, edge_ref):
@@ -343,24 +356,6 @@
     )(bounds, probes, coefficient, receiver)
 
 
-def finish_kernel(a, b, c, d, colour, coarse, out):
-    total = exact_dot(a[...] + b[...] + c[...] + d[...], match(NZ, lambda c: c), transposed=True)
-    odd = colour[EDGE : EDGE + CHUNK, :] > 0.5
-    out[0] = jnp.where(odd, total - coarse[0], 0.0)
-    out[1] = jnp.where(odd, 0.0, total - coarse[1])
-
-
-def finish(terms, colour, coarse):
-    vm = pl.BlockSpec(memory_space=pltpu.VMEM)
-    return pl.pallas_call(
-        finish_kernel,
-        out_shape=jax.ShapeDtypeStruct((2, CHUNK, NZ), jnp.float32),
-        in_specs=[vm] * 6,
-        out_specs=vm,
-        name="samples",
-    )(*terms, colour, coarse)
-
-
 AXES = ("shot", "probe")
 
 
@@ -400,6 +395,11 @@
     return routes(lambda x, zh, y, zl, c: ((x + k) % 4, zh, y, zl, c))
 
 
+def spread(array, along):
+    far = lax.ppermute(array, AXES, along(2))
+    return [array, lax.ppermute(array, AXES, along(1)), far, lax.ppermute(array, AXES, along(3))]
+
+
 def on_device(
     probes, coarse_sample, coefficient, receiver, checkpoints, encodings, wavelet, bounds
 ):
@@ -413,17 +413,19 @@
     mine, coef, recv, colours = prepare(
         bounds.reshape(1, 65), probes, coefficient, receiver
     )
-    owns[1], mine, coef, recv, colours = lax.optimization_barrier(
-        (owns[1], mine, coef, recv, colours)
+
+    own, mine, coef, recv, colours = lax.optimization_barrier(
+        (jnp.concatenate(owns, axis=0), mine, coef, recv, colours)
     )
-
-    slabs = [[own] + [lax.ppermute(own, AXES, along_y(d)) for d in (1, 2, 3)] for own in owns]
-    blocks = [mine] + [lax.ppermute(mine, AXES, along_x(d)) for d in (1, 2, 3)]
-
-    terms = apply(slabs[0], blocks, colours, coef, recv)
-    terms = apply(slabs[1], blocks, colours, coef, recv, terms)
-    parts = [terms[0]] + [lax.ppermute(terms[d], AXES, along_x(4 - d)) for d in (1, 2, 3)]
-    return finish(parts, colours, coarse_sample)
+    slabs = spread(own, along_y)
+    blocks = spread(mine, along_x)
+
+    terms = apply(slabs, blocks, colours, coef, recv)
+    parts = [terms[0]] + [lax.ppermute(terms[d], AXES, along_x(4 - d)) for d in (2, 1, 3)]
+    total = parts[0] + parts[1] + parts[2] + parts[3]
+    odd = colours[EDGE : EDGE + CHUNK] > 0.5
+    keep = odd[None] != (jnp.arange(2) == 1)[:, None, None]
+    return jnp.where(keep, total[None] - coarse_sample, 0.0)
 
 
 def solution(mesh):

time: 85.1 us -> 79.9 us (0.939)
  the two profiles are of different devices: /device:TPU:88 before, /device:TPU:1 now
where the time goes in v4:
time: 79.9 us; the launch traced here: 78.9 us
  starting transfers between devices  32.8 us (41%)
  Pallas kernels  22 us (28%)
  waiting for transfers between devices  21.3 us (27%)
  other arithmetic  1.81 us (2%)
    pallas_call x1, Pallas kernels, apply(): pl.pallas_call(functools.partial(kernel, shots=shots), out_shape=[jax.Sha...  16.3 us
    ppermute x2, starting transfers between devices, on_device(): main = lax.ppermute(levels, AXES, routes(functools.partial(main_source, k)))  10.3 us
    ppermute x2, starting transfers between devices, spread(): lax.ppermute(array, AXES, along(1))  8.55 us
    ppermute x2, waiting for transfers between devices, spread(): lax.ppermute(array, AXES, along(3))  7.9 us
    ppermute x3, starting transfers between devices, on_device(): lax.ppermute(terms[d], AXES, along_x(4 - d))  7.89 us
    ppermute x2, waiting for transfers between devices, on_device(): side = lax.ppermute(edge, AXES, routes(functools.partial(edge_source, k)))  5.98 us
    ppermute x3, waiting for transfers between devices, on_device(): lax.ppermute(terms[d], AXES, along_x(4 - d))  4.07 us
    pallas_call x1, Pallas kernels, prepare(): pl.pallas_call(prepare_kernel, out_shape=[jax.ShapeDtypeStruct((WIN, NZ),...  3.6 us
  transfers between devices with their start and end apart: 13, of which 8 were waited for; matrix products, arithmetic and copies ran while one was open for 0% of the time, Pallas kernels for 5%

profile of v4, /device:TPU:1, one launch (start us, length us, event | category | flops | bytes accessed | tf_op | source)
XLA Modules:
  0.0 78.9 jit_solution(14346433511897338433)
XLA Ops:
  0.0 2.1 %own_rows.1 = (f32[2,2,16,512]{3,2,1,0:T(8,128)}, f32[2,2,8,512]{3,2,1,0:T(8,128)}) custom-call(f32[2,2,16,512]{3,2,1,0:T(8,128)} %levels_ref.1, s32[2,256]{1,0:T(2,128)} %enc_ref.1, f32[3,256]{1,0:T(4,128)} %wav_ref.1), custom_call_target="tpu_custom_call" | custom-call | tf_op jit(solution)/shard_map/own_rows/pallas_call | solution.py:293
  2.1 10.2 %collective-permute-start = (f32[2,2,16,512]{3,2,1,0:T(8,128)}, f32[2,2,16,512]{3,2,1,0:T(8,128)S(1)}, u32[]{:S(2)}, u32[]{:S(2)}) collective-permute-start(f32[2,2,16,512]{3,2,1,0:T(8,128)} %get-tuple-element.20), channel_id=1, source_target_pairs={{0,0},{4,32},{8,64},{12,96},{16,128},{20,160},{24,192},{28,224},{1... | collective-permute-start | bytes 393224 | tf_op jit(solution)/shard_map/ppermute | solution.py:409
  12.3 0.1 collective-permute-start.2
  12.4 1.3 %collective-permute-start.1 = (f32[2,2,8,512]{3,2,1,0:T(8,128)}, f32[2,2,8,512]{3,2,1,0:T(8,128)S(1)}, u32[]{:S(2)}, u32[]{:S(2)}) collective-permute-start(f32[2,2,8,512]{3,2,1,0:T(8,128)} %get-tuple-element.21), channel_id=1, source_target_pairs={{4,0},{8,32},{12,64},{16,96},{20,128},{24,160},{28,192},{3,35},{7,... | collective-permute-start | bytes 196616 | tf_op jit(solution)/shard_map/ppermute | solution.py:410
  13.7 1.3 %collective-permute-start.3 = (f32[2,2,8,512]{3,2,1,0:T(8,128)}, f32[2,2,8,512]{3,2,1,0:T(8,128)S(1)}, u32[]{:S(2)}, u32[]{:S(2)}) collective-permute-start(f32[2,2,8,512]{3,2,1,0:T(8,128)} %get-tuple-element.21), channel_id=1, source_target_pairs={{36,0},{40,32},{44,64},{48,96},{52,128},{56,160},{60,192},{35,35},... | collective-permute-start | bytes 196616 | tf_op jit(solution)/shard_map/ppermute | solution.py:410
  15.0 3.6 %own_windows.1 = (f32[80,512]{1,0:T(8,128)}, f32[80,512]{1,0:T(8,128)}, f32[80,512]{1,0:T(8,128)}, f32[80,512]{1,0:T(8,128)}) custom-call(s32[1,65]{1,0:T(1,128)} %bitcast.1, f32[2,512,512]{2,1,0:T(8,128)} %probes.1, f32[512,512]{1,0:T(8,128)} %coefficient.1, f32[512,512]{1,0:T(8,128)} %receiver.1), custom_call_target="tpu_custom_call" | custom-call | bytes 12582912 | tf_op jit(solution)/shard_map/own_windows/pallas_call | solution.py:343
  18.6 0.0 copy-start.1
  18.6 0.0 copy-start.5
  18.7 0.0 collective-permute-done.1
  18.7 6.0 %collective-permute-done.3 = f32[2,2,8,512]{3,2,1,0:T(8,128)S(1)} collective-permute-done((f32[2,2,8,512]{3,2,1,0:T(8,128)}, f32[2,2,8,512]{3,2,1,0:T(8,128)S(1)}, u32[]{:S(2)}, u32[]{:S(2)}) %collective-permute-start.3) | collective-permute-done | bytes 65568 | tf_op jit(solution)/shard_map/ppermute | solution.py:410
  24.6 0.0 collective-permute-done
  24.6 0.0 collective-permute-done.2
  24.7 0.0 copy-start
  24.7 3.0 %collective-permute-start.4 = (f32[4,2,24,512]{3,2,1,0:T(8,128)S(1)}, f32[4,2,24,512]{3,2,1,0:T(8,128)S(1)}, u32[]{:S(2)}, u32[]{:S(2)}) collective-permute-start(f32[4,2,24,512]{3,2,1,0:T(8,128)S(1)} %maximum_maximum_fusion.refs_0_), channel_id=1, source_target_pairs={{1,0},{33,32},{65,64},{97,96},{129,128},{161,160},{193,192},{225,2... | collective-permute-start | bytes 1179656 | tf_op jit(solution)/shard_map/ppermute | solution.py:400
  27.7 0.0 collective-permute-start.5
  27.7 0.7 collective-permute-start.6
  28.4 5.5 %collective-permute-start.7 = (f32[80,512]{1,0:T(8,128)}, f32[80,512]{1,0:T(8,128)S(1)}, u32[]{:S(2)}, u32[]{:S(2)}) collective-permute-start(f32[80,512]{1,0:T(8,128)} %get-tuple-element.28.refs_4_), channel_id=1, source_target_pairs={{8,0},{40,32},{72,64},{104,96},{136,128},{168,160},{200,192},{232,... | collective-permute-start | bytes 491528 | tf_op jit(solution)/shard_map/ppermute | solution.py:400
  33.9 0.9 %collective-permute-start.8 = (f32[80,512]{1,0:T(8,128)}, f32[80,512]{1,0:T(8,128)S(1)}, u32[]{:S(2)}, u32[]{:S(2)}) collective-permute-start(f32[80,512]{1,0:T(8,128)} %get-tuple-element.28.refs_4_), channel_id=1, source_target_pairs={{16,0},{48,32},{80,64},{112,96},{144,128},{176,160},{208,192},{240... | collective-permute-start | bytes 491528 | tf_op jit(solution)/shard_map/ppermute | solution.py:399
  34.8 1.7 %collective-permute-done.7.refs_5_ = f32[80,512]{1,0:T(8,128)S(1)} collective-permute-done((f32[80,512]{1,0:T(8,128)}, f32[80,512]{1,0:T(8,128)S(1)}, u32[]{:S(2)}, u32[]{:S(2)}) %collective-permute-start.7) | collective-permute-done | bytes 163872 | tf_op jit(solution)/shard_map/ppermute | solution.py:400
  36.5 0.0 copy-start.6
  36.5 1.9 %collective-permute-start.9 = (f32[80,512]{1,0:T(8,128)}, f32[80,512]{1,0:T(8,128)S(1)}, u32[]{:S(2)}, u32[]{:S(2)}) collective-permute-start(f32[80,512]{1,0:T(8,128)} %get-tuple-element.28.refs_4_), channel_id=1, source_target_pairs={{24,0},{56,32},{88,64},{120,96},{152,128},{184,160},{216,192},{248... | collective-permute-start | bytes 491528 | tf_op jit(solution)/shard_map/ppermute | solution.py:400
  38.5 1.6 %collective-permute-done.8.refs_6_ = f32[80,512]{1,0:T(8,128)S(1)} collective-permute-done((f32[80,512]{1,0:T(8,128)}, f32[80,512]{1,0:T(8,128)S(1)}, u32[]{:S(2)}, u32[]{:S(2)}) %collective-permute-start.8) | collective-permute-done | bytes 163872 | tf_op jit(solution)/shard_map/ppermute | solution.py:399
  40.1 0.0 copy-start.7
  40.1 6.5 %collective-permute-done.9.refs_7_ = f32[80,512]{1,0:T(8,128)S(1)} collective-permute-done((f32[80,512]{1,0:T(8,128)}, f32[80,512]{1,0:T(8,128)S(1)}, u32[]{:S(2)}, u32[]{:S(2)}) %collective-permute-start.9) | collective-permute-done | bytes 163872 | tf_op jit(solution)/shard_map/ppermute | solution.py:400
  46.6 0.0 copy-start.8
  46.6 0.0 collective-permute-done.4.refs_1_
  46.6 0.0 collective-permute-done.5.refs_2_
  46.6 0.0 copy-start.3
  46.6 1.4 %collective-permute-done.6.refs_3_ = f32[4,2,24,512]{3,2,1,0:T(8,128)S(1)} collective-permute-done((f32[4,2,24,512]{3,2,1,0:T(8,128)S(1)}, f32[4,2,24,512]{3,2,1,0:T(8,128)S(1)}, u32[]{:S(2)}, u32[]{:S(2)}) %collective-permute-start.6) | collective-permute-done | bytes 393248 | tf_op jit(solution)/shard_map/ppermute | solution.py:400
  48.0 0.0 copy-done
  48.0 0.0 copy-done.6
  48.0 0.0 copy-done.7
  48.0 0.0 copy-done.8
  48.1 0.0 copy-done.2
  48.1 0.0 copy-done.3
  48.1 0.0 copy-start.4
  48.1 0.7 copy-done.4
  48.8 16.3 %hessian_rows.1 = (f32[64,512]{1,0:T(8,128)}, f32[64,512]{1,0:T(8,128)}, f32[64,512]{1,0:T(8,128)}, f32[64,512]{1,0:T(8,128)}) custom-call(f32[4,2,24,512]{3,2,1,0:T(8,128)} %copy-done, f32[4,2,24,512]{3,2,1,0:T(8,128)} %copy-done.2, f32[4,2,24,512]{3,2,1,0:T(8,128)} %copy-done.3, f32[4,2,24,512]{3,2,1,0:T(8,128)} %copy-done.4, ...), custom_call_target="tpu_custom_call" | custom-call | flops 110100480 | bytes 4194304 | tf_op jit(solution)/shard_map/hessian_rows/pallas_call | solution.py:227
  65.1 5.2 %collective-permute-start.10 = (f32[64,512]{1,0:T(8,128)}, f32[64,512]{1,0:T(8,128)S(1)}, u32[]{:S(2)}, u32[]{:S(2)}) collective-permute-start(f32[64,512]{1,0:T(8,128)} %get-tuple-element.32), channel_id=1, source_target_pairs={{16,0},{48,32},{80,64},{112,96},{144,128},{176,160},{208,192},{240... | collective-permute-start | bytes 393224 | tf_op jit(solution)/shard_map/ppermute | solution.py:424
  70.3 1.0 %collective-permute-start.11 = (f32[64,512]{1,0:T(8,128)}, f32[64,512]{1,0:T(8,128)S(1)}, u32[]{:S(2)}, u32[]{:S(2)}) collective-permute-start(f32[64,512]{1,0:T(8,128)} %get-tuple-element.33), channel_id=1, source_target_pairs={{24,0},{56,32},{88,64},{120,96},{152,128},{184,160},{216,192},{248... | collective-permute-start | bytes 393224 | tf_op jit(solution)/shard_map/ppermute | solution.py:424
  71.4 1.6 %collective-permute-start.12 = (f32[64,512]{1,0:T(8,128)}, f32[64,512]{1,0:T(8,128)S(1)}, u32[]{:S(2)}, u32[]{:S(2)}) collective-permute-start(f32[64,512]{1,0:T(8,128)} %get-tuple-element.34), channel_id=1, source_target_pairs={{8,0},{40,32},{72,64},{104,96},{136,128},{168,160},{200,192},{232,... | collective-permute-start | bytes 393224 | tf_op jit(solution)/shard_map/ppermute | solution.py:424
  73.0 0.0 copy-done.1
  73.0 1.0 %collective-permute-done.10 = f32[64,512]{1,0:T(8,128)S(1)} collective-permute-done((f32[64,512]{1,0:T(8,128)}, f32[64,512]{1,0:T(8,128)S(1)}, u32[]{:S(2)}, u32[]{:S(2)}) %collective-permute-start.10) | collective-permute-done | bytes 131104 | tf_op jit(solution)/shard_map/ppermute | solution.py:424
  74.1 2.7 %collective-permute-done.11 = f32[64,512]{1,0:T(8,128)S(1)} collective-permute-done((f32[64,512]{1,0:T(8,128)}, f32[64,512]{1,0:T(8,128)S(1)}, u32[]{:S(2)}, u32[]{:S(2)}) %collective-permute-start.11) | collective-permute-done | bytes 131104 | tf_op jit(solution)/shard_map/ppermute | solution.py:424
  76.8 0.3 collective-permute-done.12
  77.1 0.9 %add_add_fusion = f32[64,512]{1,0:T(8,128)S(1)} fusion(f32[64,512]{1,0:T(8,128)S(1)} %collective-permute-done.12, f32[64,512]{1,0:T(8,128)S(1)} %collective-permute-done.11, f32[64,512]{1,0:T(8,128)} %get-tuple-element.31, f32[64,512]{1,0:T(8,128)S(1)} %collective-permute-done.10), kind=kLoop, calls=%fused_computation.2 | loop fusion | flops 98304 | bytes 655360 | tf_op jit(solution)/shard_map/add | solution.py:425
  78.1 0.0 copy-done.5
  78.1 0.8 %subtract_select_fusion = f32[2,64,512]{2,1,0:T(8,128)} fusion(f32[2,64,512]{2,1,0:T(8,128)S(1)} %copy-done.5, f32[64,512]{1,0:T(8,128)S(1)} %add_add_fusion, pred[64,512]{1,0:T(8,128)(4,1)S(1)} %slice_compare_fusion, pred[2]{0:T(512)(128)(4,1)S(1)} %iota_compare_fusion), kind=kLoop, calls=%fused_computation.1 | loop fusion | flops 196608 | bytes 688130 | tf_op jit(solution)/shard_map/jit(_where)/select_n | solution.py:428
  (4 shorter events, 0.1 us)
Async XLA Ops:
  2.1 22.5 %collective-permute-start = (f32[2,2,16,512]{3,2,1,0:T(8,128)}, f32[2,2,16,512]{3,2,1,0:T(8,128)S(1)}, u32[]{:S(2)}, u32[]{:S(2)}) collective-permute-start(f32[2,2,16,512]{3,2,1,0:T(8,128)} %get-tuple-element.20), channel_id=1, source_target_pairs={{0,0},{4,32},{8,64},{12,96},{16,128},{20,160},{24,192},{28,224},{1... | collective-permute-start | bytes 393224 | tf_op jit(solution)/shard_map/ppermute | solution.py:409
  12.3 12.3 %collective-permute-start.2 = (f32[2,2,16,512]{3,2,1,0:T(8,128)}, f32[2,2,16,512]{3,2,1,0:T(8,128)S(1)}, u32[]{:S(2)}, u32[]{:S(2)}) collective-permute-start(f32[2,2,16,512]{3,2,1,0:T(8,128)} %get-tuple-element.20), channel_id=1, source_target_pairs={{32,0},{36,32},{40,64},{44,96},{48,128},{52,160},{56,192},{60,224}... | collective-permute-start | bytes 393224 | tf_op jit(solution)/shard_map/ppermute | solution.py:409
  12.4 6.2 %collective-permute-start.1 = (f32[2,2,8,512]{3,2,1,0:T(8,128)}, f32[2,2,8,512]{3,2,1,0:T(8,128)S(1)}, u32[]{:S(2)}, u32[]{:S(2)}) collective-permute-start(f32[2,2,8,512]{3,2,1,0:T(8,128)} %get-tuple-element.21), channel_id=1, source_target_pairs={{4,0},{8,32},{12,64},{16,96},{20,128},{24,160},{28,192},{3,35},{7,... | collective-permute-start | bytes 196616 | tf_op jit(solution)/shard_map/ppermute | solution.py:410
  13.7 10.9 %collective-permute-start.3 = (f32[2,2,8,512]{3,2,1,0:T(8,128)}, f32[2,2,8,512]{3,2,1,0:T(8,128)S(1)}, u32[]{:S(2)}, u32[]{:S(2)}) collective-permute-start(f32[2,2,8,512]{3,2,1,0:T(8,128)} %get-tuple-element.21), channel_id=1, source_target_pairs={{36,0},{40,32},{44,64},{48,96},{52,128},{56,160},{60,192},{35,35},... | collective-permute-start | bytes 196616 | tf_op jit(solution)/shard_map/ppermute | solution.py:410
  18.6 54.4 %copy-start.1 = (f32[80,512]{1,0:T(8,128)S(1)}, f32[80,512]{1,0:T(8,128)}, u32[]{:S(2)}) copy-start(f32[80,512]{1,0:T(8,128)} %get-tuple-element.26.refs_8_) | copy-start | bytes 491524
  18.6 59.4 %copy-start.5 = (f32[2,64,512]{2,1,0:T(8,128)S(1)}, f32[2,64,512]{2,1,0:T(8,128)}, u32[]{:S(2)}) copy-start(f32[2,64,512]{2,1,0:T(8,128)} %param.9) | copy-start | bytes 786436
  24.7 23.3 %copy-start = (f32[4,2,24,512]{3,2,1,0:T(8,128)}, f32[4,2,24,512]{3,2,1,0:T(8,128)S(1)}, u32[]{:S(2)}) copy-start(f32[4,2,24,512]{3,2,1,0:T(8,128)S(1)} %maximum_maximum_fusion.refs_0_) | copy-start | bytes 1179652
  24.7 21.9 %collective-permute-start.4 = (f32[4,2,24,512]{3,2,1,0:T(8,128)S(1)}, f32[4,2,24,512]{3,2,1,0:T(8,128)S(1)}, u32[]{:S(2)}, u32[]{:S(2)}) collective-permute-start(f32[4,2,24,512]{3,2,1,0:T(8,128)S(1)} %maximum_maximum_fusion.refs_0_), channel_id=1, source_target_pairs={{1,0},{33,32},{65,64},{97,96},{129,128},{161,160},{193,192},{225,2... | collective-permute-start | bytes 1179656 | tf_op jit(solution)/shard_map/ppermute | solution.py:400
  27.7 18.9 %collective-permute-start.5 = (f32[4,2,24,512]{3,2,1,0:T(8,128)S(1)}, f32[4,2,24,512]{3,2,1,0:T(8,128)S(1)}, u32[]{:S(2)}, u32[]{:S(2)}) collective-permute-start(f32[4,2,24,512]{3,2,1,0:T(8,128)S(1)} %maximum_maximum_fusion.refs_0_), channel_id=1, source_target_pairs={{2,0},{34,32},{66,64},{98,96},{130,128},{162,160},{194,192},{226,2... | collective-permute-start | bytes 1179656 | tf_op jit(solution)/shard_map/ppermute | solution.py:399
  27.7 20.3 %collective-permute-start.6 = (f32[4,2,24,512]{3,2,1,0:T(8,128)S(1)}, f32[4,2,24,512]{3,2,1,0:T(8,128)S(1)}, u32[]{:S(2)}, u32[]{:S(2)}) collective-permute-start(f32[4,2,24,512]{3,2,1,0:T(8,128)S(1)} %maximum_maximum_fusion.refs_0_), channel_id=1, source_target_pairs={{3,0},{35,32},{67,64},{99,96},{131,128},{163,160},{195,192},{227,2... | collective-permute-start | bytes 1179656 | tf_op jit(solution)/shard_map/ppermute | solution.py:400
  28.4 8.2 %collective-permute-start.7 = (f32[80,512]{1,0:T(8,128)}, f32[80,512]{1,0:T(8,128)S(1)}, u32[]{:S(2)}, u32[]{:S(2)}) collective-permute-start(f32[80,512]{1,0:T(8,128)} %get-tuple-element.28.refs_4_), channel_id=1, source_target_pairs={{8,0},{40,32},{72,64},{104,96},{136,128},{168,160},{200,192},{232,... | collective-permute-start | bytes 491528 | tf_op jit(solution)/shard_map/ppermute | solution.py:400
  33.9 6.2 %collective-permute-start.8 = (f32[80,512]{1,0:T(8,128)}, f32[80,512]{1,0:T(8,128)S(1)}, u32[]{:S(2)}, u32[]{:S(2)}) collective-permute-start(f32[80,512]{1,0:T(8,128)} %get-tuple-element.28.refs_4_), channel_id=1, source_target_pairs={{16,0},{48,32},{80,64},{112,96},{144,128},{176,160},{208,192},{240... | collective-permute-start | bytes 491528 | tf_op jit(solution)/shard_map/ppermute | solution.py:399
  36.5 11.5 %copy-start.6 = (f32[80,512]{1,0:T(8,128)}, f32[80,512]{1,0:T(8,128)S(1)}, u32[]{:S(2)}) copy-start(f32[80,512]{1,0:T(8,128)S(1)} %collective-permute-done.7.refs_5_) | copy-start | bytes 491524
  36.5 10.1 %collective-permute-start.9 = (f32[80,512]{1,0:T(8,128)}, f32[80,512]{1,0:T(8,128)S(1)}, u32[]{:S(2)}, u32[]{:S(2)}) collective-permute-start(f32[80,512]{1,0:T(8,128)} %get-tuple-element.28.refs_4_), channel_id=1, source_target_pairs={{24,0},{56,32},{88,64},{120,96},{152,128},{184,160},{216,192},{248... | collective-permute-start | bytes 491528 | tf_op jit(solution)/shard_map/ppermute | solution.py:400
  40.1 7.9 %copy-start.7 = (f32[80,512]{1,0:T(8,128)}, f32[80,512]{1,0:T(8,128)S(1)}, u32[]{:S(2)}) copy-start(f32[80,512]{1,0:T(8,128)S(1)} %collective-permute-done.8.refs_6_) | copy-start | bytes 491524
  46.6 1.4 %copy-start.8 = (f32[80,512]{1,0:T(8,128)}, f32[80,512]{1,0:T(8,128)S(1)}, u32[]{:S(2)}) copy-start(f32[80,512]{1,0:T(8,128)S(1)} %collective-permute-done.9.refs_7_) | copy-start | bytes 491524
  46.6 1.4 %copy-start.2 = (f32[4,2,24,512]{3,2,1,0:T(8,128)}, f32[4,2,24,512]{3,2,1,0:T(8,128)S(1)}, u32[]{:S(2)}) copy-start(f32[4,2,24,512]{3,2,1,0:T(8,128)S(1)} %collective-permute-done.4.refs_1_) | copy-start | bytes 1179652
  46.6 1.4 %copy-start.3 = (f32[4,2,24,512]{3,2,1,0:T(8,128)}, f32[4,2,24,512]{3,2,1,0:T(8,128)S(1)}, u32[]{:S(2)}) copy-start(f32[4,2,24,512]{3,2,1,0:T(8,128)S(1)} %collective-permute-done.5.refs_2_) | copy-start | bytes 1179652
  48.1 0.7 copy-start.4
  65.1 9.0 %collective-permute-start.10 = (f32[64,512]{1,0:T(8,128)}, f32[64,512]{1,0:T(8,128)S(1)}, u32[]{:S(2)}, u32[]{:S(2)}) collective-permute-start(f32[64,512]{1,0:T(8,128)} %get-tuple-element.32), channel_id=1, source_target_pairs={{16,0},{48,32},{80,64},{112,96},{144,128},{176,160},{208,192},{240... | collective-permute-start | bytes 393224 | tf_op jit(solution)/shard_map/ppermute | solution.py:424
  70.3 6.4 %collective-permute-start.11 = (f32[64,512]{1,0:T(8,128)}, f32[64,512]{1,0:T(8,128)S(1)}, u32[]{:S(2)}, u32[]{:S(2)}) collective-permute-start(f32[64,512]{1,0:T(8,128)} %get-tuple-element.33), channel_id=1, source_target_pairs={{24,0},{56,32},{88,64},{120,96},{152,128},{184,160},{216,192},{248... | collective-permute-start | bytes 393224 | tf_op jit(solution)/shard_map/ppermute | solution.py:424
  71.4 5.7 %collective-permute-start.12 = (f32[64,512]{1,0:T(8,128)}, f32[64,512]{1,0:T(8,128)S(1)}, u32[]{:S(2)}, u32[]{:S(2)}) collective-permute-start(f32[64,512]{1,0:T(8,128)} %get-tuple-element.34), channel_id=1, source_target_pairs={{8,0},{40,32},{72,64},{104,96},{136,128},{168,160},{200,192},{232,... | collective-permute-start | bytes 393224 | tf_op jit(solution)/shard_map/ppermute | solution.py:424

commit v5 on v4

--- a/solution.py
+++ b/solution.py
@@ -13,6 +13,7 @@
 EDGE = 8
 LANES = 128
 TILES = NZ // LANES
+FIXED = 4 + 13 + 8
 UNROLLS = (74, 72, 70, 68, 66, 64)
 
 
@@ -29,36 +30,51 @@
 def kernel(*refs, shots):
     my_y = lax.rem(lax.axis_index("probe"), 4)
     source_row = NZ // 2 + EDGE - CHUNK * lax.axis_index("shot")
-    slabs = refs[0:4]
-    blocks = refs[4:8]
-    parity_ref, coef_ref, recv_ref = refs[8:11]
-    n = 11
+    n = len(refs) - FIXED
+    slabs = refs[0 : n - 4]
+    blocks = refs[n - 4 : n - 1]
+    fields = refs[n - 1]
     outs = refs[n : n + 4]
-    u_ref, edge_ref, sem, v_ref, e_ref, w_ref, grad_ref, back_ref, *d_refs = refs[n + 4 :]
+    u_ref, edge_ref, sem, block_ref, block_sem, parity_ref, coef_ref, recv_ref, v_ref, e_ref, w_ref, grad_ref, back_ref, *d_refs = refs[n + 4 :]
     d_refs = [d_refs[4 * i : 4 * i + 4] for i in range(2)]
 
     lane = lax.broadcasted_iota(jnp.int32, (8, LANES), 1)
     first = lane == 0
     last = lane == LANES - 1
 
+    half = shots // 2
+    moves = [
+        pltpu.make_async_copy(blocks[q], block_ref.at[q], block_sem.at[q]) for q in range(3)
+    ]
+    for n, target in enumerate((parity_ref, coef_ref, recv_ref, block_ref.at[3])):
+        moves.append(pltpu.make_async_copy(fields.at[n], target, block_sem.at[3 + n]))
+    for copy in moves:
+        copy.start()
     copies = []
-    for k in range(4):
+    if len(slabs) == 5:
+        pieces = [(0, 0, shots), (1, 0, shots), (2, 0, half), (2, half, half), (3, 0, shots)]
+    else:
+        pieces = [(k, 0, shots) for k in range(4)]
+    for slab, (k, first_shot, count) in zip(slabs, pieces):
         base = pl.multiple_of(EDGE + 16 * lax.rem(my_y + k, 4), 8)
+        group = pl.ds(first_shot, count)
         for source, target in (
-            (slabs[k].at[:, :, 0:16, :], u_ref.at[:, 0:2, pl.ds(base, 16), :]),
-            (slabs[k].at[:, :, 16:24, :], edge_ref.at[k]),
+            (slab.at[:, :, 0:16, :], u_ref.at[group, 0:2, pl.ds(base, 16), :]),
+            (slab.at[:, :, 16:24, :], edge_ref.at[k, group]),
         ):
             copies.append(pltpu.make_async_copy(source, target, sem.at[len(copies)]))
             copies[-1].start()
 
     back_ref[...] = match(NZ, None, back=True)
+    for copy in moves:
+        copy.wait()
     coef = coef_ref[...]
     e_ref[...] = 2.0 - 4.0 * coef
     w_ref[...] = recv_ref[...] * recv_ref[...]
 
     odd = parity_ref[...] > 0.5
     for q in range(4):
-        w = blocks[q][...]
+        w = block_ref[(q + 3) % 4]
         for colour in range(2):
             v = jnp.where(odd if colour else jnp.logical_not(odd), w, 0.0)
             for j, tile in enumerate(split(v)):
@@ -219,20 +235,26 @@
         outs[q][...] = result[CHUNK * q : CHUNK * (q + 1)]
 
 
-def apply(slabs, blocks, parity, coef, recv):
+def apply(slabs, blocks, fields):
     shots = slabs[0].shape[0]
     vm = pl.BlockSpec(memory_space=pltpu.VMEM)
-    args = [*slabs, *blocks, parity, coef, recv]
+    anywhere = pl.BlockSpec(memory_space=pl.ANY)
+    args = [*slabs, *blocks, fields]
     big = pltpu.VMEM((TILES, 8 * WIN, LANES), jnp.float32)
     return pl.pallas_call(
         functools.partial(kernel, shots=shots),
         out_shape=[jax.ShapeDtypeStruct((CHUNK, NZ), jnp.float32)] * 4,
-        in_specs=[pl.BlockSpec(memory_space=pltpu.HBM)] * 4 + [vm] * (len(args) - 4),
+        in_specs=[anywhere] * len(args),
         out_specs=[vm] * 4,
         scratch_shapes=[
             pltpu.VMEM((shots, 7, WIN, NZ), jnp.float32),
             pltpu.VMEM((4, shots, 2, 8, NZ), jnp.float32),
-            pltpu.SemaphoreType.DMA((8,)),
+            pltpu.SemaphoreType.DMA((10,)),
+            pltpu.VMEM((4, WIN, NZ), jnp.float32),
+            pltpu.SemaphoreType.DMA((7,)),
+            pltpu.VMEM((WIN, NZ), jnp.float32),
+            pltpu.VMEM((WIN, NZ), jnp.float32),
+            pltpu.VMEM((WIN, NZ), jnp.float32),
             big,
             pltpu.VMEM((WIN, NZ), jnp.float32),
             pltpu.VMEM((WIN, NZ), jnp.float32),
@@ -240,7 +262,7 @@
             pltpu.VMEM((NZ, NZ), jnp.bfloat16),
         ]
         + [big] * 8,
-        compiler_params=pltpu.CompilerParams(vmem_limit_bytes=56 * 1024 * 1024),
+        compiler_params=pltpu.CompilerParams(vmem_limit_bytes=32 * 1024 * 1024),
         cost_estimate=pl.CostEstimate(
             flops=shots * 8 * 8 * 70 * 512 * 12, bytes_accessed=4 << 20, transcendentals=0
         ),
@@ -303,7 +325,7 @@
 
 
 def prepare_kernel(bounds_ref, probes, coefficient, receiver, *refs):
-    mine_ref, coef_ref, recv_ref, colour_ref, pair, coef, recv, sem = refs
+    mine_ref, fields_ref, pair, coef, recv, sem = refs
     chunk = lax.axis_index("shot")
     first = pl.multiple_of(chunk * CHUNK, 8)
     above = pl.multiple_of(jnp.maximum(first - EDGE, 0), 8)
@@ -326,14 +348,15 @@
     block = jnp.sum(jnp.where(counted, 1.0, 0.0), axis=1, keepdims=True)
     odd = block - 2.0 * jnp.floor(0.5 * block)
     odd = jnp.broadcast_to(odd, (WIN, NZ))
-    colour_ref[...] = odd
+    fields_ref[0] = odd
     row = chunk * CHUNK - EDGE + lax.broadcasted_iota(jnp.int32, (WIN, NZ), 0)
     inside = (row >= 0) & (row < NZ)
     for copy in copies:
         copy.wait()
     mine = jnp.where(odd > 0.5, pair[1], pair[0])
-    for value, out in ((mine, mine_ref), (coef[...], coef_ref), (recv[...], recv_ref)):
-        out[...] = exact_dot(jnp.where(inside, value, 0.0), order)
+    for n, value in enumerate((coef[...], recv[...], mine)):
+        fields_ref[1 + n] = exact_dot(jnp.where(inside, value, 0.0), order)
+    mine_ref[...] = fields_ref[3]
 
 
 def prepare(bounds, probes, coefficient, receiver):
@@ -342,9 +365,12 @@
     field = pltpu.VMEM((WIN, NZ), jnp.float32)
     return pl.pallas_call(
         prepare_kernel,
-        out_shape=[jax.ShapeDtypeStruct((WIN, NZ), jnp.float32)] * 4,
+        out_shape=[
+            jax.ShapeDtypeStruct((WIN, NZ), jnp.float32),
+            jax.ShapeDtypeStruct((4, WIN, NZ), jnp.float32),
+        ],
         in_specs=[vm, hbm, hbm, hbm],
-        out_specs=[vm] * 4,
+        out_specs=[vm] * 2,
         scratch_shapes=[
             pltpu.VMEM((2, WIN, NZ), jnp.float32),
             field,
@@ -410,20 +436,20 @@
         side = lax.ppermute(edge, AXES, routes(functools.partial(edge_source, k)))
         owns.append(jnp.concatenate([main, side], axis=2))
 
-    mine, coef, recv, colours = prepare(
+    mine, fields = prepare(
         bounds.reshape(1, 65), probes, coefficient, receiver
     )
 
-    own, mine, coef, recv, colours = lax.optimization_barrier(
-        (jnp.concatenate(owns, axis=0), mine, coef, recv, colours)
+    own, mine, fields = lax.optimization_barrier(
+        (jnp.concatenate(owns, axis=0), mine, fields)
     )
     slabs = spread(own, along_y)
     blocks = spread(mine, along_x)
 
-    terms = apply(slabs, blocks, colours, coef, recv)
+    terms = apply(slabs, blocks[1:], fields)
     parts = [terms[0]] + [lax.ppermute(terms[d], AXES, along_x(4 - d)) for d in (2, 1, 3)]
     total = parts[0] + parts[1] + parts[2] + parts[3]
-    odd = colours[EDGE : EDGE + CHUNK] > 0.5
+    odd = fields[0, EDGE : EDGE + CHUNK] > 0.5
     keep = odd[None] != (jnp.arange(2) == 1)[:, None, None]
     return jnp.where(keep, total[None] - coarse_sample, 0.0)
 

time: 79.9 us -> 78 us (0.976)
  other arithmetic: 1.81 us -> 0.91 us
  Pallas kernels: 22 us -> 21.2 us
    pallas_call x1, Pallas kernels: 16.3 us -> 15.2 us  [apply(): pl.pallas_call(functools.partial(kernel, shots=shots), out_shape=[jax.Sha...]
    add x1, other arithmetic: 0.94 us -> 0.04 us  [on_device(): total = parts[0] + parts[1] + parts[2] + parts[3]]
where the time goes in v5:
time: 78 us; the launch traced here: 77 us
  starting transfers between devices  32.8 us (42%)
  Pallas kernels  21.2 us (27%)
  waiting for transfers between devices  20.9 us (27%)
  local copies, waits for them, and re-layouts  1.09 us (1%)
  other arithmetic  0.91 us (1%)
    pallas_call x1, Pallas kernels, apply(): pl.pallas_call(functools.partial(kernel, shots=shots), out_shape=[jax.Sha...  15.2 us
    ppermute x2, starting transfers between devices, on_device(): main = lax.ppermute(levels, AXES, routes(functools.partial(main_source, k)))  10.3 us
    ppermute x2, starting transfers between devices, spread(): lax.ppermute(array, AXES, along(1))  8.55 us
    ppermute x2, waiting for transfers between devices, spread(): lax.ppermute(array, AXES, along(3))  8.14 us
    ppermute x3, starting transfers between devices, on_device(): lax.ppermute(terms[d], AXES, along_x(4 - d))  7.64 us
    ppermute x2, waiting for transfers between devices, on_device(): side = lax.ppermute(edge, AXES, routes(functools.partial(edge_source, k)))  5.76 us
    ppermute x3, waiting for transfers between devices, on_device(): lax.ppermute(terms[d], AXES, along_x(4 - d))  3.89 us
    pallas_call x1, Pallas kernels, prepare(): pl.pallas_call(prepare_kernel, out_shape=[jax.ShapeDtypeStruct((WIN, NZ),...  3.82 us
  transfers between devices with their start and end apart: 13, of which 8 were waited for; matrix products, arithmetic and copies ran while one was open for 0% of the time, Pallas kernels for 5%

profile of v5, /device:TPU:1, one launch (start us, length us, event | category | flops | bytes accessed | tf_op | source)
XLA Modules:
  0.0 77.0 jit_solution(7503979376887995988)
XLA Ops:
  0.0 2.1 %own_rows.1 = (f32[2,2,16,512]{3,2,1,0:T(8,128)}, f32[2,2,8,512]{3,2,1,0:T(8,128)}) custom-call(f32[2,2,16,512]{3,2,1,0:T(8,128)} %levels_ref.1, s32[2,256]{1,0:T(2,128)} %enc_ref.1, f32[3,256]{1,0:T(4,128)} %wav_ref.1), custom_call_target="tpu_custom_call" | custom-call | tf_op jit(solution)/shard_map/own_rows/pallas_call | solution.py:315
  2.1 10.2 %collective-permute-start = (f32[2,2,16,512]{3,2,1,0:T(8,128)}, f32[2,2,16,512]{3,2,1,0:T(8,128)S(1)}, u32[]{:S(2)}, u32[]{:S(2)}) collective-permute-start(f32[2,2,16,512]{3,2,1,0:T(8,128)} %get-tuple-element.16), channel_id=1, source_target_pairs={{0,0},{4,32},{8,64},{12,96},{16,128},{20,160},{24,192},{28,224},{1... | collective-permute-start | bytes 393224 | tf_op jit(solution)/shard_map/ppermute | solution.py:435
  12.3 0.1 collective-permute-start.2
  12.4 1.3 %collective-permute-start.1 = (f32[2,2,8,512]{3,2,1,0:T(8,128)}, f32[2,2,8,512]{3,2,1,0:T(8,128)S(1)}, u32[]{:S(2)}, u32[]{:S(2)}) collective-permute-start(f32[2,2,8,512]{3,2,1,0:T(8,128)} %get-tuple-element.17), channel_id=1, source_target_pairs={{4,0},{8,32},{12,64},{16,96},{20,128},{24,160},{28,192},{3,35},{7,... | collective-permute-start | bytes 196616 | tf_op jit(solution)/shard_map/ppermute | solution.py:436
  13.7 1.3 %collective-permute-start.3 = (f32[2,2,8,512]{3,2,1,0:T(8,128)}, f32[2,2,8,512]{3,2,1,0:T(8,128)S(1)}, u32[]{:S(2)}, u32[]{:S(2)}) collective-permute-start(f32[2,2,8,512]{3,2,1,0:T(8,128)} %get-tuple-element.17), channel_id=1, source_target_pairs={{36,0},{40,32},{44,64},{48,96},{52,128},{56,160},{60,192},{35,35},... | collective-permute-start | bytes 196616 | tf_op jit(solution)/shard_map/ppermute | solution.py:436
  15.0 3.8 %own_windows.1 = (f32[80,512]{1,0:T(8,128)}, f32[4,80,512]{2,1,0:T(8,128)}) custom-call(s32[1,65]{1,0:T(1,128)} %bitcast.3, f32[2,512,512]{2,1,0:T(8,128)} %probes.1, f32[512,512]{1,0:T(8,128)} %coefficient.1, f32[512,512]{1,0:T(8,128)} %receiver.1), custom_call_target="tpu_custom_call" | custom-call | bytes 12582912 | tf_op jit(solution)/shard_map/own_windows/pallas_call | solution.py:366
  18.9 0.0 copy-start.1
  18.9 0.0 collective-permute-done.1
  18.9 5.8 %collective-permute-done.3 = f32[2,2,8,512]{3,2,1,0:T(8,128)S(1)} collective-permute-done((f32[2,2,8,512]{3,2,1,0:T(8,128)}, f32[2,2,8,512]{3,2,1,0:T(8,128)S(1)}, u32[]{:S(2)}, u32[]{:S(2)}) %collective-permute-start.3) | collective-permute-done | bytes 65568 | tf_op jit(solution)/shard_map/ppermute | solution.py:436
  24.6 0.0 collective-permute-done
  24.6 0.0 collective-permute-done.2
  24.7 3.2 %collective-permute-start.4 = (f32[4,2,24,512]{3,2,1,0:T(8,128)S(1)}, f32[4,2,24,512]{3,2,1,0:T(8,128)S(1)}, u32[]{:S(2)}, u32[]{:S(2)}) collective-permute-start(f32[4,2,24,512]{3,2,1,0:T(8,128)S(1)} %maximum_maximum_fusion.refs_0_), channel_id=1, source_target_pairs={{1,0},{33,32},{65,64},{97,96},{129,128},{161,160},{193,192},{225,2... | collective-permute-start | bytes 1179656 | tf_op jit(solution)/shard_map/ppermute | solution.py:426
  27.9 0.0 collective-permute-start.5
  27.9 0.7 collective-permute-start.6
  28.6 5.3 %collective-permute-start.7 = (f32[80,512]{1,0:T(8,128)}, f32[80,512]{1,0:T(8,128)S(1)}, u32[]{:S(2)}, u32[]{:S(2)}) collective-permute-start(f32[80,512]{1,0:T(8,128)} %get-tuple-element.22), channel_id=1, source_target_pairs={{8,0},{40,32},{72,64},{104,96},{136,128},{168,160},{200,192},{232,... | collective-permute-start | bytes 491528 | tf_op jit(solution)/shard_map/ppermute | solution.py:426
  33.9 1.1 %collective-permute-start.8 = (f32[80,512]{1,0:T(8,128)}, f32[80,512]{1,0:T(8,128)S(1)}, u32[]{:S(2)}, u32[]{:S(2)}) collective-permute-start(f32[80,512]{1,0:T(8,128)} %get-tuple-element.22), channel_id=1, source_target_pairs={{16,0},{48,32},{80,64},{112,96},{144,128},{176,160},{208,192},{240... | collective-permute-start | bytes 491528 | tf_op jit(solution)/shard_map/ppermute | solution.py:425
  35.1 1.4 %collective-permute-done.7.refs_4_ = f32[80,512]{1,0:T(8,128)S(1)} collective-permute-done((f32[80,512]{1,0:T(8,128)}, f32[80,512]{1,0:T(8,128)S(1)}, u32[]{:S(2)}, u32[]{:S(2)}) %collective-permute-start.7) | collective-permute-done | bytes 163872 | tf_op jit(solution)/shard_map/ppermute | solution.py:426
  36.5 1.9 %collective-permute-start.9 = (f32[80,512]{1,0:T(8,128)}, f32[80,512]{1,0:T(8,128)S(1)}, u32[]{:S(2)}, u32[]{:S(2)}) collective-permute-start(f32[80,512]{1,0:T(8,128)} %get-tuple-element.22), channel_id=1, source_target_pairs={{24,0},{56,32},{88,64},{120,96},{152,128},{184,160},{216,192},{248... | collective-permute-start | bytes 491528 | tf_op jit(solution)/shard_map/ppermute | solution.py:426
  38.4 1.7 %collective-permute-done.8.refs_5_ = f32[80,512]{1,0:T(8,128)S(1)} collective-permute-done((f32[80,512]{1,0:T(8,128)}, f32[80,512]{1,0:T(8,128)S(1)}, u32[]{:S(2)}, u32[]{:S(2)}) %collective-permute-start.8) | collective-permute-done | bytes 163872 | tf_op jit(solution)/shard_map/ppermute | solution.py:425
  40.1 4.1 %collective-permute-done.9.refs_6_ = f32[80,512]{1,0:T(8,128)S(1)} collective-permute-done((f32[80,512]{1,0:T(8,128)}, f32[80,512]{1,0:T(8,128)S(1)}, u32[]{:S(2)}, u32[]{:S(2)}) %collective-permute-start.9) | collective-permute-done | bytes 163872 | tf_op jit(solution)/shard_map/ppermute | solution.py:426
  44.2 0.0 collective-permute-done.4.refs_1_
  44.2 0.0 collective-permute-done.5.refs_2_
  44.2 4.0 %collective-permute-done.6.refs_3_ = f32[4,2,24,512]{3,2,1,0:T(8,128)S(1)} collective-permute-done((f32[4,2,24,512]{3,2,1,0:T(8,128)S(1)}, f32[4,2,24,512]{3,2,1,0:T(8,128)S(1)}, u32[]{:S(2)}, u32[]{:S(2)}) %collective-permute-start.6) | collective-permute-done | bytes 393248 | tf_op jit(solution)/shard_map/ppermute | solution.py:426
  48.2 0.0 copy-start
  48.2 1.1 %copy-done = f32[4,80,512]{2,1,0:T(8,128)S(1)} copy-done((f32[4,80,512]{2,1,0:T(8,128)S(1)}, f32[4,80,512]{2,1,0:T(8,128)}, u32[]{:S(2)}) %copy-start) | copy-done | bytes 655384
  49.3 15.2 %hessian_rows.1 = (f32[64,512]{1,0:T(8,128)S(1)}, f32[64,512]{1,0:T(8,128)S(1)}, f32[64,512]{1,0:T(8,128)S(1)}, f32[64,512]{1,0:T(8,128)S(1)}) custom-call(f32[4,2,24,512]{3,2,1,0:T(8,128)S(1)} %maximum_maximum_fusion.refs_0_, f32[4,2,24,512]{3,2,1,0:T(8,128)S(1)} %collective-permute-done.4.refs_1_, f32[4,2,24,512]{3,2,1,0:T(8,128)S(1)} %collective-permute-done.5.refs_2_, ...), custom_call_target="tpu_custom_call" | custom-call | flops 110100480 | bytes 4194304 | tf_op jit(solution)/shard_map/hessian_rows/pallas_call | solution.py:244
  64.5 5.0 %collective-permute-start.10 = (f32[64,512]{1,0:T(8,128)S(1)}, f32[64,512]{1,0:T(8,128)S(1)}, u32[]{:S(2)}, u32[]{:S(2)}) collective-permute-start(f32[64,512]{1,0:T(8,128)S(1)} %get-tuple-element.24), channel_id=1, source_target_pairs={{16,0},{48,32},{80,64},{112,96},{144,128},{176,160},{208,192},{240... | collective-permute-start | bytes 393224 | tf_op jit(solution)/shard_map/ppermute | solution.py:450
  69.5 1.1 %collective-permute-start.11 = (f32[64,512]{1,0:T(8,128)S(1)}, f32[64,512]{1,0:T(8,128)S(1)}, u32[]{:S(2)}, u32[]{:S(2)}) collective-permute-start(f32[64,512]{1,0:T(8,128)S(1)} %get-tuple-element.25), channel_id=1, source_target_pairs={{24,0},{56,32},{88,64},{120,96},{152,128},{184,160},{216,192},{248... | collective-permute-start | bytes 393224 | tf_op jit(solution)/shard_map/ppermute | solution.py:450
  70.6 1.6 %collective-permute-start.12 = (f32[64,512]{1,0:T(8,128)S(1)}, f32[64,512]{1,0:T(8,128)S(1)}, u32[]{:S(2)}, u32[]{:S(2)}) collective-permute-start(f32[64,512]{1,0:T(8,128)S(1)} %get-tuple-element.26), channel_id=1, source_target_pairs={{8,0},{40,32},{72,64},{104,96},{136,128},{168,160},{200,192},{232,... | collective-permute-start | bytes 393224 | tf_op jit(solution)/shard_map/ppermute | solution.py:450
  72.2 0.8 %collective-permute-done.10 = f32[64,512]{1,0:T(8,128)S(1)} collective-permute-done((f32[64,512]{1,0:T(8,128)S(1)}, f32[64,512]{1,0:T(8,128)S(1)}, u32[]{:S(2)}, u32[]{:S(2)}) %collective-permute-start.10) | collective-permute-done | bytes 131104 | tf_op jit(solution)/shard_map/ppermute | solution.py:450
  73.1 2.7 %collective-permute-done.11 = f32[64,512]{1,0:T(8,128)S(1)} collective-permute-done((f32[64,512]{1,0:T(8,128)S(1)}, f32[64,512]{1,0:T(8,128)S(1)}, u32[]{:S(2)}, u32[]{:S(2)}) %collective-permute-start.11) | collective-permute-done | bytes 131104 | tf_op jit(solution)/shard_map/ppermute | solution.py:450
  75.7 0.4 collective-permute-done.12
  76.1 0.0 copy-done.1
  76.2 0.8 %subtract_select_fusion = f32[2,64,512]{2,1,0:T(8,128)} fusion(f32[2,64,512]{2,1,0:T(8,128)S(1)} %copy-done.1, f32[64,512]{1,0:T(8,128)S(1)} %add_add_fusion, pred[64,512]{1,0:T(8,128)(4,1)S(1)} %fusion, pred[2]{0:T(512)(128)(4,1)S(1)} %iota_compare_fusion), kind=kLoop, calls=%fused_computation.1 | loop fusion | flops 196608 | bytes 688130 | tf_op jit(solution)/shard_map/jit(_where)/select_n | solution.py:454
  (4 shorter events, 0.1 us)
Async XLA Ops:
  2.1 22.5 %collective-permute-start = (f32[2,2,16,512]{3,2,1,0:T(8,128)}, f32[2,2,16,512]{3,2,1,0:T(8,128)S(1)}, u32[]{:S(2)}, u32[]{:S(2)}) collective-permute-start(f32[2,2,16,512]{3,2,1,0:T(8,128)} %get-tuple-element.16), channel_id=1, source_target_pairs={{0,0},{4,32},{8,64},{12,96},{16,128},{20,160},{24,192},{28,224},{1... | collective-permute-start | bytes 393224 | tf_op jit(solution)/shard_map/ppermute | solution.py:435
  12.3 12.3 %collective-permute-start.2 = (f32[2,2,16,512]{3,2,1,0:T(8,128)}, f32[2,2,16,512]{3,2,1,0:T(8,128)S(1)}, u32[]{:S(2)}, u32[]{:S(2)}) collective-permute-start(f32[2,2,16,512]{3,2,1,0:T(8,128)} %get-tuple-element.16), channel_id=1, source_target_pairs={{32,0},{36,32},{40,64},{44,96},{48,128},{52,160},{56,192},{60,224}... | collective-permute-start | bytes 393224 | tf_op jit(solution)/shard_map/ppermute | solution.py:435
  12.4 6.4 %collective-permute-start.1 = (f32[2,2,8,512]{3,2,1,0:T(8,128)}, f32[2,2,8,512]{3,2,1,0:T(8,128)S(1)}, u32[]{:S(2)}, u32[]{:S(2)}) collective-permute-start(f32[2,2,8,512]{3,2,1,0:T(8,128)} %get-tuple-element.17), channel_id=1, source_target_pairs={{4,0},{8,32},{12,64},{16,96},{20,128},{24,160},{28,192},{3,35},{7,... | collective-permute-start | bytes 196616 | tf_op jit(solution)/shard_map/ppermute | solution.py:436
  13.7 10.9 %collective-permute-start.3 = (f32[2,2,8,512]{3,2,1,0:T(8,128)}, f32[2,2,8,512]{3,2,1,0:T(8,128)S(1)}, u32[]{:S(2)}, u32[]{:S(2)}) collective-permute-start(f32[2,2,8,512]{3,2,1,0:T(8,128)} %get-tuple-element.17), channel_id=1, source_target_pairs={{36,0},{40,32},{44,64},{48,96},{52,128},{56,160},{60,192},{35,35},... | collective-permute-start | bytes 196616 | tf_op jit(solution)/shard_map/ppermute | solution.py:436
  18.9 57.3 %copy-start.1 = (f32[2,64,512]{2,1,0:T(8,128)S(1)}, f32[2,64,512]{2,1,0:T(8,128)}, u32[]{:S(2)}) copy-start(f32[2,64,512]{2,1,0:T(8,128)} %param.9) | copy-start | bytes 786436
  24.7 19.6 %collective-permute-start.4 = (f32[4,2,24,512]{3,2,1,0:T(8,128)S(1)}, f32[4,2,24,512]{3,2,1,0:T(8,128)S(1)}, u32[]{:S(2)}, u32[]{:S(2)}) collective-permute-start(f32[4,2,24,512]{3,2,1,0:T(8,128)S(1)} %maximum_maximum_fusion.refs_0_), channel_id=1, source_target_pairs={{1,0},{33,32},{65,64},{97,96},{129,128},{161,160},{193,192},{225,2... | collective-permute-start | bytes 1179656 | tf_op jit(solution)/shard_map/ppermute | solution.py:426
  27.9 16.3 %collective-permute-start.5 = (f32[4,2,24,512]{3,2,1,0:T(8,128)S(1)}, f32[4,2,24,512]{3,2,1,0:T(8,128)S(1)}, u32[]{:S(2)}, u32[]{:S(2)}) collective-permute-start(f32[4,2,24,512]{3,2,1,0:T(8,128)S(1)} %maximum_maximum_fusion.refs_0_), channel_id=1, source_target_pairs={{2,0},{34,32},{66,64},{98,96},{130,128},{162,160},{194,192},{226,2... | collective-permute-start | bytes 1179656 | tf_op jit(solution)/shard_map/ppermute | solution.py:425
  27.9 20.3 %collective-permute-start.6 = (f32[4,2,24,512]{3,2,1,0:T(8,128)S(1)}, f32[4,2,24,512]{3,2,1,0:T(8,128)S(1)}, u32[]{:S(2)}, u32[]{:S(2)}) collective-permute-start(f32[4,2,24,512]{3,2,1,0:T(8,128)S(1)} %maximum_maximum_fusion.refs_0_), channel_id=1, source_target_pairs={{3,0},{35,32},{67,64},{99,96},{131,128},{163,160},{195,192},{227,2... | collective-permute-start | bytes 1179656 | tf_op jit(solution)/shard_map/ppermute | solution.py:426
  28.6 7.9 %collective-permute-start.7 = (f32[80,512]{1,0:T(8,128)}, f32[80,512]{1,0:T(8,128)S(1)}, u32[]{:S(2)}, u32[]{:S(2)}) collective-permute-start(f32[80,512]{1,0:T(8,128)} %get-tuple-element.22), channel_id=1, source_target_pairs={{8,0},{40,32},{72,64},{104,96},{136,128},{168,160},{200,192},{232,... | collective-permute-start | bytes 491528 | tf_op jit(solution)/shard_map/ppermute | solution.py:426
  33.9 6.2 %collective-permute-start.8 = (f32[80,512]{1,0:T(8,128)}, f32[80,512]{1,0:T(8,128)S(1)}, u32[]{:S(2)}, u32[]{:S(2)}) collective-permute-start(f32[80,512]{1,0:T(8,128)} %get-tuple-element.22), channel_id=1, source_target_pairs={{16,0},{48,32},{80,64},{112,96},{144,128},{176,160},{208,192},{240... | collective-permute-start | bytes 491528 | tf_op jit(solution)/shard_map/ppermute | solution.py:425
  36.5 7.7 %collective-permute-start.9 = (f32[80,512]{1,0:T(8,128)}, f32[80,512]{1,0:T(8,128)S(1)}, u32[]{:S(2)}, u32[]{:S(2)}) collective-permute-start(f32[80,512]{1,0:T(8,128)} %get-tuple-element.22), channel_id=1, source_target_pairs={{24,0},{56,32},{88,64},{120,96},{152,128},{184,160},{216,192},{248... | collective-permute-start | bytes 491528 | tf_op jit(solution)/shard_map/ppermute | solution.py:426
  48.2 1.1 %copy-start = (f32[4,80,512]{2,1,0:T(8,128)S(1)}, f32[4,80,512]{2,1,0:T(8,128)}, u32[]{:S(2)}) copy-start(f32[4,80,512]{2,1,0:T(8,128)} %get-tuple-element.20.refs_7_) | copy-start | bytes 1966084
  64.5 8.5 %collective-permute-start.10 = (f32[64,512]{1,0:T(8,128)S(1)}, f32[64,512]{1,0:T(8,128)S(1)}, u32[]{:S(2)}, u32[]{:S(2)}) collective-permute-start(f32[64,512]{1,0:T(8,128)S(1)} %get-tuple-element.24), channel_id=1, source_target_pairs={{16,0},{48,32},{80,64},{112,96},{144,128},{176,160},{208,192},{240... | collective-permute-start | bytes 393224 | tf_op jit(solution)/shard_map/ppermute | solution.py:450
  69.5 6.2 %collective-permute-start.11 = (f32[64,512]{1,0:T(8,128)S(1)}, f32[64,512]{1,0:T(8,128)S(1)}, u32[]{:S(2)}, u32[]{:S(2)}) collective-permute-start(f32[64,512]{1,0:T(8,128)S(1)} %get-tuple-element.25), channel_id=1, source_target_pairs={{24,0},{56,32},{88,64},{120,96},{152,128},{184,160},{216,192},{248... | collective-permute-start | bytes 393224 | tf_op jit(solution)/shard_map/ppermute | solution.py:450
  70.6 5.5 %collective-permute-start.12 = (f32[64,512]{1,0:T(8,128)S(1)}, f32[64,512]{1,0:T(8,128)S(1)}, u32[]{:S(2)}, u32[]{:S(2)}) collective-permute-start(f32[64,512]{1,0:T(8,128)S(1)} %get-tuple-element.26), channel_id=1, source_target_pairs={{8,0},{40,32},{72,64},{104,96},{136,128},{168,160},{200,192},{232,... | collective-permute-start | bytes 393224 | tf_op jit(solution)/shard_map/ppermute | solution.py:450

commit v6 on v5

--- a/solution.py
+++ b/solution.py
@@ -447,7 +447,7 @@
     blocks = spread(mine, along_x)
 
     terms = apply(slabs, blocks[1:], fields)
-    parts = [terms[0]] + [lax.ppermute(terms[d], AXES, along_x(4 - d)) for d in (2, 1, 3)]
+    parts = [terms[0]] + [lax.ppermute(terms[d], AXES, along_x(4 - d)) for d in (1, 2, 3)]
     total = parts[0] + parts[1] + parts[2] + parts[3]
     odd = fields[0, EDGE : EDGE + CHUNK] > 0.5
     keep = odd[None] != (jnp.arange(2) == 1)[:, None, None]

time: 78 us -> 78.5 us (level)
  waiting for transfers between devices: 20.9 us -> 22.1 us
    ppermute x3, waiting for transfers between devices: 3.89 us -> 5.1 us  [on_device(): lax.ppermute(terms[d], AXES, along_x(4 - d))]
  transfers between devices with their start and end apart: 13 -> 13, of which waited for: 8 -> 7; matrix products, arithmetic and copies ran while one was open for 0% -> 0% of each run, Pallas kernels for 5% -> 5%
where the time goes in v6:
time: 78.5 us; the launch traced here: 77.6 us
  starting transfers between devices  32.2 us (41%)
  waiting for transfers between devices  22.1 us (28%)
  Pallas kernels  21.2 us (27%)
  local copies, waits for them, and re-layouts  1.09 us (1%)
  other arithmetic  0.91 us (1%)
    pallas_call x1, Pallas kernels, apply(): pl.pallas_call(functools.partial(kernel, shots=shots), out_shape=[jax.Sha...  15.2 us
    ppermute x2, starting transfers between devices, on_device(): main = lax.ppermute(levels, AXES, routes(functools.partial(main_source, k)))  10.3 us
    ppermute x2, starting transfers between devices, spread(): lax.ppermute(array, AXES, along(1))  8.55 us
    ppermute x2, waiting for transfers between devices, spread(): lax.ppermute(array, AXES, along(3))  8.14 us
    ppermute x3, starting transfers between devices, on_device(): lax.ppermute(terms[d], AXES, along_x(4 - d))  7.03 us
    ppermute x2, waiting for transfers between devices, on_device(): side = lax.ppermute(edge, AXES, routes(functools.partial(edge_source, k)))  5.76 us
    ppermute x3, waiting for transfers between devices, on_device(): lax.ppermute(terms[d], AXES, along_x(4 - d))  5.1 us
    pallas_call x1, Pallas kernels, prepare(): pl.pallas_call(prepare_kernel, out_shape=[jax.ShapeDtypeStruct((WIN, NZ),...  3.82 us
  transfers between devices with their start and end apart: 13, of which 7 were waited for; matrix products, arithmetic and copies ran while one was open for 0% of the time, Pallas kernels for 5%

profile of v6, /device:TPU:1, one launch (start us, length us, event | category | flops | bytes accessed | tf_op | source)
XLA Modules:
  0.0 77.6 jit_solution(10641066076298727843)
XLA Ops:
  0.0 2.1 %own_rows.1 = (f32[2,2,16,512]{3,2,1,0:T(8,128)}, f32[2,2,8,512]{3,2,1,0:T(8,128)}) custom-call(f32[2,2,16,512]{3,2,1,0:T(8,128)} %levels_ref.1, s32[2,256]{1,0:T(2,128)} %enc_ref.1, f32[3,256]{1,0:T(4,128)} %wav_ref.1), custom_call_target="tpu_custom_call" | custom-call | tf_op jit(solution)/shard_map/own_rows/pallas_call | solution.py:315
  2.1 10.2 %collective-permute-start = (f32[2,2,16,512]{3,2,1,0:T(8,128)}, f32[2,2,16,512]{3,2,1,0:T(8,128)S(1)}, u32[]{:S(2)}, u32[]{:S(2)}) collective-permute-start(f32[2,2,16,512]{3,2,1,0:T(8,128)} %get-tuple-element.16), channel_id=1, source_target_pairs={{0,0},{4,32},{8,64},{12,96},{16,128},{20,160},{24,192},{28,224},{1... | collective-permute-start | bytes 393224 | tf_op jit(solution)/shard_map/ppermute | solution.py:435
  12.3 0.1 collective-permute-start.2
  12.4 1.3 %collective-permute-start.1 = (f32[2,2,8,512]{3,2,1,0:T(8,128)}, f32[2,2,8,512]{3,2,1,0:T(8,128)S(1)}, u32[]{:S(2)}, u32[]{:S(2)}) collective-permute-start(f32[2,2,8,512]{3,2,1,0:T(8,128)} %get-tuple-element.17), channel_id=1, source_target_pairs={{4,0},{8,32},{12,64},{16,96},{20,128},{24,160},{28,192},{3,35},{7,... | collective-permute-start | bytes 196616 | tf_op jit(solution)/shard_map/ppermute | solution.py:436
  13.7 1.3 %collective-permute-start.3 = (f32[2,2,8,512]{3,2,1,0:T(8,128)}, f32[2,2,8,512]{3,2,1,0:T(8,128)S(1)}, u32[]{:S(2)}, u32[]{:S(2)}) collective-permute-start(f32[2,2,8,512]{3,2,1,0:T(8,128)} %get-tuple-element.17), channel_id=1, source_target_pairs={{36,0},{40,32},{44,64},{48,96},{52,128},{56,160},{60,192},{35,35},... | collective-permute-start | bytes 196616 | tf_op jit(solution)/shard_map/ppermute | solution.py:436
  15.0 3.8 %own_windows.1 = (f32[80,512]{1,0:T(8,128)}, f32[4,80,512]{2,1,0:T(8,128)}) custom-call(s32[1,65]{1,0:T(1,128)} %bitcast.3, f32[2,512,512]{2,1,0:T(8,128)} %probes.1, f32[512,512]{1,0:T(8,128)} %coefficient.1, f32[512,512]{1,0:T(8,128)} %receiver.1), custom_call_target="tpu_custom_call" | custom-call | bytes 12582912 | tf_op jit(solution)/shard_map/own_windows/pallas_call | solution.py:366
  18.9 0.0 copy-start.1
  18.9 0.0 collective-permute-done.1
  18.9 5.8 %collective-permute-done.3 = f32[2,2,8,512]{3,2,1,0:T(8,128)S(1)} collective-permute-done((f32[2,2,8,512]{3,2,1,0:T(8,128)}, f32[2,2,8,512]{3,2,1,0:T(8,128)S(1)}, u32[]{:S(2)}, u32[]{:S(2)}) %collective-permute-start.3) | collective-permute-done | bytes 65568 | tf_op jit(solution)/shard_map/ppermute | solution.py:436
  24.6 0.0 collective-permute-done
  24.6 0.0 collective-permute-done.2
  24.7 3.2 %collective-permute-start.4 = (f32[4,2,24,512]{3,2,1,0:T(8,128)S(1)}, f32[4,2,24,512]{3,2,1,0:T(8,128)S(1)}, u32[]{:S(2)}, u32[]{:S(2)}) collective-permute-start(f32[4,2,24,512]{3,2,1,0:T(8,128)S(1)} %maximum_maximum_fusion.refs_0_), channel_id=1, source_target_pairs={{1,0},{33,32},{65,64},{97,96},{129,128},{161,160},{193,192},{225,2... | collective-permute-start | bytes 1179656 | tf_op jit(solution)/shard_map/ppermute | solution.py:426
  27.9 0.0 collective-permute-start.5
  27.9 0.7 collective-permute-start.6
  28.6 5.3 %collective-permute-start.7 = (f32[80,512]{1,0:T(8,128)}, f32[80,512]{1,0:T(8,128)S(1)}, u32[]{:S(2)}, u32[]{:S(2)}) collective-permute-start(f32[80,512]{1,0:T(8,128)} %get-tuple-element.22), channel_id=1, source_target_pairs={{8,0},{40,32},{72,64},{104,96},{136,128},{168,160},{200,192},{232,... | collective-permute-start | bytes 491528 | tf_op jit(solution)/shard_map/ppermute | solution.py:426
  33.9 1.1 %collective-permute-start.8 = (f32[80,512]{1,0:T(8,128)}, f32[80,512]{1,0:T(8,128)S(1)}, u32[]{:S(2)}, u32[]{:S(2)}) collective-permute-start(f32[80,512]{1,0:T(8,128)} %get-tuple-element.22), channel_id=1, source_target_pairs={{16,0},{48,32},{80,64},{112,96},{144,128},{176,160},{208,192},{240... | collective-permute-start | bytes 491528 | tf_op jit(solution)/shard_map/ppermute | solution.py:425
  35.1 1.4 %collective-permute-done.7.refs_4_ = f32[80,512]{1,0:T(8,128)S(1)} collective-permute-done((f32[80,512]{1,0:T(8,128)}, f32[80,512]{1,0:T(8,128)S(1)}, u32[]{:S(2)}, u32[]{:S(2)}) %collective-permute-start.7) | collective-permute-done | bytes 163872 | tf_op jit(solution)/shard_map/ppermute | solution.py:426
  36.5 1.9 %collective-permute-start.9 = (f32[80,512]{1,0:T(8,128)}, f32[80,512]{1,0:T(8,128)S(1)}, u32[]{:S(2)}, u32[]{:S(2)}) collective-permute-start(f32[80,512]{1,0:T(8,128)} %get-tuple-element.22), channel_id=1, source_target_pairs={{24,0},{56,32},{88,64},{120,96},{152,128},{184,160},{216,192},{248... | collective-permute-start | bytes 491528 | tf_op jit(solution)/shard_map/ppermute | solution.py:426
  38.4 1.7 %collective-permute-done.8.refs_5_ = f32[80,512]{1,0:T(8,128)S(1)} collective-permute-done((f32[80,512]{1,0:T(8,128)}, f32[80,512]{1,0:T(8,128)S(1)}, u32[]{:S(2)}, u32[]{:S(2)}) %collective-permute-start.8) | collective-permute-done | bytes 163872 | tf_op jit(solution)/shard_map/ppermute | solution.py:425
  40.1 4.1 %collective-permute-done.9.refs_6_ = f32[80,512]{1,0:T(8,128)S(1)} collective-permute-done((f32[80,512]{1,0:T(8,128)}, f32[80,512]{1,0:T(8,128)S(1)}, u32[]{:S(2)}, u32[]{:S(2)}) %collective-permute-start.9) | collective-permute-done | bytes 163872 | tf_op jit(solution)/shard_map/ppermute | solution.py:426
  44.2 0.0 collective-permute-done.4.refs_1_
  44.2 0.0 collective-permute-done.5.refs_2_
  44.2 4.0 %collective-permute-done.6.refs_3_ = f32[4,2,24,512]{3,2,1,0:T(8,128)S(1)} collective-permute-done((f32[4,2,24,512]{3,2,1,0:T(8,128)S(1)}, f32[4,2,24,512]{3,2,1,0:T(8,128)S(1)}, u32[]{:S(2)}, u32[]{:S(2)}) %collective-permute-start.6) | collective-permute-done | bytes 393248 | tf_op jit(solution)/shard_map/ppermute | solution.py:426
  48.2 0.0 copy-start
  48.2 1.1 %copy-done = f32[4,80,512]{2,1,0:T(8,128)S(1)} copy-done((f32[4,80,512]{2,1,0:T(8,128)S(1)}, f32[4,80,512]{2,1,0:T(8,128)}, u32[]{:S(2)}) %copy-start) | copy-done | bytes 655384
  49.3 15.2 %hessian_rows.1 = (f32[64,512]{1,0:T(8,128)S(1)}, f32[64,512]{1,0:T(8,128)S(1)}, f32[64,512]{1,0:T(8,128)S(1)}, f32[64,512]{1,0:T(8,128)S(1)}) custom-call(f32[4,2,24,512]{3,2,1,0:T(8,128)S(1)} %maximum_maximum_fusion.refs_0_, f32[4,2,24,512]{3,2,1,0:T(8,128)S(1)} %collective-permute-done.4.refs_1_, f32[4,2,24,512]{3,2,1,0:T(8,128)S(1)} %collective-permute-done.5.refs_2_, ...), custom_call_target="tpu_custom_call" | custom-call | flops 110100480 | bytes 4194304 | tf_op jit(solution)/shard_map/hessian_rows/pallas_call | solution.py:244
  64.5 2.5 %collective-permute-start.10 = (f32[64,512]{1,0:T(8,128)S(1)}, f32[64,512]{1,0:T(8,128)S(1)}, u32[]{:S(2)}, u32[]{:S(2)}) collective-permute-start(f32[64,512]{1,0:T(8,128)S(1)} %get-tuple-element.24), channel_id=1, source_target_pairs={{24,0},{56,32},{88,64},{120,96},{152,128},{184,160},{216,192},{248... | collective-permute-start | bytes 393224 | tf_op jit(solution)/shard_map/ppermute | solution.py:450
  67.1 4.1 %collective-permute-start.11 = (f32[64,512]{1,0:T(8,128)S(1)}, f32[64,512]{1,0:T(8,128)S(1)}, u32[]{:S(2)}, u32[]{:S(2)}) collective-permute-start(f32[64,512]{1,0:T(8,128)S(1)} %get-tuple-element.25), channel_id=1, source_target_pairs={{16,0},{48,32},{80,64},{112,96},{144,128},{176,160},{208,192},{240... | collective-permute-start | bytes 393224 | tf_op jit(solution)/shard_map/ppermute | solution.py:450
  71.2 0.4 collective-permute-start.12
  71.6 1.4 %collective-permute-done.10 = f32[64,512]{1,0:T(8,128)S(1)} collective-permute-done((f32[64,512]{1,0:T(8,128)S(1)}, f32[64,512]{1,0:T(8,128)S(1)}, u32[]{:S(2)}, u32[]{:S(2)}) %collective-permute-start.10) | collective-permute-done | bytes 131104 | tf_op jit(solution)/shard_map/ppermute | solution.py:450
  73.0 3.7 %collective-permute-done.11 = f32[64,512]{1,0:T(8,128)S(1)} collective-permute-done((f32[64,512]{1,0:T(8,128)S(1)}, f32[64,512]{1,0:T(8,128)S(1)}, u32[]{:S(2)}, u32[]{:S(2)}) %collective-permute-start.11) | collective-permute-done | bytes 131104 | tf_op jit(solution)/shard_map/ppermute | solution.py:450
  76.7 0.0 collective-permute-done.12
  76.7 0.0 copy-done.1
  76.8 0.8 %subtract_select_fusion = f32[2,64,512]{2,1,0:T(8,128)} fusion(f32[2,64,512]{2,1,0:T(8,128)S(1)} %copy-done.1, f32[64,512]{1,0:T(8,128)S(1)} %add_add_fusion, pred[64,512]{1,0:T(8,128)(4,1)S(1)} %fusion, pred[2]{0:T(512)(128)(4,1)S(1)} %iota_compare_fusion), kind=kLoop, calls=%fused_computation.1 | loop fusion | flops 196608 | bytes 688130 | tf_op jit(solution)/shard_map/jit(_where)/select_n | solution.py:454
  (4 shorter events, 0.1 us)
Async XLA Ops:
  2.1 22.5 %collective-permute-start = (f32[2,2,16,512]{3,2,1,0:T(8,128)}, f32[2,2,16,512]{3,2,1,0:T(8,128)S(1)}, u32[]{:S(2)}, u32[]{:S(2)}) collective-permute-start(f32[2,2,16,512]{3,2,1,0:T(8,128)} %get-tuple-element.16), channel_id=1, source_target_pairs={{0,0},{4,32},{8,64},{12,96},{16,128},{20,160},{24,192},{28,224},{1... | collective-permute-start | bytes 393224 | tf_op jit(solution)/shard_map/ppermute | solution.py:435
  12.3 12.3 %collective-permute-start.2 = (f32[2,2,16,512]{3,2,1,0:T(8,128)}, f32[2,2,16,512]{3,2,1,0:T(8,128)S(1)}, u32[]{:S(2)}, u32[]{:S(2)}) collective-permute-start(f32[2,2,16,512]{3,2,1,0:T(8,128)} %get-tuple-element.16), channel_id=1, source_target_pairs={{32,0},{36,32},{40,64},{44,96},{48,128},{52,160},{56,192},{60,224}... | collective-permute-start | bytes 393224 | tf_op jit(solution)/shard_map/ppermute | solution.py:435
  12.4 6.4 %collective-permute-start.1 = (f32[2,2,8,512]{3,2,1,0:T(8,128)}, f32[2,2,8,512]{3,2,1,0:T(8,128)S(1)}, u32[]{:S(2)}, u32[]{:S(2)}) collective-permute-start(f32[2,2,8,512]{3,2,1,0:T(8,128)} %get-tuple-element.17), channel_id=1, source_target_pairs={{4,0},{8,32},{12,64},{16,96},{20,128},{24,160},{28,192},{3,35},{7,... | collective-permute-start | bytes 196616 | tf_op jit(solution)/shard_map/ppermute | solution.py:436
  13.7 10.9 %collective-permute-start.3 = (f32[2,2,8,512]{3,2,1,0:T(8,128)}, f32[2,2,8,512]{3,2,1,0:T(8,128)S(1)}, u32[]{:S(2)}, u32[]{:S(2)}) collective-permute-start(f32[2,2,8,512]{3,2,1,0:T(8,128)} %get-tuple-element.17), channel_id=1, source_target_pairs={{36,0},{40,32},{44,64},{48,96},{52,128},{56,160},{60,192},{35,35},... | collective-permute-start | bytes 196616 | tf_op jit(solution)/shard_map/ppermute | solution.py:436
  18.9 57.9 %copy-start.1 = (f32[2,64,512]{2,1,0:T(8,128)S(1)}, f32[2,64,512]{2,1,0:T(8,128)}, u32[]{:S(2)}) copy-start(f32[2,64,512]{2,1,0:T(8,128)} %param.9) | copy-start | bytes 786436
  24.7 19.6 %collective-permute-start.4 = (f32[4,2,24,512]{3,2,1,0:T(8,128)S(1)}, f32[4,2,24,512]{3,2,1,0:T(8,128)S(1)}, u32[]{:S(2)}, u32[]{:S(2)}) collective-permute-start(f32[4,2,24,512]{3,2,1,0:T(8,128)S(1)} %maximum_maximum_fusion.refs_0_), channel_id=1, source_target_pairs={{1,0},{33,32},{65,64},{97,96},{129,128},{161,160},{193,192},{225,2... | collective-permute-start | bytes 1179656 | tf_op jit(solution)/shard_map/ppermute | solution.py:426
  27.9 16.3 %collective-permute-start.5 = (f32[4,2,24,512]{3,2,1,0:T(8,128)S(1)}, f32[4,2,24,512]{3,2,1,0:T(8,128)S(1)}, u32[]{:S(2)}, u32[]{:S(2)}) collective-permute-start(f32[4,2,24,512]{3,2,1,0:T(8,128)S(1)} %maximum_maximum_fusion.refs_0_), channel_id=1, source_target_pairs={{2,0},{34,32},{66,64},{98,96},{130,128},{162,160},{194,192},{226,2... | collective-permute-start | bytes 1179656 | tf_op jit(solution)/shard_map/ppermute | solution.py:425
  27.9 20.3 %collective-permute-start.6 = (f32[4,2,24,512]{3,2,1,0:T(8,128)S(1)}, f32[4,2,24,512]{3,2,1,0:T(8,128)S(1)}, u32[]{:S(2)}, u32[]{:S(2)}) collective-permute-start(f32[4,2,24,512]{3,2,1,0:T(8,128)S(1)} %maximum_maximum_fusion.refs_0_), channel_id=1, source_target_pairs={{3,0},{35,32},{67,64},{99,96},{131,128},{163,160},{195,192},{227,2... | collective-permute-start | bytes 1179656 | tf_op jit(solution)/shard_map/ppermute | solution.py:426
  28.6 7.9 %collective-permute-start.7 = (f32[80,512]{1,0:T(8,128)}, f32[80,512]{1,0:T(8,128)S(1)}, u32[]{:S(2)}, u32[]{:S(2)}) collective-permute-start(f32[80,512]{1,0:T(8,128)} %get-tuple-element.22), channel_id=1, source_target_pairs={{8,0},{40,32},{72,64},{104,96},{136,128},{168,160},{200,192},{232,... | collective-permute-start | bytes 491528 | tf_op jit(solution)/shard_map/ppermute | solution.py:426
  33.9 6.2 %collective-permute-start.8 = (f32[80,512]{1,0:T(8,128)}, f32[80,512]{1,0:T(8,128)S(1)}, u32[]{:S(2)}, u32[]{:S(2)}) collective-permute-start(f32[80,512]{1,0:T(8,128)} %get-tuple-element.22), channel_id=1, source_target_pairs={{16,0},{48,32},{80,64},{112,96},{144,128},{176,160},{208,192},{240... | collective-permute-start | bytes 491528 | tf_op jit(solution)/shard_map/ppermute | solution.py:425
  36.5 7.7 %collective-permute-start.9 = (f32[80,512]{1,0:T(8,128)}, f32[80,512]{1,0:T(8,128)S(1)}, u32[]{:S(2)}, u32[]{:S(2)}) collective-permute-start(f32[80,512]{1,0:T(8,128)} %get-tuple-element.22), channel_id=1, source_target_pairs={{24,0},{56,32},{88,64},{120,96},{152,128},{184,160},{216,192},{248... | collective-permute-start | bytes 491528 | tf_op jit(solution)/shard_map/ppermute | solution.py:426
  48.2 1.1 %copy-start = (f32[4,80,512]{2,1,0:T(8,128)S(1)}, f32[4,80,512]{2,1,0:T(8,128)}, u32[]{:S(2)}) copy-start(f32[4,80,512]{2,1,0:T(8,128)} %get-tuple-element.20.refs_7_) | copy-start | bytes 1966084
  64.5 8.5 %collective-permute-start.10 = (f32[64,512]{1,0:T(8,128)S(1)}, f32[64,512]{1,0:T(8,128)S(1)}, u32[]{:S(2)}, u32[]{:S(2)}) collective-permute-start(f32[64,512]{1,0:T(8,128)S(1)} %get-tuple-element.24), channel_id=1, source_target_pairs={{24,0},{56,32},{88,64},{120,96},{152,128},{184,160},{216,192},{248... | collective-permute-start | bytes 393224 | tf_op jit(solution)/shard_map/ppermute | solution.py:450
  67.1 9.6 %collective-permute-start.11 = (f32[64,512]{1,0:T(8,128)S(1)}, f32[64,512]{1,0:T(8,128)S(1)}, u32[]{:S(2)}, u32[]{:S(2)}) collective-permute-start(f32[64,512]{1,0:T(8,128)S(1)} %get-tuple-element.25), channel_id=1, source_target_pairs={{16,0},{48,32},{80,64},{112,96},{144,128},{176,160},{208,192},{240... | collective-permute-start | bytes 393224 | tf_op jit(solution)/shard_map/ppermute | solution.py:450
  71.2 5.5 %collective-permute-start.12 = (f32[64,512]{1,0:T(8,128)S(1)}, f32[64,512]{1,0:T(8,128)S(1)}, u32[]{:S(2)}, u32[]{:S(2)}) collective-permute-start(f32[64,512]{1,0:T(8,128)S(1)} %get-tuple-element.26), channel_id=1, source_target_pairs={{8,0},{40,32},{72,64},{104,96},{136,128},{168,160},{200,192},{232,... | collective-permute-start | bytes 393224 | tf_op jit(solution)/shard_map/ppermute | solution.py:450
